TPU v7x, 128 devices: a whole 4x4x4 slice. The times are simulated.
128 devices in a mesh: row: 16 (over x_lo, z, core), col: 8 (over y, x_hi).
Axes of the slice: x: 4 (x_hi: 2, x_lo: 2; x = x_hi * 2 + x_lo), y: 4, z: 4, core: 2. Of those that a mesh axis runs over, the one named last changes fastest.
Arguments:
- features: bfloat16 [32768, 256], P(('col', 'row')), may hold values from -6 to 6
- weight: bfloat16 [256, 256], replicated, may hold values from -0.375 to 0.375
- bias: float32 [256], replicated, may hold values from -4 to 4
- tile_values: bfloat16 [16, 8, 384, 128, 128], P('row', 'col'), may hold values from -0.109375 to 0.109375
- tile_row: int32 [16, 8, 384], P('row', 'col'), may hold values from 0 to 15
- tile_col: int32 [16, 8, 384], P('row', 'col'), may hold values from 0 to 31
- tile_count: int32 [16, 8], P('row', 'col'), may hold values from 48 to 384, as said below
- cotangent: bfloat16 [32768, 256], P(('row', 'col')), may hold values from -6 to 6
Outputs:
- mixed: bfloat16 [32768, 256], P(('row', 'col'))
- weight_grad: float32 [256, 256], replicated
- bias_grad: float32 [256], replicated
- feature_grad: bfloat16 [32768, 256], P(('col', 'row'))
Inputs may be any that keep to these rules, and one draw needn't show every extreme that they name: Only the first tile_count tiles of a device are used; some device uses all 384.
All inputs are finite; a program needn't handle non-finite values.
Results may differ from a plain program's by a relative error of at most 0.029.
Values may be sent and summed in bfloat16 or wider, within the bound.
No kernel may reach another device: no remote copies, remote signals or barrier semaphores. Data moves between devices by JAX's collectives and lax.ppermute only.
A program may use at most 128 MiB of HBM per device.

v0:
```python
import jax
import jax.numpy as jnp
from jax import lax
from jax.sharding import PartitionSpec as P

RB = 16


def apply_tiles(values, out_idx, in_idx, count, source, out_blocks, flipped):
    tile = values.shape[1]
    width = source.shape[1]
    flat_blocks = source.reshape(-1, tile * width)
    in_blocks = flat_blocks.shape[0]
    total = values.shape[0]
    group = min(64, total)
    turns = total // group
    items = (
        values.reshape(turns, group, tile, tile),
        out_idx.reshape(turns, group),
        in_idx.reshape(turns, group),
        jnp.arange(total, dtype=jnp.int32).reshape(turns, group),
    )
    form = "kba,kbf->kaf" if flipped else "kab,kbf->kaf"
    in_range = jnp.arange(in_blocks, dtype=jnp.int32)
    out_range = jnp.arange(out_blocks, dtype=jnp.int32)

    def step(total_acc, item):
        tiles, targets, sources, places = item
        chooser = (sources[:, None] == in_range[None, :]).astype(jnp.bfloat16)
        picked = jnp.dot(chooser, flat_blocks, preferred_element_type=jnp.float32)
        picked = picked.astype(jnp.bfloat16).reshape(group, tile, width)
        product = jnp.einsum(form, tiles, picked, preferred_element_type=jnp.float32)
        placer = ((targets[None, :] == out_range[:, None]) & (places[None, :] < count)).astype(
            jnp.float32
        )
        added = jnp.dot(
            placer,
            product.reshape(group, tile * width),
            preferred_element_type=jnp.float32,
            precision=lax.Precision.HIGHEST,
        )
        return (total_acc + added, None)

    summed = lax.scan(step, jnp.zeros((out_blocks, tile * width), jnp.float32), items)[0]
    return summed.reshape(out_blocks * tile, width)


def dense_part(aggregated, cot_rows, weight, bias):
    pre = jnp.dot(aggregated, weight, preferred_element_type=jnp.float32) + bias
    mixed = jax.nn.silu(pre).astype(jnp.bfloat16)
    sig = jax.nn.sigmoid(pre)
    slope = (cot_rows.astype(jnp.float32) * sig * (1.0 + pre * (1.0 - sig))).astype(jnp.bfloat16)
    back = jnp.einsum("ng,fg->nf", slope, weight, preferred_element_type=jnp.float32).astype(
        jnp.bfloat16
    )
    wsum = jnp.einsum("nf,ng->fg", aggregated, slope, preferred_element_type=jnp.float32)
    bsum = jnp.sum(slope.astype(jnp.float32), axis=0)
    return (mixed, back, wsum, bsum)


def on_device(features, weight, bias, tile_values, tile_row, tile_col, tile_count, cotangent):
    values = tile_values[0, 0]
    rows_idx = tile_row[0, 0]
    cols_idx = tile_col[0, 0]
    count = tile_count[0, 0]
    panel = lax.all_gather(features, "row", axis=0, tiled=True)
    tile = values.shape[1]
    col_blocks = panel.shape[0] // tile
    partial_value = apply_tiles(values, rows_idx, cols_idx, count, panel, RB, False).astype(
        jnp.bfloat16
    )
    nodes_total = features.shape[0] * lax.axis_size("row") * lax.axis_size("col")
    scale = 1.0 / jnp.sqrt(jnp.float32(nodes_total))
    summed = lax.psum_scatter(partial_value, "col", scatter_dimension=0, tiled=True).astype(
        jnp.float32
    )
    aggregated = summed.astype(jnp.bfloat16)
    mixed, back, wsum, bsum = dense_part(aggregated, cotangent, weight, bias)
    wsum, bsum = lax.psum((wsum, bsum), ("row", "col"))
    back_rows = lax.all_gather(back, "col", axis=0, tiled=True)
    grad_part = apply_tiles(values, cols_idx, rows_idx, count, back_rows, col_blocks, True).astype(
        jnp.bfloat16
    )
    feature_grad = (
        lax.psum_scatter(grad_part, "row", scatter_dimension=0, tiled=True)
        .astype(jnp.float32)
        .astype(jnp.bfloat16)
    )
    return (mixed, wsum * scale, bsum * scale, feature_grad)


def solution(mesh):
    in_specs = (
        P(("col", "row"), None),
        P(),
        P(),
        P("row", "col", None, None, None),
        P("row", "col", None),
        P("row", "col", None),
        P("row", "col"),
        P(("row", "col"), None),
    )
    out_specs = (P(("row", "col"), None), P(), P(), P(("col", "row"), None))
    return jax.shard_map(
        on_device, mesh=mesh, in_specs=in_specs, out_specs=out_specs, check_vma=False
    )
```

profile of v0, /device:TPU:32, one launch (start us, length us, event | category | flops | bytes accessed | tf_op | source)
XLA Modules:
  0.0 524.9 jit_solution(5707611830565337872)
XLA Ops:
  9.5 35.9 %all-gather.3.cloned.1.call-done = bf16[4096,256]{1,0:T(8,128)(2,1)} async-done(((bf16[256,256]{1,0:T(8,128)(2,1)}), bf16[4096,256]{1,0:T(8,128)(2,1)}) %all-gather.3.cloned.1.call-update) | async-done | bytes 2097168 | tf_op jit(solution)/shard_map/all_gather | solution.py:66
  45.4 2.9 reshape.54
  48.3 132.2 %while.22 = (s32[]{:T(128)}, f32[16,32768]{1,0:T(8,128)}, s32[6,64]{1,0:T(8,128)S(1)}, s32[6,64]{1,0:T(8,128)S(1)}, s32[]{:T(128)}, /*index=5*/bf16[6,64,128,128...) while((s32[]{:T(128)}, f32[16,32768]{1,0:T(8,128)}, ...), condition=%wide.region_1.2_spmd.clone, body=%wide.region_0.1_spmd.clone.sunk | while | flops 1076891648 | bytes 58722808 | solution.py:44
  50.7 2.9 fusion.63
  53.6 8.0 %copy.24 = f32[8,8,128,256]{3,1,2,0:T(8,128)} copy(f32[8,8,128,256]{3,2,1,0:T(8,128)S(1)} %bitcast.83) | data formatting | bytes 16777216 | tf_op jit(solution)/shard_map/while
  62.2 7.6 %convolution_add_fusion.5 = f32[16,32768]{1,0:T(8,128)} fusion(f32[64,32768]{1,0:T(8,128)} %bitcast.81, f32[16,32768]{1,0:T(8,128)} %get-tuple-element.336, pred[]{:T(512)S(6)} %compare.6, s32[64]{0:T(128)S(1)} %get-tuple-element.314, pred[64]{0:T(512)(128)(4,1)S(1)} %compare_bitcast_fusion.4), kind=kOutput, calls=%fused_computation.5.clone.1 | convolution fusion | flops 403703808 | bytes 12583233 | tf_op jit(solution)/shard_map/while/body/eval_jaxpr/dot_general | solution.py:36
  72.2 2.9 fusion.63
  75.1 8.0 %copy.24 = f32[8,8,128,256]{3,1,2,0:T(8,128)} copy(f32[8,8,128,256]{3,2,1,0:T(8,128)S(1)} %bitcast.83) | data formatting | bytes 16777216 | tf_op jit(solution)/shard_map/while
  83.7 8.2 %convolution_add_fusion.5 = f32[16,32768]{1,0:T(8,128)} fusion(f32[64,32768]{1,0:T(8,128)} %bitcast.81, f32[16,32768]{1,0:T(8,128)} %get-tuple-element.336, pred[]{:T(512)S(6)} %compare.6, s32[64]{0:T(128)S(1)} %get-tuple-element.314, pred[64]{0:T(512)(128)(4,1)S(1)} %compare_bitcast_fusion.4), kind=kOutput, calls=%fused_computation.5.clone.1 | convolution fusion | flops 403703808 | bytes 12583233 | tf_op jit(solution)/shard_map/while/body/eval_jaxpr/dot_general | solution.py:36
  94.4 2.9 fusion.63
  97.2 8.0 %copy.24 = f32[8,8,128,256]{3,1,2,0:T(8,128)} copy(f32[8,8,128,256]{3,2,1,0:T(8,128)S(1)} %bitcast.83) | data formatting | bytes 16777216 | tf_op jit(solution)/shard_map/while
  105.8 8.2 %convolution_add_fusion.5 = f32[16,32768]{1,0:T(8,128)} fusion(f32[64,32768]{1,0:T(8,128)} %bitcast.81, f32[16,32768]{1,0:T(8,128)} %get-tuple-element.336, pred[]{:T(512)S(6)} %compare.6, s32[64]{0:T(128)S(1)} %get-tuple-element.314, pred[64]{0:T(512)(128)(4,1)S(1)} %compare_bitcast_fusion.4), kind=kOutput, calls=%fused_computation.5.clone.1 | convolution fusion | flops 403703808 | bytes 12583233 | tf_op jit(solution)/shard_map/while/body/eval_jaxpr/dot_general | solution.py:36
  116.5 2.9 fusion.63
  119.3 8.0 %copy.24 = f32[8,8,128,256]{3,1,2,0:T(8,128)} copy(f32[8,8,128,256]{3,2,1,0:T(8,128)S(1)} %bitcast.83) | data formatting | bytes 16777216 | tf_op jit(solution)/shard_map/while
  127.9 8.2 %convolution_add_fusion.5 = f32[16,32768]{1,0:T(8,128)} fusion(f32[64,32768]{1,0:T(8,128)} %bitcast.81, f32[16,32768]{1,0:T(8,128)} %get-tuple-element.336, pred[]{:T(512)S(6)} %compare.6, s32[64]{0:T(128)S(1)} %get-tuple-element.314, pred[64]{0:T(512)(128)(4,1)S(1)} %compare_bitcast_fusion.4), kind=kOutput, calls=%fused_computation.5.clone.1 | convolution fusion | flops 403703808 | bytes 12583233 | tf_op jit(solution)/shard_map/while/body/eval_jaxpr/dot_general | solution.py:36
  138.6 2.9 fusion.63
  141.5 8.0 %copy.24 = f32[8,8,128,256]{3,1,2,0:T(8,128)} copy(f32[8,8,128,256]{3,2,1,0:T(8,128)S(1)} %bitcast.83) | data formatting | bytes 16777216 | tf_op jit(solution)/shard_map/while
  150.1 8.2 %convolution_add_fusion.5 = f32[16,32768]{1,0:T(8,128)} fusion(f32[64,32768]{1,0:T(8,128)} %bitcast.81, f32[16,32768]{1,0:T(8,128)} %get-tuple-element.336, pred[]{:T(512)S(6)} %compare.6, s32[64]{0:T(128)S(1)} %get-tuple-element.314, pred[64]{0:T(512)(128)(4,1)S(1)} %compare_bitcast_fusion.4), kind=kOutput, calls=%fused_computation.5.clone.1 | convolution fusion | flops 403703808 | bytes 12583233 | tf_op jit(solution)/shard_map/while/body/eval_jaxpr/dot_general | solution.py:36
  160.7 2.9 fusion.63
  163.6 8.0 %copy.24 = f32[8,8,128,256]{3,1,2,0:T(8,128)} copy(f32[8,8,128,256]{3,2,1,0:T(8,128)S(1)} %bitcast.83) | data formatting | bytes 16777216 | tf_op jit(solution)/shard_map/while
  172.2 8.2 %convolution_add_fusion.5 = f32[16,32768]{1,0:T(8,128)} fusion(f32[64,32768]{1,0:T(8,128)} %bitcast.81, f32[16,32768]{1,0:T(8,128)} %get-tuple-element.336, pred[]{:T(512)S(6)} %compare.6, s32[64]{0:T(128)S(1)} %get-tuple-element.314, pred[64]{0:T(512)(128)(4,1)S(1)} %compare_bitcast_fusion.4), kind=kOutput, calls=%fused_computation.5.clone.1 | convolution fusion | flops 403703808 | bytes 12583233 | tf_op jit(solution)/shard_map/while/body/eval_jaxpr/dot_general | solution.py:36
  180.4 1.7 convert_element_type.41
  183.7 71.9 %reduce-scatter.3.cloned.1.call-done = bf16[256,256]{1,0:T(8,128)(2,1)} async-done(((bf16[2048,256]{1,0:T(8,128)(2,1)}), bf16[256,256]{1,0:T(8,128)(2,1)}) %reduce-scatter.3.cloned.1.call-update) | async-done | bytes 131088 | tf_op jit(solution)/shard_map/reduce_scatter | solution.py:74
  255.6 1.9 convert_reduce_fusion
  258.4 16.6 %copy.12 = bf16[1,1,384,128,128]{3,4,2,1,0:T(8,128)(2,1)} copy(bf16[1,1,384,128,128]{4,3,2,1,0:T(8,128)(2,1)} %bitcast.90) | data formatting | bytes 25165824 | tf_op args[3]
  276.1 28.1 %all-gather.5.cloned.1.call-done = bf16[2048,256]{1,0:T(8,128)(2,1)} async-done(((bf16[256,256]{1,0:T(8,128)(2,1)}), bf16[2048,256]{1,0:T(8,128)(2,1)}) %all-gather.5.cloned.1.call-update) | async-done | bytes 1048592 | tf_op jit(solution)/shard_map/all_gather | solution.py:80
  305.8 142.5 %while.23 = (s32[]{:T(128)}, f32[32,32768]{1,0:T(8,128)}, s32[6,64]{1,0:T(8,128)S(1)}, s32[6,64]{1,0:T(8,128)S(1)}, s32[]{:T(128)}, /*index=5*/bf16[6,64,128,128...) while((s32[]{:T(128)}, f32[32,32768]{1,0:T(8,128)}, ...), condition=%wide.region_7.8_spmd.clone, body=%wide.region_6.7_spmd.clone.sunk | while | flops 1413485568 | bytes 61868536 | solution.py:44
  308.2 2.9 fusion.70
  311.0 7.9 %copy.26 = f32[8,8,128,256]{3,1,2,0:T(8,128)} copy(f32[8,8,128,256]{3,2,1,0:T(8,128)S(1)} %bitcast.84) | data formatting | bytes 16777216 | tf_op jit(solution)/shard_map/while
  319.6 8.9 %convolution_add_fusion.6 = f32[32,32768]{1,0:T(8,128)} fusion(f32[64,32768]{1,0:T(8,128)} %bitcast.82, f32[32,32768]{1,0:T(8,128)} %get-tuple-element.366, pred[]{:T(512)S(6)} %compare.7, s32[64]{0:T(128)S(1)} %get-tuple-element.324, pred[64]{0:T(512)(128)(4,1)S(1)} %compare_bitcast_fusion.5), kind=kOutput, calls=%fused_computation.23.clone.1 | convolution fusion | flops 807407616 | bytes 16777536 | tf_op jit(solution)/shard_map/while/body/eval_jaxpr/dot_general | solution.py:36
  330.9 2.9 fusion.70
  333.8 7.9 %copy.26 = f32[8,8,128,256]{3,1,2,0:T(8,128)} copy(f32[8,8,128,256]{3,2,1,0:T(8,128)S(1)} %bitcast.84) | data formatting | bytes 16777216 | tf_op jit(solution)/shard_map/while
  342.4 10.1 %convolution_add_fusion.6 = f32[32,32768]{1,0:T(8,128)} fusion(f32[64,32768]{1,0:T(8,128)} %bitcast.82, f32[32,32768]{1,0:T(8,128)} %get-tuple-element.366, pred[]{:T(512)S(6)} %compare.7, s32[64]{0:T(128)S(1)} %get-tuple-element.324, pred[64]{0:T(512)(128)(4,1)S(1)} %compare_bitcast_fusion.5), kind=kOutput, calls=%fused_computation.23.clone.1 | convolution fusion | flops 807407616 | bytes 16777536 | tf_op jit(solution)/shard_map/while/body/eval_jaxpr/dot_general | solution.py:36
  354.8 2.9 fusion.70
  357.7 7.9 %copy.26 = f32[8,8,128,256]{3,1,2,0:T(8,128)} copy(f32[8,8,128,256]{3,2,1,0:T(8,128)S(1)} %bitcast.84) | data formatting | bytes 16777216 | tf_op jit(solution)/shard_map/while
  366.3 10.1 %convolution_add_fusion.6 = f32[32,32768]{1,0:T(8,128)} fusion(f32[64,32768]{1,0:T(8,128)} %bitcast.82, f32[32,32768]{1,0:T(8,128)} %get-tuple-element.366, pred[]{:T(512)S(6)} %compare.7, s32[64]{0:T(128)S(1)} %get-tuple-element.324, pred[64]{0:T(512)(128)(4,1)S(1)} %compare_bitcast_fusion.5), kind=kOutput, calls=%fused_computation.23.clone.1 | convolution fusion | flops 807407616 | bytes 16777536 | tf_op jit(solution)/shard_map/while/body/eval_jaxpr/dot_general | solution.py:36
  378.8 2.9 fusion.70
  381.7 7.9 %copy.26 = f32[8,8,128,256]{3,1,2,0:T(8,128)} copy(f32[8,8,128,256]{3,2,1,0:T(8,128)S(1)} %bitcast.84) | data formatting | bytes 16777216 | tf_op jit(solution)/shard_map/while
  390.3 10.1 %convolution_add_fusion.6 = f32[32,32768]{1,0:T(8,128)} fusion(f32[64,32768]{1,0:T(8,128)} %bitcast.82, f32[32,32768]{1,0:T(8,128)} %get-tuple-element.366, pred[]{:T(512)S(6)} %compare.7, s32[64]{0:T(128)S(1)} %get-tuple-element.324, pred[64]{0:T(512)(128)(4,1)S(1)} %compare_bitcast_fusion.5), kind=kOutput, calls=%fused_computation.23.clone.1 | convolution fusion | flops 807407616 | bytes 16777536 | tf_op jit(solution)/shard_map/while/body/eval_jaxpr/dot_general | solution.py:36
  402.7 2.9 fusion.70
  405.6 7.9 %copy.26 = f32[8,8,128,256]{3,1,2,0:T(8,128)} copy(f32[8,8,128,256]{3,2,1,0:T(8,128)S(1)} %bitcast.84) | data formatting | bytes 16777216 | tf_op jit(solution)/shard_map/while
  414.2 10.1 %convolution_add_fusion.6 = f32[32,32768]{1,0:T(8,128)} fusion(f32[64,32768]{1,0:T(8,128)} %bitcast.82, f32[32,32768]{1,0:T(8,128)} %get-tuple-element.366, pred[]{:T(512)S(6)} %compare.7, s32[64]{0:T(128)S(1)} %get-tuple-element.324, pred[64]{0:T(512)(128)(4,1)S(1)} %compare_bitcast_fusion.5), kind=kOutput, calls=%fused_computation.23.clone.1 | convolution fusion | flops 807407616 | bytes 16777536 | tf_op jit(solution)/shard_map/while/body/eval_jaxpr/dot_general | solution.py:36
  426.7 2.9 fusion.70
  429.6 7.9 %copy.26 = f32[8,8,128,256]{3,1,2,0:T(8,128)} copy(f32[8,8,128,256]{3,2,1,0:T(8,128)S(1)} %bitcast.84) | data formatting | bytes 16777216 | tf_op jit(solution)/shard_map/while
  438.2 10.1 %convolution_add_fusion.6 = f32[32,32768]{1,0:T(8,128)} fusion(f32[64,32768]{1,0:T(8,128)} %bitcast.82, f32[32,32768]{1,0:T(8,128)} %get-tuple-element.366, pred[]{:T(512)S(6)} %compare.7, s32[64]{0:T(128)S(1)} %get-tuple-element.324, pred[64]{0:T(512)(128)(4,1)S(1)} %compare_bitcast_fusion.5), kind=kOutput, calls=%fused_computation.23.clone.1 | convolution fusion | flops 807407616 | bytes 16777536 | tf_op jit(solution)/shard_map/while/body/eval_jaxpr/dot_general | solution.py:36
  448.3 2.4 convert_element_type.48
  450.7 2.3 convert_element_type.49
  453.1 63.1 %psum.15 = f32[256]{0:T(256)S(1)} all-reduce(f32[256]{0:T(256)S(1)} %get-tuple-element.212), channel_id=1, replica_groups=mesh['row'=16,'col'=8] {'row','col'}, use_global_device_ids=true, to_apply=%region_5.6 | all-reduce | flops 256 | bytes 2048 | tf_op jit(solution)/shard_map/psum | solution.py:79
  (83 shorter events, 46.2 us)
Async XLA Ops:
  7.2 248.5 %copy-start = (bf16[256,256]{1,0:T(8,128)(2,1)S(1)}, bf16[256,256]{1,0:T(8,128)(2,1)}, u32[]{:S(2)}) copy-start(bf16[256,256]{1,0:T(8,128)(2,1)} %param.13) | copy-start | bytes 393220
  7.2 38.2 %all-gather.3.cloned.1.call-start = ((), (), s32[]{:S(2)}) async-start(), calls=%async_computation.2 | async-start | bytes 2228224 | tf_op jit(solution)/shard_map/all_gather | solution.py:66
  7.9 247.7 %reduce-scatter.3.cloned.1.call-start = ((), (), s32[]{:S(2)}) async-start(), calls=%async_computation.3 | async-start | bytes 1179648 | tf_op jit(solution)/shard_map/reduce_scatter | solution.py:74
  180.4 75.2 %copy-start.3 = (bf16[256,256]{1,0:T(8,128)(2,1)S(1)}, bf16[256,256]{1,0:T(8,128)(2,1)}, u32[]{:S(2)}) copy-start(bf16[256,256]{1,0:T(8,128)(2,1)} %param.19) | copy-start | bytes 393220
  180.4 75.2 %copy-start.4 = (f32[256]{0:T(256)S(1)}, f32[256]{0:T(256)}, u32[]{:S(2)}) copy-start(f32[256]{0:T(256)} %param.14) | copy-start | bytes 3076
  183.5 120.7 %all-gather.5.cloned.1.call-start = ((), (), s32[]{:S(2)}) async-start(), calls=%async_computation.5 | async-start | bytes 1179648 | tf_op jit(solution)/shard_map/all_gather | solution.py:80
  258.4 16.7 %copy-start.2 = (bf16[256,256]{1,0:T(8,128)(2,1)S(1)}, bf16[256,256]{1,0:T(8,128)(2,1)}, u32[]{:S(2)}) copy-start(bf16[256,256]{1,0:T(8,128)(2,1)} %reduce-scatter.3.cloned.1.call-done) | copy-start | bytes 393220
  258.4 258.3 %all-reduce.2.cloned.1.call-start = ((), (), s32[]{:S(2)}) async-start(), calls=%async_computation.4 | async-start | bytes 524288 | tf_op jit(solution)/shard_map/psum | solution.py:79
  276.0 242.4 %reduce-scatter.5.cloned.1.call-start = ((), (), s32[]{:S(2)}) async-start(), calls=%async_computation.6 | async-start | bytes 2228224 | tf_op jit(solution)/shard_map/reduce_scatter | solution.py:85
  448.3 70.1 %copy-start.1 = (bf16[256,256]{1,0:T(8,128)(2,1)S(1)}, bf16[256,256]{1,0:T(8,128)(2,1)}, u32[]{:S(2)}) copy-start(bf16[256,256]{1,0:T(8,128)(2,1)} %param.13) | copy-start | bytes 393220
Sparse Core Ops, SparseCore 0:
  9.7 35.6 all-gather.2
  183.6 71.9 reduce-scatter.2
  258.8 45.3 all-gather.4
  310.1 139.5 all-reduce.1
  453.2 58.4 reduce-scatter.4
where the time goes:
time: 530 us; the launch traced here: 525 us
  matrix products  162 us (31%)
  waiting for transfers between devices  137 us (26%)
  local copies, waits for them, and re-layouts  133 us (25%)
  blocking collectives  63.1 us (12%)
  other arithmetic  15.6 us (3%)
  between operations  13.8 us (3%)
    while x24, local copies, waits for them, and re-layouts  108 us
    dot_general x12, matrix products, step(): jnp.dot(placer, product.reshape(group, tile * width), preferred_element_t...  108 us
    reduce_scatter x1, waiting for transfers between devices, on_device(): lax.psum_scatter(partial_value, 'col', scatter_dimension=0, tiled=True)  71.9 us
    psum x1, blocking collectives, on_device(): wsum, bsum = lax.psum((wsum, bsum), ('row', 'col'))  63.1 us
    all_gather x1, waiting for transfers between devices, on_device(): panel = lax.all_gather(features, 'row', axis=0, tiled=True)  35.9 us
    dot_general x12, matrix products, step(): jnp.einsum(form, tiles, picked, preferred_element_type=jnp.float32)  34.3 us
    all_gather x1, waiting for transfers between devices, on_device(): back_rows = lax.all_gather(back, 'col', axis=0, tiled=True)  28.1 us
    unnamed x11, local copies, waits for them, and re-layouts  16.7 us
  transfers between devices with their start and end apart: 5, of which 3 were waited for; matrix products, arithmetic and copies ran while one was open for 32% of the time, Pallas kernels for 0%

commit v1 on v0

v1 whole, which is shorter than its diff:
```python
import jax
import jax.numpy as jnp
from jax import lax
from jax.experimental import pallas as pl
from jax.experimental.pallas import tpu as pltpu
from jax.sharding import Mesh
from jax.sharding import PartitionSpec as P

TILE = 128
F = 256
KT = 384
RB = 16
CB = 32
SLOTS = 512
FWD = (4, 4)
BWD = (2, 8)
NODES = 32768

AXES = ("xl", "z", "k", "y", "xh")
SIZES = (2, 4, 2, 4, 2)
SHIFTS = (0, 1, 3, 2)

VM = pl.BlockSpec(memory_space=pltpu.VMEM)
SM = pl.BlockSpec(memory_space=pltpu.SMEM)


def shift(value, axis, by):
    n = SIZES[AXES.index(axis)]
    return lax.ppermute(value, axis, [(i, (i + by) % n) for i in range(n)])


def swap(value, axis, bit=1):
    n = SIZES[AXES.index(axis)]
    return lax.ppermute(value, axis, [(i, i ^ bit) for i in range(n)])


def order_one(key_col, key_row, other_col, chunk, spare):
    at = lambda shape, axis: lax.broadcasted_iota(jnp.int32, shape, axis)
    f32 = jnp.float32
    before = (key_col == key_row) & (at((KT, KT), 1) < at((KT, KT), 0))
    rank = jnp.sum(before.astype(f32), axis=1, keepdims=True)
    held = jnp.sum((key_row == at((128, KT), 0)).astype(f32), axis=1, keepdims=True)
    chunks = jnp.floor((held + (chunk - 1.0)) * (1.0 / chunk))
    lower = at((128, 128), 0) < at((128, 128), 1)
    starts = jnp.sum(jnp.where(lower, chunks, 0.0), axis=0, keepdims=True)
    mine = key_col == at((KT, 128), 1)
    start = jnp.sum(jnp.where(mine, starts, 0.0), axis=1, keepdims=True)
    place = (chunk * start + rank).astype(jnp.int32)
    live = key_col < 127
    hit = (place == at((KT, SLOTS), 1)) & live
    tiles = jnp.sum(jnp.where(hit, at((KT, SLOTS), 0).astype(f32), 0.0), axis=0, keepdims=True)
    less = jnp.where(hit, other_col.astype(f32) - spare, 0.0)
    others = jnp.sum(less, axis=0, keepdims=True) + spare
    opens = (place == chunk * at((KT, SLOTS), 1)) & live
    keys = jnp.sum(jnp.where(opens, key_col.astype(f32), 0.0), axis=0, keepdims=True)
    wide = jnp.concatenate([starts, jnp.zeros((1, SLOTS - 128), f32)], axis=1)
    return [tiles, others, keys, wide]


def order_kernel(count_ref, rc_ref, cc_ref, rr_ref, cr_ref, out_ref):
    count = count_ref[0, 0]
    live_c = lax.broadcasted_iota(jnp.int32, (KT, 1), 0) < count
    live_r = lax.broadcasted_iota(jnp.int32, (1, KT), 1) < count
    rc, cc, rr, cr = rc_ref[...], cc_ref[...], rr_ref[...], cr_ref[...]
    fwd = order_one(jnp.where(live_c, rc, 127), jnp.where(live_r, rr, 127), cc, FWD[0], CB)
    bwd = order_one(jnp.where(live_c, cc, 127), jnp.where(live_r, cr, 127), rc, BWD[0], RB)
    out_ref[...] = jnp.concatenate(fwd + bwd, axis=0).astype(jnp.int32)


def order(count, rows_idx, cols_idx):
    return pl.pallas_call(
        order_kernel,
        out_shape=jax.ShapeDtypeStruct((8, SLOTS), jnp.int32),
        in_specs=[SM, VM, VM, VM, VM],
        out_specs=VM,
        name="order_tiles",
    )(
        count,
        rows_idx.reshape(KT, 1),
        cols_idx.reshape(KT, 1),
        rows_idx.reshape(1, KT),
        cols_idx.reshape(1, KT),
    )


def forward_kernel(plan, here, own_ref, other_ref, values, out_ref, panel, acc):
    xl, z, k, y, xh = (here[n] for n in range(5))
    panel[CB] = jnp.zeros((TILE, F), jnp.bfloat16)
    for kk, ref in ((0, own_ref), (1, other_ref)):
        for s, by in enumerate(SHIFTS):
            for xx in range(2):
                piece = (
                    (jnp.bitwise_xor(xl, xx) * 4 + jnp.bitwise_and(z - by, 3)) * 2
                    + jnp.bitwise_xor(k, kk)
                )
                first = (s * 2 + xx) * 2 * TILE
                for h in range(2):
                    panel[2 * piece + h] = ref[first + h * TILE : first + (h + 1) * TILE, :]

    acc[...] = jnp.zeros_like(acc)
    chunk, group = FWD

    def step(q, _):
        found = []
        for u in range(group):
            base = (q * group + u) * chunk
            left = jnp.concatenate([values[plan[0, base + i]] for i in range(chunk)], axis=1)
            right = jnp.concatenate([panel[plan[1, base + i]] for i in range(chunk)], axis=0)
            found.append(jnp.dot(left, right, preferred_element_type=jnp.float32))
        for u in range(group):
            row = plan[2, q * group + u]
            acc[row] = acc[row] + found[u]
        return 0

    lax.fori_loop(0, lax.div(plan[3, RB] + (group - 1), group), step, 0)
    for n in range(RB):
        yy, xx, h = n // 4, (n // 2) % 2, n % 2
        row = (jnp.bitwise_and(y + yy, 3) * 2 + jnp.bitwise_xor(xh, xx)) * 2 + h
        out_ref[n] = acc[row].astype(jnp.bfloat16)


def forward(plan, here, own, other, values):
    return pl.pallas_call(
        forward_kernel,
        out_shape=jax.ShapeDtypeStruct((RB, TILE, F), jnp.bfloat16),
        in_specs=[SM, SM, VM, VM, VM],
        out_specs=VM,
        scratch_shapes=[
            pltpu.VMEM((CB + 1, TILE, F), jnp.bfloat16),
            pltpu.VMEM((RB, TILE, F), jnp.float32),
        ],
        compiler_params=pltpu.CompilerParams(vmem_limit_bytes=40 << 20),
        name="forward_tiles",
    )(plan, here, own, other, values)


def dense_kernel(near, far, weight, bias, cot, mixed_ref, back_ref, grads_ref):
    f32 = jnp.float32
    agg = (near[...] + far[...].astype(f32)).astype(jnp.bfloat16)
    w = weight[...]
    pre = jnp.dot(agg, w, preferred_element_type=f32) + bias[...]
    sig = jax.nn.sigmoid(pre)
    mixed_ref[...] = (pre * sig).astype(jnp.bfloat16)
    slope = (cot[...].astype(f32) * sig * (1.0 + pre * (1.0 - sig))).astype(jnp.bfloat16)
    back = lax.dot_general(slope, w, (((1,), (1,)), ((), ())), preferred_element_type=f32)
    back_ref[...] = back.astype(jnp.bfloat16)
    wsum = lax.dot_general(agg, slope, (((0,), (0,)), ((), ())), preferred_element_type=f32)
    bsum = jnp.sum(slope.astype(f32), axis=0, keepdims=True)
    grads_ref[0:F, :] = wsum.astype(jnp.bfloat16)
    grads_ref[F : F + 16, :] = jnp.broadcast_to(bsum, (16, F)).astype(jnp.bfloat16)


def dense(near, far, weight, bias, cot):
    return pl.pallas_call(
        dense_kernel,
        out_shape=(
            jax.ShapeDtypeStruct((F, F), jnp.bfloat16),
            jax.ShapeDtypeStruct((F, F), jnp.bfloat16),
            jax.ShapeDtypeStruct((F + 16, F), jnp.bfloat16),
        ),
        in_specs=[VM] * 5,
        out_specs=(VM, VM, VM),
        name="dense_part",
    )(near, far, weight, bias.reshape(1, F), cot)


def backward_kernel(plan, here, ref, values, own_ref, other_ref, panel, acc):
    xl, z, k, y, xh = (here[n] for n in range(5))
    panel[RB] = jnp.zeros((TILE, F), jnp.bfloat16)
    for s, by in enumerate(SHIFTS):
        for xx in range(2):
            piece = jnp.bitwise_and(y - by, 3) * 2 + jnp.bitwise_xor(xh, xx)
            first = (s * 2 + xx) * 2 * TILE
            for h in range(2):
                panel[2 * piece + h] = ref[first + h * TILE : first + (h + 1) * TILE, :]
    acc[...] = jnp.zeros_like(acc)
    chunk, group = BWD

    def step(q, _):
        found = []
        for u in range(group):
            base = (q * group + u) * chunk
            left = jnp.concatenate([values[plan[4, base + i]] for i in range(chunk)], axis=0)
            right = jnp.concatenate([panel[plan[5, base + i]] for i in range(chunk)], axis=0)
            found.append(
                lax.dot_general(
                    left, right, (((0,), (0,)), ((), ())), preferred_element_type=jnp.float32
                )
            )
        for u in range(group):
            col = plan[6, q * group + u]
            acc[col] = acc[col] + found[u]
        return 0

    lax.fori_loop(0, lax.div(plan[7, CB] + (group - 1), group), step, 0)
    for kk, out_ref in ((1, other_ref), (0, own_ref)):
        for n in range(CB // 2):
            zz, xx, h = n // 4, (n // 2) % 2, n % 2
            col = (
                (jnp.bitwise_xor(xl, xx) * 4 + jnp.bitwise_and(z + zz, 3)) * 2
                + jnp.bitwise_xor(k, kk)
            ) * 2 + h
            out_ref[n] = acc[col].astype(jnp.bfloat16)


def backward(plan, here, pieces, values):
    half = jax.ShapeDtypeStruct((CB // 2, TILE, F), jnp.bfloat16)
    return pl.pallas_call(
        backward_kernel,
        out_shape=(half, half),
        in_specs=[SM, SM, VM, VM],
        out_specs=(VM, VM),
        scratch_shapes=[
            pltpu.VMEM((RB + 1, TILE, F), jnp.bfloat16),
            pltpu.VMEM((CB, TILE, F), jnp.float32),
        ],
        compiler_params=pltpu.CompilerParams(vmem_limit_bytes=40 << 20),
        name="backward_tiles",
    )(plan, here, pieces, values)


def gather(piece, pair_axis, ring_axis):
    both = jnp.concatenate([piece, swap(piece, pair_axis)], axis=0)
    parts = [both] + [shift(both, ring_axis, by) for by in SHIFTS[1:]]
    return jnp.concatenate(parts, axis=0)


def scatter_sum(parts, pair_axis, ring_axis):
    f32 = jnp.float32
    half = parts[0].shape[0] // 2
    got = [shift(parts[by], ring_axis, by) for by in (1, 2, 3)]
    total = parts[0].astype(f32) + got[0].astype(f32) + got[1].astype(f32) + got[2].astype(f32)
    far = swap(total[half:].astype(jnp.bfloat16), pair_axis)
    return total[:half], far


def all_sum(value):
    for axis, bit in (("k", 1), ("xl", 1), ("z", 1), ("z", 2), ("xh", 1), ("y", 1), ("y", 2)):
        got = swap(value, axis, bit)
        value = (value.astype(jnp.float32) + got.astype(jnp.float32)).astype(jnp.bfloat16)
    return value


def on_device(features, weight, bias, tile_values, tile_row, tile_col, tile_count, cotangent):
    f32 = jnp.float32
    values = tile_values[0, 0]
    here = jnp.stack([lax.axis_index(a) for a in AXES] + [jnp.int32(0)] * 3).astype(jnp.int32)
    plan = order(tile_count, tile_row[0, 0], tile_col[0, 0])

    own = gather(features, "xl", "z")
    other = swap(own, "k")
    partial = forward(plan, here, own, other, values).reshape(4, 2 * F, F)
    near, far = scatter_sum([partial[n] for n in range(4)], "xh", "y")
    mixed, back, grads = dense(near, far, weight, bias, cotangent)

    pieces = gather(back, "xh", "y")
    part_own, part_other = backward(plan, here, pieces, values)
    got = swap(part_other, "k")
    both = (part_own.astype(f32) + got.astype(f32)).astype(jnp.bfloat16)
    both = both.reshape(4, 2 * F, F)
    near, far = scatter_sum([both[n] for n in range(4)], "xl", "z")
    feature_grad = (near + far.astype(f32)).astype(jnp.bfloat16)

    grads = all_sum(grads)
    scale = 1.0 / jnp.sqrt(f32(NODES))
    grads = grads.astype(f32) * scale
    return (mixed, grads[:F], grads[F], feature_grad)


def solution(mesh):
    fine = Mesh(mesh.devices.reshape(SIZES), AXES)
    row, col = ("xl", "z", "k"), ("y", "xh")
    in_specs = (
        P(col + row, None),
        P(),
        P(),
        P(row, col, None, None, None),
        P(row, col, None),
        P(row, col, None),
        P(row, col),
        P(row + col, None),
    )
    out_specs = (P(row + col, None), P(), P(), P(col + row, None))
    return jax.shard_map(
        on_device, mesh=fine, in_specs=in_specs, out_specs=out_specs, check_vma=False
    )
```

time: 530 us -> 141 us (0.27)
  the two profiles are of different devices: /device:TPU:32 before, /device:TPU:16 now
where the time goes in v1:
time: 141 us; the launch traced here: 140 us
  waiting for transfers between devices  63.5 us (45%)
  starting transfers between devices  45.6 us (32%)
  Pallas kernels  19.6 us (14%)
  local copies, waits for them, and re-layouts  7.36 us (5%)
  other arithmetic  2.48 us (2%)
  between operations  1.57 us (1%)
    ppermute x12, waiting for transfers between devices, shift(): return lax.ppermute(value, axis, [(i, (i + by) % n) for i in range(n)])  40.4 us
    ppermute x13, starting transfers between devices, swap(): return lax.ppermute(value, axis, [(i, i ^ bit) for i in range(n)])  24.3 us
    ppermute x13, waiting for transfers between devices, swap(): return lax.ppermute(value, axis, [(i, i ^ bit) for i in range(n)])  23.2 us
    ppermute x12, starting transfers between devices, shift(): return lax.ppermute(value, axis, [(i, (i + by) % n) for i in range(n)])  21.4 us
    pallas_call x1, Pallas kernels, forward(): pl.pallas_call(forward_kernel, out_shape=jax.ShapeDtypeStruct((RB, TILE,...  7.27 us
    pallas_call x1, Pallas kernels, backward(): pl.pallas_call(backward_kernel, out_shape=(half, half), in_specs=[SM, SM,...  7.21 us
    unnamed x16, local copies, waits for them, and re-layouts  3.37 us
    pallas_call x1, Pallas kernels, order(): pl.pallas_call(order_kernel, out_shape=jax.ShapeDtypeStruct((8, SLOTS), j...  2.92 us
  transfers between devices with their start and end apart: 25, of which 15 were waited for; matrix products, arithmetic and copies ran while one was open for 5% of the time, Pallas kernels for 7%

profile of v1, /device:TPU:16, one launch (start us, length us, event | category | flops | bytes accessed | tf_op | source)
XLA Modules:
  0.0 140.2 jit_solution(11814001101612326947)
XLA Ops:
  0.7 1.6 %collective-permute-start = (bf16[256,256]{1,0:T(8,128)(2,1)}, bf16[256,256]{1,0:T(8,128)(2,1)S(1)}, u32[]{:S(2)}, u32[]{:S(2)}) collective-permute-start(bf16[256,256]{1,0:T(8,128)(2,1)} %param.8), channel_id=1, source_target_pairs={{0,64},{64,0},{1,65},{65,1},{2,66},{66,2},{3,67},{67,3},{4,68},{68... | collective-permute-start | bytes 393224 | tf_op jit(solution)/shard_map/ppermute | solution.py:34
  2.2 1.0 constant_dynamic-update-slice_fusion.1
  3.2 3.0 %collective-permute-done = bf16[256,256]{1,0:T(8,128)(2,1)S(1)} collective-permute-done((bf16[256,256]{1,0:T(8,128)(2,1)}, bf16[256,256]{1,0:T(8,128)(2,1)S(1)}, u32[]{:S(2)}, u32[]{:S(2)}) %collective-permute-start) | collective-permute-done | bytes 131104 | tf_op jit(solution)/shard_map/ppermute | solution.py:34
  6.2 2.0 %collective-permute-start.1 = (bf16[512,256]{1,0:T(8,128)(2,1)S(1)}, bf16[512,256]{1,0:T(8,128)(2,1)S(1)}, u32[]{:S(2)}, u32[]{:S(2)}) collective-permute-start(bf16[512,256]{1,0:T(8,128)(2,1)S(1)} %get-tuple-element.26), channel_id=1, source_target_pairs={{0,16},{16,32},{32,48},{48,0},{1,17},{17,33},{33,49},{49,1},{2,18}... | collective-permute-start | bytes 786440 | tf_op jit(solution)/shard_map/ppermute | solution.py:29
  8.2 2.2 %collective-permute-start.2 = (bf16[512,256]{1,0:T(8,128)(2,1)S(1)}, bf16[512,256]{1,0:T(8,128)(2,1)S(1)}, u32[]{:S(2)}, u32[]{:S(2)}) collective-permute-start(bf16[512,256]{1,0:T(8,128)(2,1)S(1)} %get-tuple-element.26), channel_id=1, source_target_pairs={{0,48},{16,0},{32,16},{48,32},{1,49},{17,1},{33,17},{49,33},{2,50}... | collective-permute-start | bytes 786440 | tf_op jit(solution)/shard_map/ppermute | solution.py:29
  10.4 1.8 %collective-permute-start.3 = (bf16[512,256]{1,0:T(8,128)(2,1)S(1)}, bf16[512,256]{1,0:T(8,128)(2,1)S(1)}, u32[]{:S(2)}, u32[]{:S(2)}) collective-permute-start(bf16[512,256]{1,0:T(8,128)(2,1)S(1)} %get-tuple-element.26), channel_id=1, source_target_pairs={{0,32},{16,48},{32,0},{48,16},{1,33},{17,49},{33,1},{49,17},{2,34}... | collective-permute-start | bytes 786440 | tf_op jit(solution)/shard_map/ppermute | solution.py:29
  12.2 4.5 %collective-permute-done.1 = bf16[512,256]{1,0:T(8,128)(2,1)S(1)} collective-permute-done((bf16[512,256]{1,0:T(8,128)(2,1)S(1)}, bf16[512,256]{1,0:T(8,128)(2,1)S(1)}, u32[]{:S(2)}, u32[]{:S(2)}) %collective-permute-start.1) | collective-permute-done | bytes 262176 | tf_op jit(solution)/shard_map/ppermute | solution.py:29
  16.7 4.1 %collective-permute-done.2 = bf16[512,256]{1,0:T(8,128)(2,1)S(1)} collective-permute-done((bf16[512,256]{1,0:T(8,128)(2,1)S(1)}, bf16[512,256]{1,0:T(8,128)(2,1)S(1)}, u32[]{:S(2)}, u32[]{:S(2)}) %collective-permute-start.2) | collective-permute-done | bytes 262176 | tf_op jit(solution)/shard_map/ppermute | solution.py:29
  20.8 1.8 %collective-permute-done.3 = bf16[512,256]{1,0:T(8,128)(2,1)S(1)} collective-permute-done((bf16[512,256]{1,0:T(8,128)(2,1)S(1)}, bf16[512,256]{1,0:T(8,128)(2,1)S(1)}, u32[]{:S(2)}, u32[]{:S(2)}) %collective-permute-start.3) | collective-permute-done | bytes 262176 | tf_op jit(solution)/shard_map/ppermute | solution.py:29
  22.7 0.8 copy.12.rc_ref
  23.5 0.8 copy.13.cc_ref
  25.0 2.9 %order_tiles.1.plan = s32[8,512]{1,0:T(8,128)} custom-call(s32[1,1]{1,0:T(1,128)S(6)} %copy.24.count_ref, s32[384,1]{1,0:T(8,128)} %copy.12.rc_ref, s32[384,1]{1,0:T(8,128)} %copy.13.cc_ref, s32[1,384]{1,0:T(1,128)} %bitcast.32, s32[1,384]{1,0:T(1,128)} %bitcast.34), custom_call_target="tpu_custom_call" | custom-call | tf_op jit(solution)/shard_map/order_tiles/pallas_call | solution.py:71
  28.0 0.7 copy-done
  28.7 7.3 %forward_tiles.1 = bf16[16,128,256]{2,1,0:T(8,128)(2,1)S(1)} custom-call(s32[8,512]{1,0:T(8,128)S(1)} %copy-done, s32[8]{0:T(128)S(1)} %stack.23.here, bf16[2048,256]{1,0:T(8,128)(2,1)S(1)} %constant_dynamic-update-slice_fusion.2.own_ref, bf16[2048,256]{1,0:T(8,128)(2,1)S(1)} %collective-permute-done.4.other_ref, bf16[384,128,128]{2,1,0:T(8,128)(2,1)} %bitcast.24), custom_call_target="tpu_custom_call" | custom-call | tf_op jit(solution)/shard_map/forward_tiles/pallas_call | solution.py:123
  36.1 6.9 %collective-permute-start.5 = (bf16[512,256]{1,0:T(8,128)(2,1)S(1)}, bf16[512,256]{1,0:T(8,128)(2,1)S(1)}, u32[]{:S(2)}, u32[]{:S(2)}) collective-permute-start(bf16[512,256]{1,0:T(8,128)(2,1)S(1)} %bitcast.31), channel_id=1, source_target_pairs={{0,2},{2,4},{4,6},{6,0},{1,3},{3,5},{5,7},{7,1},{8,10},{10,12},{12... | collective-permute-start | bytes 786440 | tf_op jit(solution)/shard_map/ppermute | solution.py:29
  43.0 1.6 %collective-permute-start.7 = (bf16[512,256]{1,0:T(8,128)(2,1)S(1)}, bf16[512,256]{1,0:T(8,128)(2,1)S(1)}, u32[]{:S(2)}, u32[]{:S(2)}) collective-permute-start(bf16[512,256]{1,0:T(8,128)(2,1)S(1)} %bitcast.29), channel_id=1, source_target_pairs={{0,6},{2,0},{4,2},{6,4},{1,7},{3,1},{5,3},{7,5},{8,14},{10,8},{12,... | collective-permute-start | bytes 786440 | tf_op jit(solution)/shard_map/ppermute | solution.py:29
  44.6 5.1 %collective-permute-done.5 = bf16[512,256]{1,0:T(8,128)(2,1)S(1)} collective-permute-done((bf16[512,256]{1,0:T(8,128)(2,1)S(1)}, bf16[512,256]{1,0:T(8,128)(2,1)S(1)}, u32[]{:S(2)}, u32[]{:S(2)}) %collective-permute-start.5) | collective-permute-done | bytes 262176 | tf_op jit(solution)/shard_map/ppermute | solution.py:29
  49.7 4.6 %collective-permute-done.6 = bf16[512,256]{1,0:T(8,128)(2,1)S(1)} collective-permute-done((bf16[512,256]{1,0:T(8,128)(2,1)S(1)}, bf16[512,256]{1,0:T(8,128)(2,1)S(1)}, u32[]{:S(2)}, u32[]{:S(2)}) %collective-permute-start.6) | collective-permute-done | bytes 262176 | tf_op jit(solution)/shard_map/ppermute | solution.py:29
  54.3 0.9 collective-permute-done.7
  55.4 5.9 %collective-permute-start.8 = (bf16[256,256]{1,0:T(8,128)(2,1)S(1)}, bf16[256,256]{1,0:T(8,128)(2,1)S(1)}, u32[]{:S(2)}, u32[]{:S(2)}) collective-permute-start(bf16[256,256]{1,0:T(8,128)(2,1)S(1)} %slice.86), channel_id=1, source_target_pairs={{0,1},{1,0},{2,3},{3,2},{4,5},{5,4},{6,7},{7,6},{8,9},{9,8},{10,11... | collective-permute-start | bytes 393224 | tf_op jit(solution)/shard_map/ppermute | solution.py:34
  61.3 0.7 slice.70.near
  62.0 2.7 %collective-permute-done.8.far = bf16[256,256]{1,0:T(8,128)(2,1)S(1)} collective-permute-done((bf16[256,256]{1,0:T(8,128)(2,1)S(1)}, bf16[256,256]{1,0:T(8,128)(2,1)S(1)}, u32[]{:S(2)}, u32[]{:S(2)}) %collective-permute-start.8) | collective-permute-done | bytes 131104 | tf_op jit(solution)/shard_map/ppermute | solution.py:34
  64.7 0.7 copy-done.2
  65.4 2.2 %dense_part.1 = (bf16[256,256]{1,0:T(8,128)(2,1)}, bf16[256,256]{1,0:T(8,128)(2,1)}, bf16[272,256]{1,0:T(8,128)(2,1)}) custom-call(f32[256,256]{1,0:T(8,128)} %slice.70.near, bf16[256,256]{1,0:T(8,128)(2,1)} %copy-done.2, bf16[256,256]{1,0:T(8,128)(2,1)} %weight.1, f32[1,256]{1,0:T(1,128)} %bitcast.36, bf16[256,256]{1,0:T(8,128)(2,1)} %cot.1), custom_call_target="tpu_custom_call" | custom-call | tf_op jit(solution)/shard_map/dense_part/pallas_call | solution.py:154
  67.6 3.2 %collective-permute-start.16 = (bf16[256,256]{1,0:T(8,128)(2,1)}, bf16[256,256]{1,0:T(8,128)(2,1)S(1)}, u32[]{:S(2)}, u32[]{:S(2)}) collective-permute-start(bf16[256,256]{1,0:T(8,128)(2,1)} %get-tuple-element.11), channel_id=1, source_target_pairs={{0,1},{1,0},{2,3},{3,2},{4,5},{5,4},{6,7},{7,6},{8,9},{9,8},{10,11... | collective-permute-start | bytes 393224 | tf_op jit(solution)/shard_map/ppermute | solution.py:34
  70.8 1.0 constant_dynamic-update-slice_fusion.8
  71.8 0.9 add_convert_fusion.7
  72.8 2.8 %collective-permute-done.16 = bf16[256,256]{1,0:T(8,128)(2,1)S(1)} collective-permute-done((bf16[256,256]{1,0:T(8,128)(2,1)}, bf16[256,256]{1,0:T(8,128)(2,1)S(1)}, u32[]{:S(2)}, u32[]{:S(2)}) %collective-permute-start.16) | collective-permute-done | bytes 131104 | tf_op jit(solution)/shard_map/ppermute | solution.py:34
  75.6 0.8 collective-permute-start.17
  76.4 1.3 collective-permute-start.18
  77.7 1.5 %collective-permute-start.19 = (bf16[512,256]{1,0:T(8,128)(2,1)S(1)}, bf16[512,256]{1,0:T(8,128)(2,1)S(1)}, u32[]{:S(2)}, u32[]{:S(2)}) collective-permute-start(bf16[512,256]{1,0:T(8,128)(2,1)S(1)} %get-tuple-element.22), channel_id=1, source_target_pairs={{0,4},{2,6},{4,0},{6,2},{1,5},{3,7},{5,1},{7,3},{8,12},{10,14},{12... | collective-permute-start | bytes 786440 | tf_op jit(solution)/shard_map/ppermute | solution.py:29
  79.3 1.0 collective-permute-start.11
  80.3 8.6 %collective-permute-done.17 = bf16[512,256]{1,0:T(8,128)(2,1)S(1)} collective-permute-done((bf16[512,256]{1,0:T(8,128)(2,1)S(1)}, bf16[512,256]{1,0:T(8,128)(2,1)S(1)}, u32[]{:S(2)}, u32[]{:S(2)}) %collective-permute-start.17) | collective-permute-done | bytes 262176 | tf_op jit(solution)/shard_map/ppermute | solution.py:29
  89.0 7.2 %backward_tiles.1 = (bf16[16,128,256]{2,1,0:T(8,128)(2,1)S(1)}, bf16[16,128,256]{2,1,0:T(8,128)(2,1)S(1)}) custom-call(s32[8,512]{1,0:T(8,128)S(1)} %copy-done.1, s32[8]{0:T(128)S(1)} %stack.23.here, bf16[2048,256]{1,0:T(8,128)(2,1)S(1)} %constant_dynamic-update-slice_fusion.9.ref, bf16[384,128,128]{2,1,0:T(8,128)(2,1)} %bitcast.25), custom_call_target="tpu_custom_call" | custom-call | tf_op jit(solution)/shard_map/backward_tiles/pallas_call | solution.py:208
  96.4 7.5 %collective-permute-done.12 = bf16[272,256]{1,0:T(8,128)(2,1)S(1)} collective-permute-done((bf16[272,256]{1,0:T(8,128)(2,1)S(1)}, bf16[272,256]{1,0:T(8,128)(2,1)S(1)}, u32[]{:S(2)}, u32[]{:S(2)}) %collective-permute-start.12) | collective-permute-done | bytes 139296 | tf_op jit(solution)/shard_map/ppermute | solution.py:34
  104.0 9.5 %collective-permute-start.13 = (bf16[272,256]{1,0:T(8,128)(2,1)S(1)}, bf16[272,256]{1,0:T(8,128)(2,1)S(1)}, u32[]{:S(2)}, u32[]{:S(2)}) collective-permute-start(bf16[272,256]{1,0:T(8,128)(2,1)S(1)} %add_convert_fusion.4), channel_id=1, source_target_pairs={{0,1},{1,0},{2,3},{3,2},{4,5},{5,4},{6,7},{7,6},{8,9},{9,8},{10,11... | collective-permute-start | bytes 417800 | tf_op jit(solution)/shard_map/ppermute | solution.py:34
  113.6 3.5 %collective-permute-done.13 = bf16[272,256]{1,0:T(8,128)(2,1)S(1)} collective-permute-done((bf16[272,256]{1,0:T(8,128)(2,1)S(1)}, bf16[272,256]{1,0:T(8,128)(2,1)S(1)}, u32[]{:S(2)}, u32[]{:S(2)}) %collective-permute-start.13) | collective-permute-done | bytes 139296 | tf_op jit(solution)/shard_map/ppermute | solution.py:34
  117.1 2.5 %collective-permute-start.14 = (bf16[272,256]{1,0:T(8,128)(2,1)S(1)}, bf16[272,256]{1,0:T(8,128)(2,1)S(1)}, u32[]{:S(2)}, u32[]{:S(2)}) collective-permute-start(bf16[272,256]{1,0:T(8,128)(2,1)S(1)} %add_convert_fusion.3), channel_id=1, source_target_pairs={{0,2},{2,0},{4,6},{6,4},{1,3},{3,1},{5,7},{7,5},{8,10},{10,8},{12,... | collective-permute-start | bytes 417800 | tf_op jit(solution)/shard_map/ppermute | solution.py:34
  119.6 0.3 add_convert_fusion
  120.1 0.9 collective-permute-start.22
  121.0 2.3 %collective-permute-start.23 = (bf16[512,256]{1,0:T(8,128)(2,1)S(1)}, bf16[512,256]{1,0:T(8,128)(2,1)S(1)}, u32[]{:S(2)}, u32[]{:S(2)}) collective-permute-start(bf16[512,256]{1,0:T(8,128)(2,1)S(1)} %bitcast.26), channel_id=1, source_target_pairs={{0,48},{16,0},{32,16},{48,32},{1,49},{17,1},{33,17},{49,33},{2,50}... | collective-permute-start | bytes 786440 | tf_op jit(solution)/shard_map/ppermute | solution.py:29
  123.5 10.2 %collective-permute-done.21 = bf16[512,256]{1,0:T(8,128)(2,1)S(1)} collective-permute-done((bf16[512,256]{1,0:T(8,128)(2,1)S(1)}, bf16[512,256]{1,0:T(8,128)(2,1)S(1)}, u32[]{:S(2)}, u32[]{:S(2)}) %collective-permute-start.21) | collective-permute-done | bytes 262176 | tf_op jit(solution)/shard_map/ppermute | solution.py:29
  133.7 0.6 collective-permute-done.23
  134.3 0.2 fusion.1
  134.6 0.7 slice.72
  135.3 0.6 slice.73
  135.9 3.6 %collective-permute-done.24 = bf16[256,256]{1,0:T(8,128)(2,1)S(1)} collective-permute-done((bf16[256,256]{1,0:T(8,128)(2,1)S(1)}, bf16[256,256]{1,0:T(8,128)(2,1)S(1)}, u32[]{:S(2)}, u32[]{:S(2)}) %collective-permute-start.24) | collective-permute-done | bytes 131104 | tf_op jit(solution)/shard_map/ppermute | solution.py:34
  139.5 0.7 fusion.4
  (48 shorter events, 1.5 us)
Async XLA Ops:
  0.6 22.0 %copy-start.3 = (s32[1,1,384]{2,1,0:T(1,128)S(1)}, s32[1,1,384]{2,1,0:T(1,128)}, u32[]{:S(2)}) copy-start(s32[1,1,384]{2,1,0:T(1,128)} %param.12) | copy-start | bytes 4612
  0.6 22.9 %copy-start.4 = (s32[1,1,384]{2,1,0:T(1,128)S(1)}, s32[1,1,384]{2,1,0:T(1,128)}, u32[]{:S(2)}) copy-start(s32[1,1,384]{2,1,0:T(1,128)} %param.13) | copy-start | bytes 4612
  0.7 5.5 %collective-permute-start = (bf16[256,256]{1,0:T(8,128)(2,1)}, bf16[256,256]{1,0:T(8,128)(2,1)S(1)}, u32[]{:S(2)}, u32[]{:S(2)}) collective-permute-start(bf16[256,256]{1,0:T(8,128)(2,1)} %param.8), channel_id=1, source_target_pairs={{0,64},{64,0},{1,65},{65,1},{2,66},{66,2},{3,67},{67,3},{4,68},{68... | collective-permute-start | bytes 393224 | tf_op jit(solution)/shard_map/ppermute | solution.py:34
  6.2 10.4 %collective-permute-start.1 = (bf16[512,256]{1,0:T(8,128)(2,1)S(1)}, bf16[512,256]{1,0:T(8,128)(2,1)S(1)}, u32[]{:S(2)}, u32[]{:S(2)}) collective-permute-start(bf16[512,256]{1,0:T(8,128)(2,1)S(1)} %get-tuple-element.26), channel_id=1, source_target_pairs={{0,16},{16,32},{32,48},{48,0},{1,17},{17,33},{33,49},{49,1},{2,18}... | collective-permute-start | bytes 786440 | tf_op jit(solution)/shard_map/ppermute | solution.py:29
  8.2 12.5 %collective-permute-start.2 = (bf16[512,256]{1,0:T(8,128)(2,1)S(1)}, bf16[512,256]{1,0:T(8,128)(2,1)S(1)}, u32[]{:S(2)}, u32[]{:S(2)}) collective-permute-start(bf16[512,256]{1,0:T(8,128)(2,1)S(1)} %get-tuple-element.26), channel_id=1, source_target_pairs={{0,48},{16,0},{32,16},{48,32},{1,49},{17,1},{33,17},{49,33},{2,50}... | collective-permute-start | bytes 786440 | tf_op jit(solution)/shard_map/ppermute | solution.py:29
  10.4 12.1 %collective-permute-start.3 = (bf16[512,256]{1,0:T(8,128)(2,1)S(1)}, bf16[512,256]{1,0:T(8,128)(2,1)S(1)}, u32[]{:S(2)}, u32[]{:S(2)}) collective-permute-start(bf16[512,256]{1,0:T(8,128)(2,1)S(1)} %get-tuple-element.26), channel_id=1, source_target_pairs={{0,32},{16,48},{32,0},{48,16},{1,33},{17,49},{33,1},{49,17},{2,34}... | collective-permute-start | bytes 786440 | tf_op jit(solution)/shard_map/ppermute | solution.py:29
  22.6 5.4 %collective-permute-start.4 = (bf16[2048,256]{1,0:T(8,128)(2,1)S(1)}, bf16[2048,256]{1,0:T(8,128)(2,1)S(1)}, u32[]{:S(2)}, u32[]{:S(2)}) collective-permute-start(bf16[2048,256]{1,0:T(8,128)(2,1)S(1)} %constant_dynamic-update-slice_fusion.2.own_ref), channel_id=1, source_target_pairs={{0,8},{8,0},{1,9},{9,1},{2,10},{10,2},{3,11},{11,3},{4,12},{12,4},... | collective-permute-start | bytes 3145736 | tf_op jit(solution)/shard_map/ppermute | solution.py:34
  28.0 0.7 copy-start
  36.1 13.6 %collective-permute-start.5 = (bf16[512,256]{1,0:T(8,128)(2,1)S(1)}, bf16[512,256]{1,0:T(8,128)(2,1)S(1)}, u32[]{:S(2)}, u32[]{:S(2)}) collective-permute-start(bf16[512,256]{1,0:T(8,128)(2,1)S(1)} %bitcast.31), channel_id=1, source_target_pairs={{0,2},{2,4},{4,6},{6,0},{1,3},{3,5},{5,7},{7,1},{8,10},{10,12},{12... | collective-permute-start | bytes 786440 | tf_op jit(solution)/shard_map/ppermute | solution.py:29
  43.0 11.3 %collective-permute-start.6 = (bf16[512,256]{1,0:T(8,128)(2,1)S(1)}, bf16[512,256]{1,0:T(8,128)(2,1)S(1)}, u32[]{:S(2)}, u32[]{:S(2)}) collective-permute-start(bf16[512,256]{1,0:T(8,128)(2,1)S(1)} %bitcast.30), channel_id=1, source_target_pairs={{0,4},{2,6},{4,0},{6,2},{1,5},{3,7},{5,1},{7,3},{8,12},{10,14},{12... | collective-permute-start | bytes 786440 | tf_op jit(solution)/shard_map/ppermute | solution.py:29
  43.0 12.2 %collective-permute-start.7 = (bf16[512,256]{1,0:T(8,128)(2,1)S(1)}, bf16[512,256]{1,0:T(8,128)(2,1)S(1)}, u32[]{:S(2)}, u32[]{:S(2)}) collective-permute-start(bf16[512,256]{1,0:T(8,128)(2,1)S(1)} %bitcast.29), channel_id=1, source_target_pairs={{0,6},{2,0},{4,2},{6,4},{1,7},{3,1},{5,3},{7,5},{8,14},{10,8},{12,... | collective-permute-start | bytes 786440 | tf_op jit(solution)/shard_map/ppermute | solution.py:29
  55.4 33.6 %copy-start.1 = (s32[8,512]{1,0:T(8,128)S(1)}, s32[8,512]{1,0:T(8,128)}, u32[]{:S(2)}) copy-start(s32[8,512]{1,0:T(8,128)} %order_tiles.1.plan) | copy-start | bytes 49156
  55.4 9.3 %collective-permute-start.8 = (bf16[256,256]{1,0:T(8,128)(2,1)S(1)}, bf16[256,256]{1,0:T(8,128)(2,1)S(1)}, u32[]{:S(2)}, u32[]{:S(2)}) collective-permute-start(bf16[256,256]{1,0:T(8,128)(2,1)S(1)} %slice.86), channel_id=1, source_target_pairs={{0,1},{1,0},{2,3},{3,2},{4,5},{5,4},{6,7},{7,6},{8,9},{9,8},{10,11... | collective-permute-start | bytes 393224 | tf_op jit(solution)/shard_map/ppermute | solution.py:34
  64.7 0.7 copy-start.2
  67.6 4.2 %collective-permute-start.9 = (bf16[272,256]{1,0:T(8,128)(2,1)}, bf16[272,256]{1,0:T(8,128)(2,1)S(1)}, u32[]{:S(2)}, u32[]{:S(2)}) collective-permute-start(bf16[272,256]{1,0:T(8,128)(2,1)} %get-tuple-element.10), channel_id=1, source_target_pairs={{0,8},{8,0},{1,9},{9,1},{2,10},{10,2},{3,11},{11,3},{4,12},{12,4},... | collective-permute-start | bytes 417800 | tf_op jit(solution)/shard_map/ppermute | solution.py:34
  67.6 8.0 %collective-permute-start.16 = (bf16[256,256]{1,0:T(8,128)(2,1)}, bf16[256,256]{1,0:T(8,128)(2,1)S(1)}, u32[]{:S(2)}, u32[]{:S(2)}) collective-permute-start(bf16[256,256]{1,0:T(8,128)(2,1)} %get-tuple-element.11), channel_id=1, source_target_pairs={{0,1},{1,0},{2,3},{3,2},{4,5},{5,4},{6,7},{7,6},{8,9},{9,8},{10,11... | collective-permute-start | bytes 393224 | tf_op jit(solution)/shard_map/ppermute | solution.py:34
  72.7 6.5 %collective-permute-start.10 = (bf16[272,256]{1,0:T(8,128)(2,1)S(1)}, bf16[272,256]{1,0:T(8,128)(2,1)S(1)}, u32[]{:S(2)}, u32[]{:S(2)}) collective-permute-start(bf16[272,256]{1,0:T(8,128)(2,1)S(1)} %add_convert_fusion.7), channel_id=1, source_target_pairs={{0,64},{64,0},{1,65},{65,1},{2,66},{66,2},{3,67},{67,3},{4,68},{68... | collective-permute-start | bytes 417800 | tf_op jit(solution)/shard_map/ppermute | solution.py:34
  75.6 13.2 %collective-permute-start.17 = (bf16[512,256]{1,0:T(8,128)(2,1)S(1)}, bf16[512,256]{1,0:T(8,128)(2,1)S(1)}, u32[]{:S(2)}, u32[]{:S(2)}) collective-permute-start(bf16[512,256]{1,0:T(8,128)(2,1)S(1)} %get-tuple-element.22), channel_id=1, source_target_pairs={{0,2},{2,4},{4,6},{6,0},{1,3},{3,5},{5,7},{7,1},{8,10},{10,12},{12... | collective-permute-start | bytes 786440 | tf_op jit(solution)/shard_map/ppermute | solution.py:29
  76.4 12.5 %collective-permute-start.18 = (bf16[512,256]{1,0:T(8,128)(2,1)S(1)}, bf16[512,256]{1,0:T(8,128)(2,1)S(1)}, u32[]{:S(2)}, u32[]{:S(2)}) collective-permute-start(bf16[512,256]{1,0:T(8,128)(2,1)S(1)} %get-tuple-element.22), channel_id=1, source_target_pairs={{0,6},{2,0},{4,2},{6,4},{1,7},{3,1},{5,3},{7,5},{8,14},{10,8},{12,... | collective-permute-start | bytes 786440 | tf_op jit(solution)/shard_map/ppermute | solution.py:29
  77.7 11.2 %collective-permute-start.19 = (bf16[512,256]{1,0:T(8,128)(2,1)S(1)}, bf16[512,256]{1,0:T(8,128)(2,1)S(1)}, u32[]{:S(2)}, u32[]{:S(2)}) collective-permute-start(bf16[512,256]{1,0:T(8,128)(2,1)S(1)} %get-tuple-element.22), channel_id=1, source_target_pairs={{0,4},{2,6},{4,0},{6,2},{1,5},{3,7},{5,1},{7,3},{8,12},{10,14},{12... | collective-permute-start | bytes 786440 | tf_op jit(solution)/shard_map/ppermute | solution.py:29
  79.3 17.0 %collective-permute-start.11 = (bf16[272,256]{1,0:T(8,128)(2,1)S(1)}, bf16[272,256]{1,0:T(8,128)(2,1)S(1)}, u32[]{:S(2)}, u32[]{:S(2)}) collective-permute-start(bf16[272,256]{1,0:T(8,128)(2,1)S(1)} %add_convert_fusion.6), channel_id=1, source_target_pairs={{0,16},{16,0},{32,48},{48,32},{1,17},{17,1},{33,49},{49,33},{2,18}... | collective-permute-start | bytes 417800 | tf_op jit(solution)/shard_map/ppermute | solution.py:34
  96.2 23.4 %collective-permute-start.20 = (bf16[16,128,256]{2,1,0:T(8,128)(2,1)S(1)}, bf16[16,128,256]{2,1,0:T(8,128)(2,1)S(1)}, u32[]{:S(2)}, u32[]{:S(2)}) collective-permute-start(bf16[16,128,256]{2,1,0:T(8,128)(2,1)S(1)} %get-tuple-element.13), channel_id=1, source_target_pairs={{0,8},{8,0},{1,9},{9,1},{2,10},{10,2},{3,11},{11,3},{4,12},{12,4},... | collective-permute-start | bytes 3145736 | tf_op jit(solution)/shard_map/ppermute | solution.py:34
  96.4 7.6 %collective-permute-start.12 = (bf16[272,256]{1,0:T(8,128)(2,1)S(1)}, bf16[272,256]{1,0:T(8,128)(2,1)S(1)}, u32[]{:S(2)}, u32[]{:S(2)}) collective-permute-start(bf16[272,256]{1,0:T(8,128)(2,1)S(1)} %add_convert_fusion.5), channel_id=1, source_target_pairs={{0,32},{16,48},{32,0},{48,16},{1,33},{17,49},{33,1},{49,17},{2,34}... | collective-permute-start | bytes 417800 | tf_op jit(solution)/shard_map/ppermute | solution.py:34
  104.0 13.1 %collective-permute-start.13 = (bf16[272,256]{1,0:T(8,128)(2,1)S(1)}, bf16[272,256]{1,0:T(8,128)(2,1)S(1)}, u32[]{:S(2)}, u32[]{:S(2)}) collective-permute-start(bf16[272,256]{1,0:T(8,128)(2,1)S(1)} %add_convert_fusion.4), channel_id=1, source_target_pairs={{0,1},{1,0},{2,3},{3,2},{4,5},{5,4},{6,7},{7,6},{8,9},{9,8},{10,11... | collective-permute-start | bytes 417800 | tf_op jit(solution)/shard_map/ppermute | solution.py:34
  117.1 6.2 %collective-permute-start.14 = (bf16[272,256]{1,0:T(8,128)(2,1)S(1)}, bf16[272,256]{1,0:T(8,128)(2,1)S(1)}, u32[]{:S(2)}, u32[]{:S(2)}) collective-permute-start(bf16[272,256]{1,0:T(8,128)(2,1)S(1)} %add_convert_fusion.3), channel_id=1, source_target_pairs={{0,2},{2,0},{4,6},{6,4},{1,3},{3,1},{5,7},{7,5},{8,10},{10,8},{12,... | collective-permute-start | bytes 417800 | tf_op jit(solution)/shard_map/ppermute | solution.py:34
  120.0 13.6 %collective-permute-start.21 = (bf16[512,256]{1,0:T(8,128)(2,1)S(1)}, bf16[512,256]{1,0:T(8,128)(2,1)S(1)}, u32[]{:S(2)}, u32[]{:S(2)}) collective-permute-start(bf16[512,256]{1,0:T(8,128)(2,1)S(1)} %bitcast.28), channel_id=1, source_target_pairs={{0,16},{16,32},{32,48},{48,0},{1,17},{17,33},{33,49},{49,1},{2,18}... | collective-permute-start | bytes 786440 | tf_op jit(solution)/shard_map/ppermute | solution.py:29
  120.1 13.6 %collective-permute-start.22 = (bf16[512,256]{1,0:T(8,128)(2,1)S(1)}, bf16[512,256]{1,0:T(8,128)(2,1)S(1)}, u32[]{:S(2)}, u32[]{:S(2)}) collective-permute-start(bf16[512,256]{1,0:T(8,128)(2,1)S(1)} %bitcast.27), channel_id=1, source_target_pairs={{0,32},{16,48},{32,0},{48,16},{1,33},{17,49},{33,1},{49,17},{2,34}... | collective-permute-start | bytes 786440 | tf_op jit(solution)/shard_map/ppermute | solution.py:29
  121.0 13.2 %collective-permute-start.23 = (bf16[512,256]{1,0:T(8,128)(2,1)S(1)}, bf16[512,256]{1,0:T(8,128)(2,1)S(1)}, u32[]{:S(2)}, u32[]{:S(2)}) collective-permute-start(bf16[512,256]{1,0:T(8,128)(2,1)S(1)} %bitcast.26), channel_id=1, source_target_pairs={{0,48},{16,0},{32,16},{48,32},{1,49},{17,1},{33,17},{49,33},{2,50}... | collective-permute-start | bytes 786440 | tf_op jit(solution)/shard_map/ppermute | solution.py:29
  123.4 11.2 %collective-permute-start.15 = (bf16[272,256]{1,0:T(8,128)(2,1)S(1)}, bf16[272,256]{1,0:T(8,128)(2,1)S(1)}, u32[]{:S(2)}, u32[]{:S(2)}) collective-permute-start(bf16[272,256]{1,0:T(8,128)(2,1)S(1)} %add_convert_fusion.2), channel_id=1, source_target_pairs={{0,4},{2,6},{4,0},{6,2},{1,5},{3,7},{5,1},{7,3},{8,12},{10,14},{12... | collective-permute-start | bytes 417800 | tf_op jit(solution)/shard_map/ppermute | solution.py:34
  134.5 5.0 %collective-permute-start.24 = (bf16[256,256]{1,0:T(8,128)(2,1)S(1)}, bf16[256,256]{1,0:T(8,128)(2,1)S(1)}, u32[]{:S(2)}, u32[]{:S(2)}) collective-permute-start(bf16[256,256]{1,0:T(8,128)(2,1)S(1)} %slice.85), channel_id=1, source_target_pairs={{0,64},{64,0},{1,65},{65,1},{2,66},{66,2},{3,67},{67,3},{4,68},{68... | collective-permute-start | bytes 393224 | tf_op jit(solution)/shard_map/ppermute | solution.py:34

commit v2 on v1

v2 whole, which is shorter than its diff:
```python
import functools

import jax
import jax.numpy as jnp
from jax import lax
from jax.experimental import pallas as pl
from jax.experimental.pallas import tpu as pltpu
from jax.sharding import Mesh
from jax.sharding import PartitionSpec as P

TILE = 128
F = 256
KT = 384
RB = 16
CB = 32
SLOTS = 512
FWD = (4, 4)
BWD = (2, 8)
NODES = 32768

AXES = ("xl", "z", "k", "y", "xh")
SIZES = (2, 4, 2, 4, 2)
SHIFTS = (0, 1, 3, 2)

VM = pl.BlockSpec(memory_space=pltpu.VMEM)
SM = pl.BlockSpec(memory_space=pltpu.SMEM)


def shift(value, axis, by):
    n = SIZES[AXES.index(axis)]
    return lax.ppermute(value, axis, [(i, (i + by) % n) for i in range(n)])


def swap(value, axis, bit=1):
    n = SIZES[AXES.index(axis)]
    return lax.ppermute(value, axis, [(i, i ^ bit) for i in range(n)])


def order_one(key_col, key_row, other_col, chunk, spare):
    at = lambda shape, axis: lax.broadcasted_iota(jnp.int32, shape, axis)
    f32 = jnp.float32
    before = (key_col == key_row) & (at((KT, KT), 1) < at((KT, KT), 0))
    rank = jnp.sum(before.astype(f32), axis=1, keepdims=True)
    held = jnp.sum((key_row == at((128, KT), 0)).astype(f32), axis=1, keepdims=True)
    chunks = jnp.floor((held + (chunk - 1.0)) * (1.0 / chunk))
    lower = at((128, 128), 0) < at((128, 128), 1)
    starts = jnp.sum(jnp.where(lower, chunks, 0.0), axis=0, keepdims=True)
    mine = key_col == at((KT, 128), 1)
    start = jnp.sum(jnp.where(mine, starts, 0.0), axis=1, keepdims=True)
    place = (chunk * start + rank).astype(jnp.int32)
    live = key_col < 127
    hit = (place == at((KT, SLOTS), 1)) & live
    tiles = jnp.sum(jnp.where(hit, at((KT, SLOTS), 0).astype(f32), 0.0), axis=0, keepdims=True)
    less = jnp.where(hit, other_col.astype(f32) - spare, 0.0)
    others = jnp.sum(less, axis=0, keepdims=True) + spare
    opens = (place == chunk * at((KT, SLOTS), 1)) & live
    keys = jnp.sum(jnp.where(opens, key_col.astype(f32), 0.0), axis=0, keepdims=True)
    wide = jnp.concatenate([starts, jnp.zeros((1, SLOTS - 128), f32)], axis=1)
    return [tiles, others, keys, wide]


def row_key(row, here):
    piece = row >> 1
    yy = jnp.bitwise_and((piece >> 1) - here[3], 3)
    xx = jnp.bitwise_xor(jnp.bitwise_and(piece, 1), here[4])
    turn = jnp.where(yy == 2, 0, jnp.where(yy == 0, 3, (yy + 1) >> 1))
    return turn * 4 + xx * 2 + jnp.bitwise_and(row, 1)


def col_key(col, here):
    piece = col >> 1
    kk = jnp.bitwise_xor(jnp.bitwise_and(piece, 1), here[2])
    zz = jnp.bitwise_and((piece >> 1) - here[1], 3)
    far = jnp.where(zz == 2, 0, jnp.where(zz == 0, 3, (zz + 1) >> 1))
    turn = jnp.where(kk == 1, far, 4 + jnp.bitwise_and(far + 1, 3))
    xx = jnp.bitwise_xor(piece >> 3, here[0])
    return turn * 4 + xx * 2 + jnp.bitwise_and(col, 1)


def order_kernel(count_ref, here, rr_ref, cr_ref, values, fwd_ref, bwd_ref, held, sem):
    copy = pltpu.make_async_copy(values, held, sem)
    copy.start()
    count = count_ref[0, 0]
    live_c = lax.broadcasted_iota(jnp.int32, (KT, 1), 0) < count
    live_r = lax.broadcasted_iota(jnp.int32, (1, KT), 1) < count
    rr, cr = rr_ref[...], cr_ref[...]
    both = jnp.concatenate([rr, cr] * 4, axis=0).astype(jnp.float32).T.astype(jnp.int32)
    rc, cc = both[:, 0:1], both[:, 1:2]
    key = lambda of, idx, live: jnp.where(live, of(idx, here), 127)
    fwd = order_one(key(row_key, rc, live_c), key(row_key, rr, live_r), cc, FWD[0], CB)
    bwd = order_one(key(col_key, cc, live_c), key(col_key, cr, live_r), rc, BWD[0], RB)
    fwd_ref[...] = jnp.concatenate(fwd, axis=0).astype(jnp.int32)
    bwd_ref[...] = jnp.concatenate(bwd, axis=0).astype(jnp.int32)
    copy.wait()


def order(count, here, rows_idx, cols_idx, values):
    table = jax.ShapeDtypeStruct((4, SLOTS), jnp.int32)
    return pl.pallas_call(
        order_kernel,
        out_shape=(table, table, pltpu.VMEM((KT, TILE, TILE), jnp.bfloat16)),
        in_specs=[SM, SM, VM, VM, pl.BlockSpec(memory_space=pltpu.HBM)],
        out_specs=(VM, VM, VM),
        scratch_shapes=[pltpu.SemaphoreType.DMA],
        compiler_params=pltpu.CompilerParams(vmem_limit_bytes=8 << 20),
        name="order_tiles",
    )(
        count,
        here,
        rows_idx.reshape(1, KT),
        cols_idx.reshape(1, KT),
        pltpu.with_memory_space_constraint(values, pltpu.HBM),
    )


def products(flip, first, plan, panel, values, outs, extra, acc):
    chunk, group = BWD if flip else FWD
    keys = sum(out.shape[0] for out in outs) // TILE
    acc[...] = jnp.zeros_like(acc)
    low, high = plan[3, first], plan[3, first + keys]

    def step(q, _):
        found = []
        for u in range(group):
            base = (low + q * group + u) * chunk
            tiles = [values[plan[0, base + i]] for i in range(chunk)]
            right = jnp.concatenate([panel[plan[1, base + i]] for i in range(chunk)], axis=0)
            if flip:
                left, dims = jnp.concatenate(tiles, axis=0), (((0,), (0,)), ((), ()))
            else:
                left, dims = jnp.concatenate(tiles, axis=1), (((1,), (0,)), ((), ()))
            found.append(lax.dot_general(left, right, dims, preferred_element_type=jnp.float32))
        for u in range(group):
            at = low + q * group + u
            target = jnp.where(at < high, plan[2, at] - first, keys)
            acc[target] = acc[target] + found[u]
        return 0

    lax.fori_loop(0, lax.div(high - low + (group - 1), group), step, 0)
    n = 0
    for out in outs:
        for r in range(0, out.shape[0], TILE):
            block = acc[n]
            if extra is not None:
                ref, base = extra
                block = block.astype(jnp.bfloat16).astype(jnp.float32)
                block += ref[base + n * TILE : base + (n + 1) * TILE, :].astype(jnp.float32)
            out[r : r + TILE, :] = block.astype(out.dtype)
            n += 1


def forward_first(first, plan, here, own_ref, other_ref, values, out_ref, panel, acc):
    xl, z, k = (here[n] for n in range(3))
    panel[CB] = jnp.zeros((TILE, F), jnp.bfloat16)
    for kk, ref in ((0, own_ref), (1, other_ref)):
        for s, by in enumerate(SHIFTS):
            for xx in range(2):
                piece = (
                    (jnp.bitwise_xor(xl, xx) * 4 + jnp.bitwise_and(z - by, 3)) * 2
                    + jnp.bitwise_xor(k, kk)
                )
                base = (s * 2 + xx) * 2 * TILE
                for h in range(2):
                    panel[2 * piece + h] = ref[base + h * TILE : base + (h + 1) * TILE, :]
    products(False, first, plan, panel, values, (out_ref,), None, acc)


def backward_first(first, plan, here, ref, values, out_ref, panel, acc):
    y, xh = here[3], here[4]
    panel[RB] = jnp.zeros((TILE, F), jnp.bfloat16)
    for s, by in enumerate(SHIFTS):
        for xx in range(2):
            piece = jnp.bitwise_and(y - by, 3) * 2 + jnp.bitwise_xor(xh, xx)
            base = (s * 2 + xx) * 2 * TILE
            for h in range(2):
                panel[2 * piece + h] = ref[base + h * TILE : base + (h + 1) * TILE, :]
    products(True, first, plan, panel, values, (out_ref,), None, acc)


def later(flip, first, n_outs, base, plan, panel, values, *refs):
    extra = None if base is None else (refs[0], base)
    outs = refs[-1 - n_outs : -1]
    products(flip, first, plan, panel, values, outs, extra, refs[-1])


COST = pl.CostEstimate(flops=1000, bytes_accessed=1000, transcendentals=0)
PARAMS = pltpu.CompilerParams(vmem_limit_bytes=16 << 20)


def rows_of(*blocks, dtype=jnp.bfloat16):
    return tuple(jax.ShapeDtypeStruct((n * TILE, F), dtype) for n in blocks)


def call_first(kernel, name, first, keys, blocks, plan, here, pieces, values):
    return pl.pallas_call(
        functools.partial(kernel, first),
        out_shape=rows_of(keys) + (pltpu.VMEM((blocks + 1, TILE, F), jnp.bfloat16),),
        in_specs=[SM, SM] + [VM] * len(pieces) + [VM],
        out_specs=(VM, VM),
        scratch_shapes=[pltpu.VMEM((keys + 1, TILE, F), jnp.float32)],
        compiler_params=PARAMS,
        cost_estimate=COST,
        name=name,
    )(plan, here, *pieces, values)


def call_later(flip, name, first, outs, plan, panel, values, add=None, base=None, after=()):
    keys = sum(o.shape[0] for o in outs) // TILE
    adds = () if add is None else (add,)
    return pl.pallas_call(
        functools.partial(later, flip, first, len(outs), base),
        out_shape=outs,
        in_specs=[SM, VM, VM] + [VM] * len(adds) + [pl.BlockSpec(memory_space=pl.ANY)] * len(after),
        out_specs=(VM,) * len(outs),
        scratch_shapes=[pltpu.VMEM((keys + 1, TILE, F), jnp.float32)],
        compiler_params=PARAMS,
        cost_estimate=COST,
        name=name,
    )(plan, panel, values, *adds, *after)


def dense_kernel(near, far, weight, bias, cot, mixed_ref, back_ref, grads_ref):
    f32 = jnp.float32
    agg = (near[...] + far[...].astype(f32)).astype(jnp.bfloat16)
    w = weight[...]
    pre = jnp.dot(agg, w, preferred_element_type=f32) + bias[...]
    sig = jax.nn.sigmoid(pre)
    mixed_ref[...] = (pre * sig).astype(jnp.bfloat16)
    slope = (cot[...].astype(f32) * sig * (1.0 + pre * (1.0 - sig))).astype(jnp.bfloat16)
    back = lax.dot_general(slope, w, (((1,), (1,)), ((), ())), preferred_element_type=f32)
    back_ref[...] = back.astype(jnp.bfloat16)
    wsum = lax.dot_general(agg, slope, (((0,), (0,)), ((), ())), preferred_element_type=f32)
    bsum = jnp.sum(slope.astype(f32), axis=0, keepdims=True)
    grads_ref[0:F, :] = wsum.astype(jnp.bfloat16)
    grads_ref[F : F + 16, :] = jnp.broadcast_to(bsum, (16, F)).astype(jnp.bfloat16)


def dense(near, far, weight, bias, cot):
    return pl.pallas_call(
        dense_kernel,
        out_shape=(
            jax.ShapeDtypeStruct((F, F), jnp.bfloat16),
            jax.ShapeDtypeStruct((F, F), jnp.bfloat16),
            jax.ShapeDtypeStruct((F + 16, F), jnp.bfloat16),
        ),
        in_specs=[VM] * 5,
        out_specs=(VM, VM, VM),
        compiler_params=pltpu.CompilerParams(vmem_limit_bytes=8 << 20),
        name="dense_part",
    )(near, far, weight, bias.reshape(1, F), cot)


def gather(piece, pair_axis, ring_axis):
    both = jnp.concatenate([piece, swap(piece, pair_axis)], axis=0)
    parts = [both] + [shift(both, ring_axis, by) for by in SHIFTS[1:]]
    return jnp.concatenate(parts, axis=0)


def tie(value, *others):
    return lax.optimization_barrier((value,) + others)[0]


def add_up(value, axis, bit=1, after=()):
    got = tie(swap(value, axis, bit), *after)
    return (value.astype(jnp.float32) + got.astype(jnp.float32)).astype(jnp.bfloat16)


def on_device(features, weight, bias, tile_values, tile_row, tile_col, tile_count, cotangent):
    f32, bf16 = jnp.float32, jnp.bfloat16
    here = jnp.stack([lax.axis_index(a) for a in AXES] + [jnp.int32(0)] * 3).astype(jnp.int32)
    plan, turned, values = order(
        tile_count, here, tile_row[0, 0], tile_col[0, 0], tile_values[0, 0]
    )

    own = gather(features, "xl", "z")
    own = tie(own, plan, turned)
    other = swap(own, "k")
    part, panel = call_first(forward_first, "rows_y2", 0, 4, CB, plan, here, (own, other), values)
    got = shift(part, "y", 2)
    one, three = call_later(False, "rows_y1_y3", 4, rows_of(4, 4), plan, panel, values)
    one, three = shift(one, "y", 1), shift(three, "y", 3)
    (total,) = call_later(
        False, "rows_y0", 12, rows_of(4, dtype=f32), plan, panel, values, add=got, base=0
    )
    total = total + one.astype(f32) + three.astype(f32)
    far = swap(total[F:].astype(bf16), "xh")
    mixed, back, grads = dense(total[:F], far, weight, bias, cotangent)

    pieces = gather(back, "xh", "y")
    for axis, bit in (("k", 1), ("xl", 1), ("z", 1)):
        grads = add_up(grads, axis, bit)
    sent, panel = call_first(
        backward_first, "columns_far", 0, 12, RB, turned, here, (pieces,), values
    )
    grads = add_up(grads, "z", 2, (sent,))
    got = swap(sent, "k")
    sent, zero = call_later(True, "columns_z0", 12, rows_of(4, 4), turned, panel, values)
    grads = add_up(grads, "xh", 1, (zero,))
    total = zero.astype(f32) + swap(sent, "k").astype(f32)
    (two,) = call_later(True, "columns_z2", 20, rows_of(4), turned, panel, values, got, 0)
    two = shift(two, "z", 2)
    one, three = call_later(
        True, "columns_z1_z3", 24, rows_of(4, 4), turned, panel, values, got, 4 * TILE
    )
    grads = add_up(grads, "y", 1, (one,))
    one, three = shift(one, "z", 1), shift(three, "z", 3)
    total = total + two.astype(f32) + one.astype(f32) + three.astype(f32)
    far = swap(total[F:].astype(bf16), "xl")
    feature_grad = (total[:F] + far.astype(f32)).astype(bf16)

    grads = add_up(grads, "y", 2)
    scale = 1.0 / jnp.sqrt(f32(NODES))
    grads = grads.astype(f32) * scale
    return (mixed, grads[:F], grads[F], feature_grad)


def solution(mesh):
    fine = Mesh(mesh.devices.reshape(SIZES), AXES)
    row, col = ("xl", "z", "k"), ("y", "xh")
    in_specs = (
        P(col + row, None),
        P(),
        P(),
        P(row, col, None, None, None),
        P(row, col, None),
        P(row, col, None),
        P(row, col),
        P(row + col, None),
    )
    out_specs = (P(row + col, None), P(), P(), P(col + row, None))
    return jax.shard_map(
        on_device, mesh=fine, in_specs=in_specs, out_specs=out_specs, check_vma=False
    )
```

time: 141 us -> 115 us (0.82)
  the two profiles are of different devices: /device:TPU:16 before, /device:TPU:32 now
where the time goes in v2:
time: 115 us; the launch traced here: 113 us
  waiting for transfers between devices  47.2 us (41%)
  starting transfers between devices  41.4 us (36%)
  Pallas kernels  17.8 us (15%)
  local copies, waits for them, and re-layouts  3.93 us (3%)
  between operations  1.56 us (1%)
  other arithmetic  1.18 us (1%)
    ppermute x14, waiting for transfers between devices, swap(): return lax.ppermute(value, axis, [(i, i ^ bit) for i in range(n)])  26.5 us
    ppermute x14, starting transfers between devices, swap(): return lax.ppermute(value, axis, [(i, i ^ bit) for i in range(n)])  23.3 us
    ppermute x12, waiting for transfers between devices, shift(): return lax.ppermute(value, axis, [(i, (i + by) % n) for i in range(n)])  20.7 us
    ppermute x12, starting transfers between devices, shift(): return lax.ppermute(value, axis, [(i, (i + by) % n) for i in range(n)])  18.1 us
    pallas_call x5, Pallas kernels, call_later(): pl.pallas_call(functools.partial(later, flip, first, len(outs), base), ou...  8.25 us
    pallas_call x1, Pallas kernels, order(): pl.pallas_call(order_kernel, out_shape=(table, table, pltpu.VMEM((KT, TIL...  5.13 us
    pallas_call x2, Pallas kernels, call_first(): pl.pallas_call(functools.partial(kernel, first), out_shape=rows_of(keys)...  3.52 us
    unnamed x16, local copies, waits for them, and re-layouts  2.43 us
  transfers between devices with their start and end apart: 26, of which 16 were waited for; matrix products, arithmetic and copies ran while one was open for 2% of the time, Pallas kernels for 14%

profile of v2, /device:TPU:32, one launch (start us, length us, event | category | flops | bytes accessed | tf_op | source)
XLA Modules:
  0.0 113.1 jit_solution(1149061219639342523)
XLA Ops:
  0.6 1.6 %collective-permute-start = (bf16[256,256]{1,0:T(8,128)(2,1)}, bf16[256,256]{1,0:T(8,128)(2,1)S(1)}, u32[]{:S(2)}, u32[]{:S(2)}) collective-permute-start(bf16[256,256]{1,0:T(8,128)(2,1)} %param.8), channel_id=1, source_target_pairs={{0,64},{64,0},{1,65},{65,1},{2,66},{66,2},{3,67},{67,3},{4,68},{68... | collective-permute-start | bytes 393224 | tf_op jit(solution)/shard_map/ppermute | solution.py:36
  2.2 1.0 constant_dynamic-update-slice_fusion.1
  3.2 3.0 %collective-permute-done = bf16[256,256]{1,0:T(8,128)(2,1)S(1)} collective-permute-done((bf16[256,256]{1,0:T(8,128)(2,1)}, bf16[256,256]{1,0:T(8,128)(2,1)S(1)}, u32[]{:S(2)}, u32[]{:S(2)}) %collective-permute-start) | collective-permute-done | bytes 131104 | tf_op jit(solution)/shard_map/ppermute | solution.py:36
  6.2 2.0 %collective-permute-start.1 = (bf16[512,256]{1,0:T(8,128)(2,1)S(1)}, bf16[512,256]{1,0:T(8,128)(2,1)S(1)}, u32[]{:S(2)}, u32[]{:S(2)}) collective-permute-start(bf16[512,256]{1,0:T(8,128)(2,1)S(1)} %get-tuple-element.48), channel_id=1, source_target_pairs={{0,16},{16,32},{32,48},{48,0},{1,17},{17,33},{33,49},{49,1},{2,18}... | collective-permute-start | bytes 786440 | tf_op jit(solution)/shard_map/ppermute | solution.py:31
  8.3 3.0 %collective-permute-start.3 = (bf16[512,256]{1,0:T(8,128)(2,1)S(1)}, bf16[512,256]{1,0:T(8,128)(2,1)S(1)}, u32[]{:S(2)}, u32[]{:S(2)}) collective-permute-start(bf16[512,256]{1,0:T(8,128)(2,1)S(1)} %get-tuple-element.48), channel_id=1, source_target_pairs={{0,32},{16,48},{32,0},{48,16},{1,33},{17,49},{33,1},{49,17},{2,34}... | collective-permute-start | bytes 786440 | tf_op jit(solution)/shard_map/ppermute | solution.py:31
  12.0 0.7 copy-done.2
  12.7 0.7 copy-done.3
  13.4 5.1 %order_tiles.1 = (s32[4,512]{1,0:T(4,128)S(1)}, s32[4,512]{1,0:T(4,128)S(1)}, bf16[384,128,128]{2,1,0:T(8,128)(2,1)S(1)}) custom-call(s32[1,1]{1,0:T(1,128)S(6)} %copy.22.count_ref, s32[8]{0:T(128)S(1)} %stack.23.here, s32[1,384]{1,0:T(1,128)S(1)} %bitcast.10, s32[1,384]{1,0:T(1,128)S(1)} %bitcast.11, bf16[384,128,128]{2,1,0:T(8,128)(2,1)} %bitcast.13), custom_call_target="tpu_custom_call" | custom-call | tf_op jit(solution)/shard_map/order_tiles/pallas_call | solution.py:99
  18.6 3.2 %collective-permute-done.3 = bf16[512,256]{1,0:T(8,128)(2,1)S(1)} collective-permute-done((bf16[512,256]{1,0:T(8,128)(2,1)S(1)}, bf16[512,256]{1,0:T(8,128)(2,1)S(1)}, u32[]{:S(2)}, u32[]{:S(2)}) %collective-permute-start.3) | collective-permute-done | bytes 262176 | tf_op jit(solution)/shard_map/ppermute | solution.py:31
  21.9 2.6 %collective-permute-done.4.other_ref = bf16[2048,256]{1,0:T(8,128)(2,1)S(1)} collective-permute-done((bf16[2048,256]{1,0:T(8,128)(2,1)S(1)}, bf16[2048,256]{1,0:T(8,128)(2,1)S(1)}, u32[]{:S(2)}, u32[]{:S(2)}) %collective-permute-start.4) | collective-permute-done | bytes 1048608 | tf_op jit(solution)/shard_map/ppermute | solution.py:36
  24.5 1.5 %rows_y2.1 = (bf16[512,256]{1,0:T(8,128)(2,1)S(1)}, bf16[33,128,256]{2,1,0:T(8,128)(2,1)S(1)}) custom-call(s32[4,512]{1,0:T(4,128)S(1)} %get-tuple-element.24.plan, s32[8]{0:T(128)S(1)} %stack.23.here, bf16[2048,256]{1,0:T(8,128)(2,1)S(1)} %constant_dynamic-update-slice_fusion.2.own_ref, bf16[2048,256]{1,0:T(8,128)(2,1)S(1)} %collective-permute-done.4.other_ref, ...), custom_call_target="tpu_custom_call" | custom-call | flops 1000 | bytes 1000 | tf_op jit(solution)/shard_map/rows_y2/pallas_call | solution.py:195
  26.1 2.9 %collective-permute-start.5 = (bf16[512,256]{1,0:T(8,128)(2,1)S(1)}, bf16[512,256]{1,0:T(8,128)(2,1)S(1)}, u32[]{:S(2)}, u32[]{:S(2)}) collective-permute-start(bf16[512,256]{1,0:T(8,128)(2,1)S(1)} %get-tuple-element.29), channel_id=1, source_target_pairs={{0,4},{2,6},{4,0},{6,2},{1,5},{3,7},{5,1},{7,3},{8,12},{10,14},{12... | collective-permute-start | bytes 786440 | tf_op jit(solution)/shard_map/ppermute | solution.py:31
  29.0 2.1 %rows_y1_y3.1 = (bf16[512,256]{1,0:T(8,128)(2,1)S(1)}, bf16[512,256]{1,0:T(8,128)(2,1)S(1)}) custom-call(s32[4,512]{1,0:T(4,128)S(1)} %get-tuple-element.24.plan, bf16[33,128,256]{2,1,0:T(8,128)(2,1)S(1)} %get-tuple-element.28.panel, bf16[384,128,128]{2,1,0:T(8,128)(2,1)S(1)} %get-tuple-element.27.values), custom_call_target="tpu_custom_call" | custom-call | flops 1000 | bytes 1000 | tf_op jit(solution)/shard_map/rows_y1_y3/pallas_call | solution.py:210
  31.2 2.1 %collective-permute-start.6 = (bf16[512,256]{1,0:T(8,128)(2,1)S(1)}, bf16[512,256]{1,0:T(8,128)(2,1)S(1)}, u32[]{:S(2)}, u32[]{:S(2)}) collective-permute-start(bf16[512,256]{1,0:T(8,128)(2,1)S(1)} %get-tuple-element.30), channel_id=1, source_target_pairs={{0,2},{2,4},{4,6},{6,0},{1,3},{3,5},{5,7},{7,1},{8,10},{10,12},{12... | collective-permute-start | bytes 786440 | tf_op jit(solution)/shard_map/ppermute | solution.py:31
  33.2 1.2 %collective-permute-start.7 = (bf16[512,256]{1,0:T(8,128)(2,1)S(1)}, bf16[512,256]{1,0:T(8,128)(2,1)S(1)}, u32[]{:S(2)}, u32[]{:S(2)}) collective-permute-start(bf16[512,256]{1,0:T(8,128)(2,1)S(1)} %get-tuple-element.31), channel_id=1, source_target_pairs={{0,6},{2,0},{4,2},{6,4},{1,7},{3,1},{5,3},{7,5},{8,14},{10,8},{12,... | collective-permute-start | bytes 786440 | tf_op jit(solution)/shard_map/ppermute | solution.py:31
  34.5 2.4 %collective-permute-done.5.refs_0_ = bf16[512,256]{1,0:T(8,128)(2,1)S(1)} collective-permute-done((bf16[512,256]{1,0:T(8,128)(2,1)S(1)}, bf16[512,256]{1,0:T(8,128)(2,1)S(1)}, u32[]{:S(2)}, u32[]{:S(2)}) %collective-permute-start.5) | collective-permute-done | bytes 262176 | tf_op jit(solution)/shard_map/ppermute | solution.py:31
  36.8 1.8 %rows_y0.1 = f32[512,256]{1,0:T(8,128)S(1)} custom-call(s32[4,512]{1,0:T(4,128)S(1)} %get-tuple-element.24.plan, bf16[33,128,256]{2,1,0:T(8,128)(2,1)S(1)} %get-tuple-element.28.panel, bf16[384,128,128]{2,1,0:T(8,128)(2,1)S(1)} %get-tuple-element.27.values, bf16[512,256]{1,0:T(8,128)(2,1)S(1)} %collective-permute-done.5.refs_0_), custom_call_target="tpu_custom_call" | custom-call | flops 1000 | bytes 1000 | tf_op jit(solution)/shard_map/rows_y0/pallas_call | solution.py:210
  38.6 3.6 %collective-permute-done.6 = bf16[512,256]{1,0:T(8,128)(2,1)S(1)} collective-permute-done((bf16[512,256]{1,0:T(8,128)(2,1)S(1)}, bf16[512,256]{1,0:T(8,128)(2,1)S(1)}, u32[]{:S(2)}, u32[]{:S(2)}) %collective-permute-start.6) | collective-permute-done | bytes 262176 | tf_op jit(solution)/shard_map/ppermute | solution.py:31
  42.4 4.4 %collective-permute-start.8 = (bf16[256,256]{1,0:T(8,128)(2,1)S(1)}, bf16[256,256]{1,0:T(8,128)(2,1)S(1)}, u32[]{:S(2)}, u32[]{:S(2)}) collective-permute-start(bf16[256,256]{1,0:T(8,128)(2,1)S(1)} %slice.38), channel_id=1, source_target_pairs={{0,1},{1,0},{2,3},{3,2},{4,5},{5,4},{6,7},{7,6},{8,9},{9,8},{10,11... | collective-permute-start | bytes 393224 | tf_op jit(solution)/shard_map/ppermute | solution.py:36
  46.9 3.1 %collective-permute-done.8.far = bf16[256,256]{1,0:T(8,128)(2,1)S(1)} collective-permute-done((bf16[256,256]{1,0:T(8,128)(2,1)S(1)}, bf16[256,256]{1,0:T(8,128)(2,1)S(1)}, u32[]{:S(2)}, u32[]{:S(2)}) %collective-permute-start.8) | collective-permute-done | bytes 131104 | tf_op jit(solution)/shard_map/ppermute | solution.py:36
  50.0 0.9 dense_part.1
  50.9 3.4 %collective-permute-start.13 = (bf16[256,256]{1,0:T(8,128)(2,1)S(1)}, bf16[256,256]{1,0:T(8,128)(2,1)S(1)}, u32[]{:S(2)}, u32[]{:S(2)}) collective-permute-start(bf16[256,256]{1,0:T(8,128)(2,1)S(1)} %get-tuple-element.34), channel_id=1, source_target_pairs={{0,1},{1,0},{2,3},{3,2},{4,5},{5,4},{6,7},{7,6},{8,9},{9,8},{10,11... | collective-permute-start | bytes 393224 | tf_op jit(solution)/shard_map/ppermute | solution.py:36
  54.4 4.3 %collective-permute-done.13 = bf16[256,256]{1,0:T(8,128)(2,1)S(1)} collective-permute-done((bf16[256,256]{1,0:T(8,128)(2,1)S(1)}, bf16[256,256]{1,0:T(8,128)(2,1)S(1)}, u32[]{:S(2)}, u32[]{:S(2)}) %collective-permute-start.13) | collective-permute-done | bytes 131104 | tf_op jit(solution)/shard_map/ppermute | solution.py:36
  58.8 1.5 %collective-permute-start.14 = (bf16[512,256]{1,0:T(8,128)(2,1)S(1)}, bf16[512,256]{1,0:T(8,128)(2,1)S(1)}, u32[]{:S(2)}, u32[]{:S(2)}) collective-permute-start(bf16[512,256]{1,0:T(8,128)(2,1)S(1)} %get-tuple-element.44), channel_id=1, source_target_pairs={{0,2},{2,4},{4,6},{6,0},{1,3},{3,5},{5,7},{7,1},{8,10},{10,12},{12... | collective-permute-start | bytes 786440 | tf_op jit(solution)/shard_map/ppermute | solution.py:31
  60.2 2.7 %collective-permute-start.16 = (bf16[512,256]{1,0:T(8,128)(2,1)S(1)}, bf16[512,256]{1,0:T(8,128)(2,1)S(1)}, u32[]{:S(2)}, u32[]{:S(2)}) collective-permute-start(bf16[512,256]{1,0:T(8,128)(2,1)S(1)} %get-tuple-element.44), channel_id=1, source_target_pairs={{0,4},{2,6},{4,0},{6,2},{1,5},{3,7},{5,1},{7,3},{8,12},{10,14},{12... | collective-permute-start | bytes 786440 | tf_op jit(solution)/shard_map/ppermute | solution.py:31
  63.6 1.7 %collective-permute-start.11 = (bf16[272,256]{1,0:T(8,128)(2,1)S(1)}, bf16[272,256]{1,0:T(8,128)(2,1)S(1)}, u32[]{:S(2)}, u32[]{:S(2)}) collective-permute-start(bf16[272,256]{1,0:T(8,128)(2,1)S(1)} %add_convert_fusion.5), channel_id=1, source_target_pairs={{0,16},{16,0},{32,48},{48,32},{1,17},{17,1},{33,49},{49,33},{2,18}... | collective-permute-start | bytes 417800 | tf_op jit(solution)/shard_map/ppermute | solution.py:36
  65.3 3.3 %collective-permute-done.14 = bf16[512,256]{1,0:T(8,128)(2,1)S(1)} collective-permute-done((bf16[512,256]{1,0:T(8,128)(2,1)S(1)}, bf16[512,256]{1,0:T(8,128)(2,1)S(1)}, u32[]{:S(2)}, u32[]{:S(2)}) %collective-permute-start.14) | collective-permute-done | bytes 262176 | tf_op jit(solution)/shard_map/ppermute | solution.py:31
  68.7 5.3 %collective-permute-done.15 = bf16[512,256]{1,0:T(8,128)(2,1)S(1)} collective-permute-done((bf16[512,256]{1,0:T(8,128)(2,1)S(1)}, bf16[512,256]{1,0:T(8,128)(2,1)S(1)}, u32[]{:S(2)}, u32[]{:S(2)}) %collective-permute-start.15) | collective-permute-done | bytes 262176 | tf_op jit(solution)/shard_map/ppermute | solution.py:31
  74.1 1.3 %collective-permute-start.12 = (bf16[272,256]{1,0:T(8,128)(2,1)S(1)}, bf16[272,256]{1,0:T(8,128)(2,1)S(1)}, u32[]{:S(2)}, u32[]{:S(2)}) collective-permute-start(bf16[272,256]{1,0:T(8,128)(2,1)S(1)} %add_convert_fusion.4), channel_id=1, source_target_pairs={{0,32},{16,48},{32,0},{48,16},{1,33},{17,49},{33,1},{49,17},{2,34}... | collective-permute-start | bytes 417800 | tf_op jit(solution)/shard_map/ppermute | solution.py:36
  75.4 2.0 %columns_far.1 = (bf16[1536,256]{1,0:T(8,128)(2,1)S(1)}, bf16[17,128,256]{2,1,0:T(8,128)(2,1)S(1)}) custom-call(s32[4,512]{1,0:T(4,128)S(1)} %get-tuple-element.25.plan, s32[8]{0:T(128)S(1)} %stack.23.here, bf16[2048,256]{1,0:T(8,128)(2,1)S(1)} %constant_dynamic-update-slice_fusion.9.ref, bf16[384,128,128]{2,1,0:T(8,128)(2,1)S(1)} %get-tuple-element.27.values), custom_call_target="tpu_custom_call" | custom-call | flops 1000 | bytes 1000 | tf_op jit(solution)/shard_map/columns_far/pallas_call | solution.py:195
  77.4 3.3 %collective-permute-done.12 = bf16[272,256]{1,0:T(8,128)(2,1)S(1)} collective-permute-done((bf16[272,256]{1,0:T(8,128)(2,1)S(1)}, bf16[272,256]{1,0:T(8,128)(2,1)S(1)}, u32[]{:S(2)}, u32[]{:S(2)}) %collective-permute-start.12) | collective-permute-done | bytes 139296 | tf_op jit(solution)/shard_map/ppermute | solution.py:36
  80.7 3.3 %collective-permute-start.17 = (bf16[272,256]{1,0:T(8,128)(2,1)S(1)}, bf16[272,256]{1,0:T(8,128)(2,1)S(1)}, u32[]{:S(2)}, u32[]{:S(2)}) collective-permute-start(bf16[272,256]{1,0:T(8,128)(2,1)S(1)} %add_convert_fusion.3), channel_id=1, source_target_pairs={{0,1},{1,0},{2,3},{3,2},{4,5},{5,4},{6,7},{7,6},{8,9},{9,8},{10,11... | collective-permute-start | bytes 417800 | tf_op jit(solution)/shard_map/ppermute | solution.py:36
  84.0 1.5 %columns_z0.1 = (bf16[512,256]{1,0:T(8,128)(2,1)S(1)}, bf16[512,256]{1,0:T(8,128)(2,1)S(1)}) custom-call(s32[4,512]{1,0:T(4,128)S(1)} %get-tuple-element.25.plan, bf16[17,128,256]{2,1,0:T(8,128)(2,1)S(1)} %get-tuple-element.37.panel, bf16[384,128,128]{2,1,0:T(8,128)(2,1)S(1)} %get-tuple-element.27.values), custom_call_target="tpu_custom_call" | custom-call | flops 1000 | bytes 1000 | tf_op jit(solution)/shard_map/columns_z0/pallas_call | solution.py:210
  85.5 1.9 %collective-permute-done.17 = bf16[272,256]{1,0:T(8,128)(2,1)S(1)} collective-permute-done((bf16[272,256]{1,0:T(8,128)(2,1)S(1)}, bf16[272,256]{1,0:T(8,128)(2,1)S(1)}, u32[]{:S(2)}, u32[]{:S(2)}) %collective-permute-start.17) | collective-permute-done | bytes 139296 | tf_op jit(solution)/shard_map/ppermute | solution.py:36
  87.4 2.3 %collective-permute-start.18 = (bf16[272,256]{1,0:T(8,128)(2,1)S(1)}, bf16[272,256]{1,0:T(8,128)(2,1)S(1)}, u32[]{:S(2)}, u32[]{:S(2)}) collective-permute-start(bf16[272,256]{1,0:T(8,128)(2,1)S(1)} %add_convert_fusion.2), channel_id=1, source_target_pairs={{0,2},{2,0},{4,6},{6,4},{1,3},{3,1},{5,7},{7,5},{8,10},{10,8},{12,... | collective-permute-start | bytes 417800 | tf_op jit(solution)/shard_map/ppermute | solution.py:36
  89.7 1.8 %columns_z1_z3.1 = (bf16[512,256]{1,0:T(8,128)(2,1)S(1)}, bf16[512,256]{1,0:T(8,128)(2,1)S(1)}) custom-call(s32[4,512]{1,0:T(4,128)S(1)} %get-tuple-element.25.plan, bf16[17,128,256]{2,1,0:T(8,128)(2,1)S(1)} %get-tuple-element.37.panel, bf16[384,128,128]{2,1,0:T(8,128)(2,1)S(1)} %get-tuple-element.27.values, ...), custom_call_target="tpu_custom_call" | custom-call | flops 1000 | bytes 1000 | tf_op jit(solution)/shard_map/columns_z1_z3/pallas_call | solution.py:210
  91.5 1.2 %collective-permute-done.18 = bf16[272,256]{1,0:T(8,128)(2,1)S(1)} collective-permute-done((bf16[272,256]{1,0:T(8,128)(2,1)S(1)}, bf16[272,256]{1,0:T(8,128)(2,1)S(1)}, u32[]{:S(2)}, u32[]{:S(2)}) %collective-permute-start.18) | collective-permute-done | bytes 139296 | tf_op jit(solution)/shard_map/ppermute | solution.py:36
  92.7 0.8 collective-permute-start.24
  93.6 1.1 columns_z2.1
  94.7 1.1 collective-permute-start.22
  95.9 3.0 %collective-permute-start.20 = (bf16[272,256]{1,0:T(8,128)(2,1)S(1)}, bf16[272,256]{1,0:T(8,128)(2,1)S(1)}, u32[]{:S(2)}, u32[]{:S(2)}) collective-permute-start(bf16[272,256]{1,0:T(8,128)(2,1)S(1)} %add_convert_fusion.1), channel_id=1, source_target_pairs={{0,4},{2,6},{4,0},{6,2},{1,5},{3,7},{5,1},{7,3},{8,12},{10,14},{12... | collective-permute-start | bytes 417800 | tf_op jit(solution)/shard_map/ppermute | solution.py:36
  98.9 4.8 %collective-permute-done.20 = bf16[272,256]{1,0:T(8,128)(2,1)S(1)} collective-permute-done((bf16[272,256]{1,0:T(8,128)(2,1)S(1)}, bf16[272,256]{1,0:T(8,128)(2,1)S(1)}, u32[]{:S(2)}, u32[]{:S(2)}) %collective-permute-start.20) | collective-permute-done | bytes 139296 | tf_op jit(solution)/shard_map/ppermute | solution.py:36
  103.7 2.8 %collective-permute-done.24 = bf16[512,256]{1,0:T(8,128)(2,1)S(1)} collective-permute-done((bf16[512,256]{1,0:T(8,128)(2,1)S(1)}, bf16[512,256]{1,0:T(8,128)(2,1)S(1)}, u32[]{:S(2)}, u32[]{:S(2)}) %collective-permute-start.24) | collective-permute-done | bytes 262176 | tf_op jit(solution)/shard_map/ppermute | solution.py:31
  106.7 2.1 %collective-permute-start.25 = (bf16[256,256]{1,0:T(8,128)(2,1)S(1)}, bf16[256,256]{1,0:T(8,128)(2,1)S(1)}, u32[]{:S(2)}, u32[]{:S(2)}) collective-permute-start(bf16[256,256]{1,0:T(8,128)(2,1)S(1)} %slice.37), channel_id=1, source_target_pairs={{0,64},{64,0},{1,65},{65,1},{2,66},{66,2},{3,67},{67,3},{4,68},{68... | collective-permute-start | bytes 393224 | tf_op jit(solution)/shard_map/ppermute | solution.py:36
  108.8 0.6 slice.29
  109.4 0.7 slice.28
  110.1 2.3 %collective-permute-done.25 = bf16[256,256]{1,0:T(8,128)(2,1)S(1)} collective-permute-done((bf16[256,256]{1,0:T(8,128)(2,1)S(1)}, bf16[256,256]{1,0:T(8,128)(2,1)S(1)}, u32[]{:S(2)}, u32[]{:S(2)}) %collective-permute-start.25) | collective-permute-done | bytes 131104 | tf_op jit(solution)/shard_map/ppermute | solution.py:36
  112.4 0.7 fusion
  (50 shorter events, 2.0 us)
Async XLA Ops:
  0.6 5.5 %collective-permute-start = (bf16[256,256]{1,0:T(8,128)(2,1)}, bf16[256,256]{1,0:T(8,128)(2,1)S(1)}, u32[]{:S(2)}, u32[]{:S(2)}) collective-permute-start(bf16[256,256]{1,0:T(8,128)(2,1)} %param.8), channel_id=1, source_target_pairs={{0,64},{64,0},{1,65},{65,1},{2,66},{66,2},{3,67},{67,3},{4,68},{68... | collective-permute-start | bytes 393224 | tf_op jit(solution)/shard_map/ppermute | solution.py:36
  6.2 12.3 %collective-permute-start.1 = (bf16[512,256]{1,0:T(8,128)(2,1)S(1)}, bf16[512,256]{1,0:T(8,128)(2,1)S(1)}, u32[]{:S(2)}, u32[]{:S(2)}) collective-permute-start(bf16[512,256]{1,0:T(8,128)(2,1)S(1)} %get-tuple-element.48), channel_id=1, source_target_pairs={{0,16},{16,32},{32,48},{48,0},{1,17},{17,33},{33,49},{49,1},{2,18}... | collective-permute-start | bytes 786440 | tf_op jit(solution)/shard_map/ppermute | solution.py:31
  8.2 10.4 %collective-permute-start.2 = (bf16[512,256]{1,0:T(8,128)(2,1)S(1)}, bf16[512,256]{1,0:T(8,128)(2,1)S(1)}, u32[]{:S(2)}, u32[]{:S(2)}) collective-permute-start(bf16[512,256]{1,0:T(8,128)(2,1)S(1)} %get-tuple-element.48), channel_id=1, source_target_pairs={{0,48},{16,0},{32,16},{48,32},{1,49},{17,1},{33,17},{49,33},{2,50}... | collective-permute-start | bytes 786440 | tf_op jit(solution)/shard_map/ppermute | solution.py:31
  8.3 13.5 %collective-permute-start.3 = (bf16[512,256]{1,0:T(8,128)(2,1)S(1)}, bf16[512,256]{1,0:T(8,128)(2,1)S(1)}, u32[]{:S(2)}, u32[]{:S(2)}) collective-permute-start(bf16[512,256]{1,0:T(8,128)(2,1)S(1)} %get-tuple-element.48), channel_id=1, source_target_pairs={{0,32},{16,48},{32,0},{48,16},{1,33},{17,49},{33,1},{49,17},{2,34}... | collective-permute-start | bytes 786440 | tf_op jit(solution)/shard_map/ppermute | solution.py:31
  12.0 0.7 copy-start.2
  12.7 0.7 copy-start.3
  21.8 2.7 %collective-permute-start.4 = (bf16[2048,256]{1,0:T(8,128)(2,1)S(1)}, bf16[2048,256]{1,0:T(8,128)(2,1)S(1)}, u32[]{:S(2)}, u32[]{:S(2)}) collective-permute-start(bf16[2048,256]{1,0:T(8,128)(2,1)S(1)} %constant_dynamic-update-slice_fusion.2.own_ref), channel_id=1, source_target_pairs={{0,8},{8,0},{1,9},{9,1},{2,10},{10,2},{3,11},{11,3},{4,12},{12,4},... | collective-permute-start | bytes 3145736 | tf_op jit(solution)/shard_map/ppermute | solution.py:36
  26.1 10.8 %collective-permute-start.5 = (bf16[512,256]{1,0:T(8,128)(2,1)S(1)}, bf16[512,256]{1,0:T(8,128)(2,1)S(1)}, u32[]{:S(2)}, u32[]{:S(2)}) collective-permute-start(bf16[512,256]{1,0:T(8,128)(2,1)S(1)} %get-tuple-element.29), channel_id=1, source_target_pairs={{0,4},{2,6},{4,0},{6,2},{1,5},{3,7},{5,1},{7,3},{8,12},{10,14},{12... | collective-permute-start | bytes 786440 | tf_op jit(solution)/shard_map/ppermute | solution.py:31
  31.1 18.8 %copy-start = (bf16[256,256]{1,0:T(8,128)(2,1)S(1)}, bf16[256,256]{1,0:T(8,128)(2,1)}, u32[]{:S(2)}) copy-start(bf16[256,256]{1,0:T(8,128)(2,1)} %weight.1) | copy-start | bytes 393220
  31.1 18.8 %copy-start.1 = (bf16[256,256]{1,0:T(8,128)(2,1)S(1)}, bf16[256,256]{1,0:T(8,128)(2,1)}, u32[]{:S(2)}) copy-start(bf16[256,256]{1,0:T(8,128)(2,1)} %cot.1) | copy-start | bytes 393220
  31.1 18.8 %copy-start.4 = (f32[256]{0:T(256)S(1)}, f32[256]{0:T(256)}, u32[]{:S(2)}) copy-start(f32[256]{0:T(256)} %param.10) | copy-start | bytes 3076
  31.2 11.1 %collective-permute-start.6 = (bf16[512,256]{1,0:T(8,128)(2,1)S(1)}, bf16[512,256]{1,0:T(8,128)(2,1)S(1)}, u32[]{:S(2)}, u32[]{:S(2)}) collective-permute-start(bf16[512,256]{1,0:T(8,128)(2,1)S(1)} %get-tuple-element.30), channel_id=1, source_target_pairs={{0,2},{2,4},{4,6},{6,0},{1,3},{3,5},{5,7},{7,1},{8,10},{10,12},{12... | collective-permute-start | bytes 786440 | tf_op jit(solution)/shard_map/ppermute | solution.py:31
  33.2 9.1 %collective-permute-start.7 = (bf16[512,256]{1,0:T(8,128)(2,1)S(1)}, bf16[512,256]{1,0:T(8,128)(2,1)S(1)}, u32[]{:S(2)}, u32[]{:S(2)}) collective-permute-start(bf16[512,256]{1,0:T(8,128)(2,1)S(1)} %get-tuple-element.31), channel_id=1, source_target_pairs={{0,6},{2,0},{4,2},{6,4},{1,7},{3,1},{5,3},{7,5},{8,14},{10,8},{12,... | collective-permute-start | bytes 786440 | tf_op jit(solution)/shard_map/ppermute | solution.py:31
  42.4 7.5 %collective-permute-start.8 = (bf16[256,256]{1,0:T(8,128)(2,1)S(1)}, bf16[256,256]{1,0:T(8,128)(2,1)S(1)}, u32[]{:S(2)}, u32[]{:S(2)}) collective-permute-start(bf16[256,256]{1,0:T(8,128)(2,1)S(1)} %slice.38), channel_id=1, source_target_pairs={{0,1},{1,0},{2,3},{3,2},{4,5},{5,4},{6,7},{7,6},{8,9},{9,8},{10,11... | collective-permute-start | bytes 393224 | tf_op jit(solution)/shard_map/ppermute | solution.py:36
  50.9 3.4 %collective-permute-start.9 = (bf16[272,256]{1,0:T(8,128)(2,1)S(1)}, bf16[272,256]{1,0:T(8,128)(2,1)S(1)}, u32[]{:S(2)}, u32[]{:S(2)}) collective-permute-start(bf16[272,256]{1,0:T(8,128)(2,1)S(1)} %get-tuple-element.33), channel_id=1, source_target_pairs={{0,8},{8,0},{1,9},{9,1},{2,10},{10,2},{3,11},{11,3},{4,12},{12,4},... | collective-permute-start | bytes 417800 | tf_op jit(solution)/shard_map/ppermute | solution.py:36
  50.9 7.9 %collective-permute-start.13 = (bf16[256,256]{1,0:T(8,128)(2,1)S(1)}, bf16[256,256]{1,0:T(8,128)(2,1)S(1)}, u32[]{:S(2)}, u32[]{:S(2)}) collective-permute-start(bf16[256,256]{1,0:T(8,128)(2,1)S(1)} %get-tuple-element.34), channel_id=1, source_target_pairs={{0,1},{1,0},{2,3},{3,2},{4,5},{5,4},{6,7},{7,6},{8,9},{9,8},{10,11... | collective-permute-start | bytes 393224 | tf_op jit(solution)/shard_map/ppermute | solution.py:36
  54.3 9.2 %collective-permute-start.10 = (bf16[272,256]{1,0:T(8,128)(2,1)S(1)}, bf16[272,256]{1,0:T(8,128)(2,1)S(1)}, u32[]{:S(2)}, u32[]{:S(2)}) collective-permute-start(bf16[272,256]{1,0:T(8,128)(2,1)S(1)} %add_convert_fusion.6), channel_id=1, source_target_pairs={{0,64},{64,0},{1,65},{65,1},{2,66},{66,2},{3,67},{67,3},{4,68},{68... | collective-permute-start | bytes 417800 | tf_op jit(solution)/shard_map/ppermute | solution.py:36
  58.8 9.9 %collective-permute-start.14 = (bf16[512,256]{1,0:T(8,128)(2,1)S(1)}, bf16[512,256]{1,0:T(8,128)(2,1)S(1)}, u32[]{:S(2)}, u32[]{:S(2)}) collective-permute-start(bf16[512,256]{1,0:T(8,128)(2,1)S(1)} %get-tuple-element.44), channel_id=1, source_target_pairs={{0,2},{2,4},{4,6},{6,0},{1,3},{3,5},{5,7},{7,1},{8,10},{10,12},{12... | collective-permute-start | bytes 786440 | tf_op jit(solution)/shard_map/ppermute | solution.py:31
  60.2 15.1 %collective-permute-start.16 = (bf16[512,256]{1,0:T(8,128)(2,1)S(1)}, bf16[512,256]{1,0:T(8,128)(2,1)S(1)}, u32[]{:S(2)}, u32[]{:S(2)}) collective-permute-start(bf16[512,256]{1,0:T(8,128)(2,1)S(1)} %get-tuple-element.44), channel_id=1, source_target_pairs={{0,4},{2,6},{4,0},{6,2},{1,5},{3,7},{5,1},{7,3},{8,12},{10,14},{12... | collective-permute-start | bytes 786440 | tf_op jit(solution)/shard_map/ppermute | solution.py:31
  63.0 11.0 %collective-permute-start.15 = (bf16[512,256]{1,0:T(8,128)(2,1)S(1)}, bf16[512,256]{1,0:T(8,128)(2,1)S(1)}, u32[]{:S(2)}, u32[]{:S(2)}) collective-permute-start(bf16[512,256]{1,0:T(8,128)(2,1)S(1)} %get-tuple-element.44), channel_id=1, source_target_pairs={{0,6},{2,0},{4,2},{6,4},{1,7},{3,1},{5,3},{7,5},{8,14},{10,8},{12,... | collective-permute-start | bytes 786440 | tf_op jit(solution)/shard_map/ppermute | solution.py:31
  63.6 10.4 %collective-permute-start.11 = (bf16[272,256]{1,0:T(8,128)(2,1)S(1)}, bf16[272,256]{1,0:T(8,128)(2,1)S(1)}, u32[]{:S(2)}, u32[]{:S(2)}) collective-permute-start(bf16[272,256]{1,0:T(8,128)(2,1)S(1)} %add_convert_fusion.5), channel_id=1, source_target_pairs={{0,16},{16,0},{32,48},{48,32},{1,17},{17,1},{33,49},{49,33},{2,18}... | collective-permute-start | bytes 417800 | tf_op jit(solution)/shard_map/ppermute | solution.py:36
  74.1 6.6 %collective-permute-start.12 = (bf16[272,256]{1,0:T(8,128)(2,1)S(1)}, bf16[272,256]{1,0:T(8,128)(2,1)S(1)}, u32[]{:S(2)}, u32[]{:S(2)}) collective-permute-start(bf16[272,256]{1,0:T(8,128)(2,1)S(1)} %add_convert_fusion.4), channel_id=1, source_target_pairs={{0,32},{16,48},{32,0},{48,16},{1,33},{17,49},{33,1},{49,17},{2,34}... | collective-permute-start | bytes 417800 | tf_op jit(solution)/shard_map/ppermute | solution.py:36
  77.3 12.4 %collective-permute-start.19 = (bf16[1536,256]{1,0:T(8,128)(2,1)S(1)}, bf16[1536,256]{1,0:T(8,128)(2,1)S(1)}, u32[]{:S(2)}, u32[]{:S(2)}) collective-permute-start(bf16[1536,256]{1,0:T(8,128)(2,1)S(1)} %get-tuple-element.35), channel_id=1, source_target_pairs={{0,8},{8,0},{1,9},{9,1},{2,10},{10,2},{3,11},{11,3},{4,12},{12,4},... | collective-permute-start | bytes 2359304 | tf_op jit(solution)/shard_map/ppermute | solution.py:36
  80.7 6.6 %collective-permute-start.17 = (bf16[272,256]{1,0:T(8,128)(2,1)S(1)}, bf16[272,256]{1,0:T(8,128)(2,1)S(1)}, u32[]{:S(2)}, u32[]{:S(2)}) collective-permute-start(bf16[272,256]{1,0:T(8,128)(2,1)S(1)} %add_convert_fusion.3), channel_id=1, source_target_pairs={{0,1},{1,0},{2,3},{3,2},{4,5},{5,4},{6,7},{7,6},{8,9},{9,8},{10,11... | collective-permute-start | bytes 417800 | tf_op jit(solution)/shard_map/ppermute | solution.py:36
  87.4 5.3 %collective-permute-start.18 = (bf16[272,256]{1,0:T(8,128)(2,1)S(1)}, bf16[272,256]{1,0:T(8,128)(2,1)S(1)}, u32[]{:S(2)}, u32[]{:S(2)}) collective-permute-start(bf16[272,256]{1,0:T(8,128)(2,1)S(1)} %add_convert_fusion.2), channel_id=1, source_target_pairs={{0,2},{2,0},{4,6},{6,4},{1,3},{3,1},{5,7},{7,5},{8,10},{10,8},{12,... | collective-permute-start | bytes 417800 | tf_op jit(solution)/shard_map/ppermute | solution.py:36
  89.7 14.0 %collective-permute-start.21 = (bf16[512,256]{1,0:T(8,128)(2,1)S(1)}, bf16[512,256]{1,0:T(8,128)(2,1)S(1)}, u32[]{:S(2)}, u32[]{:S(2)}) collective-permute-start(bf16[512,256]{1,0:T(8,128)(2,1)S(1)} %get-tuple-element.42), channel_id=1, source_target_pairs={{0,8},{8,0},{1,9},{9,1},{2,10},{10,2},{3,11},{11,3},{4,12},{12,4},... | collective-permute-start | bytes 786440 | tf_op jit(solution)/shard_map/ppermute | solution.py:36
  91.5 15.0 %collective-permute-start.23 = (bf16[512,256]{1,0:T(8,128)(2,1)S(1)}, bf16[512,256]{1,0:T(8,128)(2,1)S(1)}, u32[]{:S(2)}, u32[]{:S(2)}) collective-permute-start(bf16[512,256]{1,0:T(8,128)(2,1)S(1)} %get-tuple-element.40), channel_id=1, source_target_pairs={{0,16},{16,32},{32,48},{48,0},{1,17},{17,33},{33,49},{49,1},{2,18}... | collective-permute-start | bytes 786440 | tf_op jit(solution)/shard_map/ppermute | solution.py:31
  92.7 13.8 %collective-permute-start.24 = (bf16[512,256]{1,0:T(8,128)(2,1)S(1)}, bf16[512,256]{1,0:T(8,128)(2,1)S(1)}, u32[]{:S(2)}, u32[]{:S(2)}) collective-permute-start(bf16[512,256]{1,0:T(8,128)(2,1)S(1)} %get-tuple-element.43), channel_id=1, source_target_pairs={{0,48},{16,0},{32,16},{48,32},{1,49},{17,1},{33,17},{49,33},{2,50}... | collective-permute-start | bytes 786440 | tf_op jit(solution)/shard_map/ppermute | solution.py:31
  94.7 11.8 %collective-permute-start.22 = (bf16[512,256]{1,0:T(8,128)(2,1)S(1)}, bf16[512,256]{1,0:T(8,128)(2,1)S(1)}, u32[]{:S(2)}, u32[]{:S(2)}) collective-permute-start(bf16[512,256]{1,0:T(8,128)(2,1)S(1)} %columns_z2.1), channel_id=1, source_target_pairs={{0,32},{16,48},{32,0},{48,16},{1,33},{17,49},{33,1},{49,17},{2,34}... | collective-permute-start | bytes 786440 | tf_op jit(solution)/shard_map/ppermute | solution.py:31
  95.9 7.8 %collective-permute-start.20 = (bf16[272,256]{1,0:T(8,128)(2,1)S(1)}, bf16[272,256]{1,0:T(8,128)(2,1)S(1)}, u32[]{:S(2)}, u32[]{:S(2)}) collective-permute-start(bf16[272,256]{1,0:T(8,128)(2,1)S(1)} %add_convert_fusion.1), channel_id=1, source_target_pairs={{0,4},{2,6},{4,0},{6,2},{1,5},{3,7},{5,1},{7,3},{8,12},{10,14},{12... | collective-permute-start | bytes 417800 | tf_op jit(solution)/shard_map/ppermute | solution.py:36
  106.7 5.7 %collective-permute-start.25 = (bf16[256,256]{1,0:T(8,128)(2,1)S(1)}, bf16[256,256]{1,0:T(8,128)(2,1)S(1)}, u32[]{:S(2)}, u32[]{:S(2)}) collective-permute-start(bf16[256,256]{1,0:T(8,128)(2,1)S(1)} %slice.37), channel_id=1, source_target_pairs={{0,64},{64,0},{1,65},{65,1},{2,66},{66,2},{3,67},{67,3},{4,68},{68... | collective-permute-start | bytes 393224 | tf_op jit(solution)/shard_map/ppermute | solution.py:36

commit v3 on v2

--- a/solution.py
+++ b/solution.py
@@ -14,13 +14,13 @@
 RB = 16
 CB = 32
 SLOTS = 512
-FWD = (4, 4)
-BWD = (2, 8)
+FWD = (4, 8)
+BWD = (2, 16)
 NODES = 32768
 
 AXES = ("xl", "z", "k", "y", "xh")
 SIZES = (2, 4, 2, 4, 2)
-SHIFTS = (0, 1, 3, 2)
+SHIFTS = (0, 2, 1, 3)
 
 VM = pl.BlockSpec(memory_space=pltpu.VMEM)
 SM = pl.BlockSpec(memory_space=pltpu.SMEM)
@@ -107,8 +107,8 @@
     )(
         count,
         here,
-        rows_idx.reshape(1, KT),
-        cols_idx.reshape(1, KT),
+        pltpu.with_memory_space_constraint(rows_idx.reshape(1, KT), pltpu.HBM),
+        pltpu.with_memory_space_constraint(cols_idx.reshape(1, KT), pltpu.HBM),
         pltpu.with_memory_space_constraint(values, pltpu.HBM),
     )
 
@@ -183,7 +183,11 @@
     products(flip, first, plan, panel, values, outs, extra, refs[-1])
 
 
-COST = pl.CostEstimate(flops=1000, bytes_accessed=1000, transcendentals=0)
+def cost(keys, targets):
+    flops = keys * 2 * KT * TILE * TILE * F // targets
+    return pl.CostEstimate(flops=4 * flops, bytes_accessed=1000, transcendentals=0)
+
+
 PARAMS = pltpu.CompilerParams(vmem_limit_bytes=16 << 20)
 
 
@@ -199,7 +203,7 @@
         out_specs=(VM, VM),
         scratch_shapes=[pltpu.VMEM((keys + 1, TILE, F), jnp.float32)],
         compiler_params=PARAMS,
-        cost_estimate=COST,
+        cost_estimate=cost(keys, 48 - blocks),
         name=name,
     )(plan, here, *pieces, values)
 
@@ -214,7 +218,7 @@
         out_specs=(VM,) * len(outs),
         scratch_shapes=[pltpu.VMEM((keys + 1, TILE, F), jnp.float32)],
         compiler_params=PARAMS,
-        cost_estimate=COST,
+        cost_estimate=cost(keys, CB if flip else RB),
         name=name,
     )(plan, panel, values, *adds, *after)
 
@@ -287,28 +291,27 @@
     mixed, back, grads = dense(total[:F], far, weight, bias, cotangent)
 
     pieces = gather(back, "xh", "y")
-    for axis, bit in (("k", 1), ("xl", 1), ("z", 1)):
+    for axis, bit in (("k", 1), ("z", 2), ("z", 1)):
         grads = add_up(grads, axis, bit)
     sent, panel = call_first(
         backward_first, "columns_far", 0, 12, RB, turned, here, (pieces,), values
     )
-    grads = add_up(grads, "z", 2, (sent,))
+    grads = add_up(grads, "xl", 1, (sent,))
     got = swap(sent, "k")
     sent, zero = call_later(True, "columns_z0", 12, rows_of(4, 4), turned, panel, values)
-    grads = add_up(grads, "xh", 1, (zero,))
     total = zero.astype(f32) + swap(sent, "k").astype(f32)
     (two,) = call_later(True, "columns_z2", 20, rows_of(4), turned, panel, values, got, 0)
     two = shift(two, "z", 2)
     one, three = call_later(
         True, "columns_z1_z3", 24, rows_of(4, 4), turned, panel, values, got, 4 * TILE
     )
-    grads = add_up(grads, "y", 1, (one,))
+    grads = add_up(grads, "xh", 1, (one,))
     one, three = shift(one, "z", 1), shift(three, "z", 3)
     total = total + two.astype(f32) + one.astype(f32) + three.astype(f32)
     far = swap(total[F:].astype(bf16), "xl")
     feature_grad = (total[:F] + far.astype(f32)).astype(bf16)
 
-    grads = add_up(grads, "y", 2)
+    grads = add_up(add_up(grads, "y", 1), "y", 2)
     scale = 1.0 / jnp.sqrt(f32(NODES))
     grads = grads.astype(f32) * scale
     return (mixed, grads[:F], grads[F], feature_grad)

time: 115 us -> 110 us (0.957); the launches traced: 113 us -> 110 us
  waiting for transfers between devices: 47.2 us -> 42.8 us
  starting transfers between devices: 41.4 us -> 45.6 us
  Pallas kernels: 17.8 us -> 16.4 us
  local copies, waits for them, and re-layouts: 3.93 us -> 2.56 us
    ppermute x14, waiting for transfers between devices: 26.5 us -> 17.3 us  [swap(): return lax.ppermute(value, axis, [(i, i ^ bit) for i in range(n)])]
    ppermute x12, waiting for transfers between devices: 20.7 us -> 25.5 us  [shift(): return lax.ppermute(value, axis, [(i, (i + by) % n) for i in range(n)])]
    ppermute x12, starting transfers between devices: 18.1 us -> 21.1 us  [shift(): return lax.ppermute(value, axis, [(i, (i + by) % n) for i in range(n)])]
    unnamed x16 -> x12, local copies, waits for them, and re-layouts: 2.43 us -> 1.06 us
    ppermute x14, starting transfers between devices: 23.3 us -> 24.5 us  [swap(): return lax.ppermute(value, axis, [(i, i ^ bit) for i in range(n)])]
  transfers between devices with their start and end apart: 26 -> 26, of which waited for: 16 -> 14; matrix products, arithmetic and copies ran while one was open for 2% -> 3% of each run, Pallas kernels for 14% -> 13%
where the time goes in v3:
time: 110 us
  starting transfers between devices  45.6 us (41%)
  waiting for transfers between devices  42.8 us (39%)
  Pallas kernels  16.4 us (15%)
  local copies, waits for them, and re-layouts  2.56 us (2%)
  between operations  1.55 us (1%)
  other arithmetic  1.18 us (1%)
    ppermute x12, waiting for transfers between devices, shift(): return lax.ppermute(value, axis, [(i, (i + by) % n) for i in range(n)])  25.5 us
    ppermute x14, starting transfers between devices, swap(): return lax.ppermute(value, axis, [(i, i ^ bit) for i in range(n)])  24.5 us
    ppermute x12, starting transfers between devices, shift(): return lax.ppermute(value, axis, [(i, (i + by) % n) for i in range(n)])  21.1 us
    ppermute x14, waiting for transfers between devices, swap(): return lax.ppermute(value, axis, [(i, i ^ bit) for i in range(n)])  17.3 us
    pallas_call x5, Pallas kernels, call_later(): pl.pallas_call(functools.partial(later, flip, first, len(outs), base), ou...  7.32 us
    pallas_call x1, Pallas kernels, order(): pl.pallas_call(order_kernel, out_shape=(table, table, pltpu.VMEM((KT, TIL...  5.29 us
    pallas_call x2, Pallas kernels, call_first(): pl.pallas_call(functools.partial(kernel, first), out_shape=rows_of(keys)...  2.9 us
  transfers between devices with their start and end apart: 26, of which 14 were waited for; matrix products, arithmetic and copies ran while one was open for 3% of the time, Pallas kernels for 13%

profile of v3, /device:TPU:32, one launch (start us, length us, event | category | flops | bytes accessed | tf_op | source)
XLA Modules:
  0.0 110.2 jit_solution(14373427079572071855)
XLA Ops:
  0.6 1.6 %collective-permute-start = (bf16[256,256]{1,0:T(8,128)(2,1)}, bf16[256,256]{1,0:T(8,128)(2,1)S(1)}, u32[]{:S(2)}, u32[]{:S(2)}) collective-permute-start(bf16[256,256]{1,0:T(8,128)(2,1)} %param.8), channel_id=1, source_target_pairs={{0,64},{64,0},{1,65},{65,1},{2,66},{66,2},{3,67},{67,3},{4,68},{68... | collective-permute-start | bytes 393224 | tf_op jit(solution)/shard_map/ppermute | solution.py:36
  2.2 1.0 constant_dynamic-update-slice_fusion.1
  3.2 3.0 %collective-permute-done = bf16[256,256]{1,0:T(8,128)(2,1)S(1)} collective-permute-done((bf16[256,256]{1,0:T(8,128)(2,1)}, bf16[256,256]{1,0:T(8,128)(2,1)S(1)}, u32[]{:S(2)}, u32[]{:S(2)}) %collective-permute-start) | collective-permute-done | bytes 131104 | tf_op jit(solution)/shard_map/ppermute | solution.py:36
  6.2 3.1 %collective-permute-start.1 = (bf16[512,256]{1,0:T(8,128)(2,1)S(1)}, bf16[512,256]{1,0:T(8,128)(2,1)S(1)}, u32[]{:S(2)}, u32[]{:S(2)}) collective-permute-start(bf16[512,256]{1,0:T(8,128)(2,1)S(1)} %get-tuple-element.46), channel_id=1, source_target_pairs={{0,32},{16,48},{32,0},{48,16},{1,33},{17,49},{33,1},{49,17},{2,34}... | collective-permute-start | bytes 786440 | tf_op jit(solution)/shard_map/ppermute | solution.py:31
  9.2 2.0 %collective-permute-start.3 = (bf16[512,256]{1,0:T(8,128)(2,1)S(1)}, bf16[512,256]{1,0:T(8,128)(2,1)S(1)}, u32[]{:S(2)}, u32[]{:S(2)}) collective-permute-start(bf16[512,256]{1,0:T(8,128)(2,1)S(1)} %get-tuple-element.46), channel_id=1, source_target_pairs={{0,48},{16,0},{32,16},{48,32},{1,49},{17,1},{33,17},{49,33},{2,50}... | collective-permute-start | bytes 786440 | tf_op jit(solution)/shard_map/ppermute | solution.py:31
  12.0 5.3 %order_tiles.1 = (s32[4,512]{1,0:T(4,128)S(1)}, s32[4,512]{1,0:T(4,128)S(1)}, bf16[384,128,128]{2,1,0:T(8,128)(2,1)S(1)}) custom-call(s32[1,1]{1,0:T(1,128)S(6)} %copy.22.count_ref, s32[8]{0:T(128)S(1)} %stack.23.here, s32[1,384]{1,0:T(1,128)} %bitcast.12, s32[1,384]{1,0:T(1,128)} %bitcast.13, bf16[384,128,128]{2,1,0:T(8,128)(2,1)} %bitcast.11), custom_call_target="tpu_custom_call" | custom-call | tf_op jit(solution)/shard_map/order_tiles/pallas_call | solution.py:99
  17.4 3.7 %collective-permute-done.2 = bf16[512,256]{1,0:T(8,128)(2,1)S(1)} collective-permute-done((bf16[512,256]{1,0:T(8,128)(2,1)S(1)}, bf16[512,256]{1,0:T(8,128)(2,1)S(1)}, u32[]{:S(2)}, u32[]{:S(2)}) %collective-permute-start.2) | collective-permute-done | bytes 262176 | tf_op jit(solution)/shard_map/ppermute | solution.py:31
  21.2 2.6 %collective-permute-done.4.other_ref = bf16[2048,256]{1,0:T(8,128)(2,1)S(1)} collective-permute-done((bf16[2048,256]{1,0:T(8,128)(2,1)S(1)}, bf16[2048,256]{1,0:T(8,128)(2,1)S(1)}, u32[]{:S(2)}, u32[]{:S(2)}) %collective-permute-start.4) | collective-permute-done | bytes 1048608 | tf_op jit(solution)/shard_map/ppermute | solution.py:36
  23.9 1.4 %rows_y2.1 = (bf16[512,256]{1,0:T(8,128)(2,1)S(1)}, bf16[33,128,256]{2,1,0:T(8,128)(2,1)S(1)}) custom-call(s32[4,512]{1,0:T(4,128)S(1)} %get-tuple-element.23.plan, s32[8]{0:T(128)S(1)} %stack.23.here, bf16[2048,256]{1,0:T(8,128)(2,1)S(1)} %constant_dynamic-update-slice_fusion.2.own_ref, bf16[2048,256]{1,0:T(8,128)(2,1)S(1)} %collective-permute-done.4.other_ref, ...), custom_call_target="tpu_custom_call" | custom-call | flops 3221225472 | bytes 1000 | tf_op jit(solution)/shard_map/rows_y2/pallas_call | solution.py:199
  25.2 3.3 %collective-permute-start.5 = (bf16[512,256]{1,0:T(8,128)(2,1)S(1)}, bf16[512,256]{1,0:T(8,128)(2,1)S(1)}, u32[]{:S(2)}, u32[]{:S(2)}) collective-permute-start(bf16[512,256]{1,0:T(8,128)(2,1)S(1)} %get-tuple-element.28), channel_id=1, source_target_pairs={{0,4},{2,6},{4,0},{6,2},{1,5},{3,7},{5,1},{7,3},{8,12},{10,14},{12... | collective-permute-start | bytes 786440 | tf_op jit(solution)/shard_map/ppermute | solution.py:31
  28.5 1.8 %rows_y1_y3.1 = (bf16[512,256]{1,0:T(8,128)(2,1)S(1)}, bf16[512,256]{1,0:T(8,128)(2,1)S(1)}) custom-call(s32[4,512]{1,0:T(4,128)S(1)} %get-tuple-element.23.plan, bf16[33,128,256]{2,1,0:T(8,128)(2,1)S(1)} %get-tuple-element.27.panel, bf16[384,128,128]{2,1,0:T(8,128)(2,1)S(1)} %get-tuple-element.26.values), custom_call_target="tpu_custom_call" | custom-call | flops 6442450944 | bytes 1000 | tf_op jit(solution)/shard_map/rows_y1_y3/pallas_call | solution.py:214
  30.3 1.7 %collective-permute-start.6 = (bf16[512,256]{1,0:T(8,128)(2,1)S(1)}, bf16[512,256]{1,0:T(8,128)(2,1)S(1)}, u32[]{:S(2)}, u32[]{:S(2)}) collective-permute-start(bf16[512,256]{1,0:T(8,128)(2,1)S(1)} %get-tuple-element.29), channel_id=1, source_target_pairs={{0,2},{2,4},{4,6},{6,0},{1,3},{3,5},{5,7},{7,1},{8,10},{10,12},{12... | collective-permute-start | bytes 786440 | tf_op jit(solution)/shard_map/ppermute | solution.py:31
  32.1 1.6 %collective-permute-start.7 = (bf16[512,256]{1,0:T(8,128)(2,1)S(1)}, bf16[512,256]{1,0:T(8,128)(2,1)S(1)}, u32[]{:S(2)}, u32[]{:S(2)}) collective-permute-start(bf16[512,256]{1,0:T(8,128)(2,1)S(1)} %get-tuple-element.30), channel_id=1, source_target_pairs={{0,6},{2,0},{4,2},{6,4},{1,7},{3,1},{5,3},{7,5},{8,14},{10,8},{12,... | collective-permute-start | bytes 786440 | tf_op jit(solution)/shard_map/ppermute | solution.py:31
  33.6 2.3 %collective-permute-done.5.refs_0_ = bf16[512,256]{1,0:T(8,128)(2,1)S(1)} collective-permute-done((bf16[512,256]{1,0:T(8,128)(2,1)S(1)}, bf16[512,256]{1,0:T(8,128)(2,1)S(1)}, u32[]{:S(2)}, u32[]{:S(2)}) %collective-permute-start.5) | collective-permute-done | bytes 262176 | tf_op jit(solution)/shard_map/ppermute | solution.py:31
  35.9 1.3 %rows_y0.1 = f32[512,256]{1,0:T(8,128)S(1)} custom-call(s32[4,512]{1,0:T(4,128)S(1)} %get-tuple-element.23.plan, bf16[33,128,256]{2,1,0:T(8,128)(2,1)S(1)} %get-tuple-element.27.panel, bf16[384,128,128]{2,1,0:T(8,128)(2,1)S(1)} %get-tuple-element.26.values, bf16[512,256]{1,0:T(8,128)(2,1)S(1)} %collective-permute-done.5.refs_0_), custom_call_target="tpu_custom_call" | custom-call | flops 3221225472 | bytes 1000 | tf_op jit(solution)/shard_map/rows_y0/pallas_call | solution.py:214
  37.2 4.4 %collective-permute-done.6 = bf16[512,256]{1,0:T(8,128)(2,1)S(1)} collective-permute-done((bf16[512,256]{1,0:T(8,128)(2,1)S(1)}, bf16[512,256]{1,0:T(8,128)(2,1)S(1)}, u32[]{:S(2)}, u32[]{:S(2)}) %collective-permute-start.6) | collective-permute-done | bytes 262176 | tf_op jit(solution)/shard_map/ppermute | solution.py:31
  41.7 3.3 %collective-permute-start.8 = (bf16[256,256]{1,0:T(8,128)(2,1)S(1)}, bf16[256,256]{1,0:T(8,128)(2,1)S(1)}, u32[]{:S(2)}, u32[]{:S(2)}) collective-permute-start(bf16[256,256]{1,0:T(8,128)(2,1)S(1)} %slice.38), channel_id=1, source_target_pairs={{0,1},{1,0},{2,3},{3,2},{4,5},{5,4},{6,7},{7,6},{8,9},{9,8},{10,11... | collective-permute-start | bytes 393224 | tf_op jit(solution)/shard_map/ppermute | solution.py:36
  45.0 3.8 %collective-permute-done.8.far = bf16[256,256]{1,0:T(8,128)(2,1)S(1)} collective-permute-done((bf16[256,256]{1,0:T(8,128)(2,1)S(1)}, bf16[256,256]{1,0:T(8,128)(2,1)S(1)}, u32[]{:S(2)}, u32[]{:S(2)}) %collective-permute-start.8) | collective-permute-done | bytes 131104 | tf_op jit(solution)/shard_map/ppermute | solution.py:36
  48.8 0.9 dense_part.1
  49.7 3.2 %collective-permute-start.13 = (bf16[256,256]{1,0:T(8,128)(2,1)S(1)}, bf16[256,256]{1,0:T(8,128)(2,1)S(1)}, u32[]{:S(2)}, u32[]{:S(2)}) collective-permute-start(bf16[256,256]{1,0:T(8,128)(2,1)S(1)} %get-tuple-element.33), channel_id=1, source_target_pairs={{0,1},{1,0},{2,3},{3,2},{4,5},{5,4},{6,7},{7,6},{8,9},{9,8},{10,11... | collective-permute-start | bytes 393224 | tf_op jit(solution)/shard_map/ppermute | solution.py:36
  53.1 2.0 %collective-permute-start.10 = (bf16[272,256]{1,0:T(8,128)(2,1)S(1)}, bf16[272,256]{1,0:T(8,128)(2,1)S(1)}, u32[]{:S(2)}, u32[]{:S(2)}) collective-permute-start(bf16[272,256]{1,0:T(8,128)(2,1)S(1)} %add_convert_fusion.6), channel_id=1, source_target_pairs={{0,32},{16,48},{32,0},{48,16},{1,33},{17,49},{33,1},{49,17},{2,34}... | collective-permute-start | bytes 417800 | tf_op jit(solution)/shard_map/ppermute | solution.py:36
  55.0 2.1 %collective-permute-done.13 = bf16[256,256]{1,0:T(8,128)(2,1)S(1)} collective-permute-done((bf16[256,256]{1,0:T(8,128)(2,1)S(1)}, bf16[256,256]{1,0:T(8,128)(2,1)S(1)}, u32[]{:S(2)}, u32[]{:S(2)}) %collective-permute-start.13) | collective-permute-done | bytes 131104 | tf_op jit(solution)/shard_map/ppermute | solution.py:36
  57.2 2.7 %collective-permute-start.14 = (bf16[512,256]{1,0:T(8,128)(2,1)S(1)}, bf16[512,256]{1,0:T(8,128)(2,1)S(1)}, u32[]{:S(2)}, u32[]{:S(2)}) collective-permute-start(bf16[512,256]{1,0:T(8,128)(2,1)S(1)} %get-tuple-element.42), channel_id=1, source_target_pairs={{0,4},{2,6},{4,0},{6,2},{1,5},{3,7},{5,1},{7,3},{8,12},{10,14},{12... | collective-permute-start | bytes 786440 | tf_op jit(solution)/shard_map/ppermute | solution.py:31
  59.9 1.3 %collective-permute-start.16 = (bf16[512,256]{1,0:T(8,128)(2,1)S(1)}, bf16[512,256]{1,0:T(8,128)(2,1)S(1)}, u32[]{:S(2)}, u32[]{:S(2)}) collective-permute-start(bf16[512,256]{1,0:T(8,128)(2,1)S(1)} %get-tuple-element.42), channel_id=1, source_target_pairs={{0,6},{2,0},{4,2},{6,4},{1,7},{3,1},{5,3},{7,5},{8,14},{10,8},{12,... | collective-permute-start | bytes 786440 | tf_op jit(solution)/shard_map/ppermute | solution.py:31
  61.1 0.8 collective-permute-start.15
  61.9 1.2 %collective-permute-start.11 = (bf16[272,256]{1,0:T(8,128)(2,1)S(1)}, bf16[272,256]{1,0:T(8,128)(2,1)S(1)}, u32[]{:S(2)}, u32[]{:S(2)}) collective-permute-start(bf16[272,256]{1,0:T(8,128)(2,1)S(1)} %add_convert_fusion.5), channel_id=1, source_target_pairs={{0,16},{16,0},{32,48},{48,32},{1,17},{17,1},{33,49},{49,33},{2,18}... | collective-permute-start | bytes 417800 | tf_op jit(solution)/shard_map/ppermute | solution.py:36
  63.2 4.8 %collective-permute-done.14 = bf16[512,256]{1,0:T(8,128)(2,1)S(1)} collective-permute-done((bf16[512,256]{1,0:T(8,128)(2,1)S(1)}, bf16[512,256]{1,0:T(8,128)(2,1)S(1)}, u32[]{:S(2)}, u32[]{:S(2)}) %collective-permute-start.14) | collective-permute-done | bytes 262176 | tf_op jit(solution)/shard_map/ppermute | solution.py:31
  68.0 4.3 %collective-permute-done.15 = bf16[512,256]{1,0:T(8,128)(2,1)S(1)} collective-permute-done((bf16[512,256]{1,0:T(8,128)(2,1)S(1)}, bf16[512,256]{1,0:T(8,128)(2,1)S(1)}, u32[]{:S(2)}, u32[]{:S(2)}) %collective-permute-start.15) | collective-permute-done | bytes 262176 | tf_op jit(solution)/shard_map/ppermute | solution.py:31
  72.4 1.5 %columns_far.1 = (bf16[1536,256]{1,0:T(8,128)(2,1)S(1)}, bf16[17,128,256]{2,1,0:T(8,128)(2,1)S(1)}) custom-call(s32[4,512]{1,0:T(4,128)S(1)} %get-tuple-element.24.plan, s32[8]{0:T(128)S(1)} %stack.23.here, bf16[2048,256]{1,0:T(8,128)(2,1)S(1)} %constant_dynamic-update-slice_fusion.9.ref, bf16[384,128,128]{2,1,0:T(8,128)(2,1)S(1)} %get-tuple-element.26.values), custom_call_target="tpu_custom_call" | custom-call | flops 4831838208 | bytes 1000 | tf_op jit(solution)/shard_map/columns_far/pallas_call | solution.py:199
  73.9 2.3 %collective-permute-start.18 = (bf16[1536,256]{1,0:T(8,128)(2,1)S(1)}, bf16[1536,256]{1,0:T(8,128)(2,1)S(1)}, u32[]{:S(2)}, u32[]{:S(2)}) collective-permute-start(bf16[1536,256]{1,0:T(8,128)(2,1)S(1)} %get-tuple-element.34), channel_id=1, source_target_pairs={{0,8},{8,0},{1,9},{9,1},{2,10},{10,2},{3,11},{11,3},{4,12},{12,4},... | collective-permute-start | bytes 2359304 | tf_op jit(solution)/shard_map/ppermute | solution.py:36
  76.3 0.7 collective-permute-start.12
  76.9 1.4 %columns_z0.1 = (bf16[512,256]{1,0:T(8,128)(2,1)S(1)}, bf16[512,256]{1,0:T(8,128)(2,1)S(1)}) custom-call(s32[4,512]{1,0:T(4,128)S(1)} %get-tuple-element.24.plan, bf16[17,128,256]{2,1,0:T(8,128)(2,1)S(1)} %get-tuple-element.36.panel, bf16[384,128,128]{2,1,0:T(8,128)(2,1)S(1)} %get-tuple-element.26.values), custom_call_target="tpu_custom_call" | custom-call | flops 3221225472 | bytes 1000 | tf_op jit(solution)/shard_map/columns_z0/pallas_call | solution.py:214
  78.3 1.5 %collective-permute-start.21 = (bf16[512,256]{1,0:T(8,128)(2,1)S(1)}, bf16[512,256]{1,0:T(8,128)(2,1)S(1)}, u32[]{:S(2)}, u32[]{:S(2)}) collective-permute-start(bf16[512,256]{1,0:T(8,128)(2,1)S(1)} %get-tuple-element.40), channel_id=1, source_target_pairs={{0,8},{8,0},{1,9},{9,1},{2,10},{10,2},{3,11},{11,3},{4,12},{12,4},... | collective-permute-start | bytes 786440 | tf_op jit(solution)/shard_map/ppermute | solution.py:36
  79.8 2.1 %collective-permute-done.12 = bf16[272,256]{1,0:T(8,128)(2,1)S(1)} collective-permute-done((bf16[272,256]{1,0:T(8,128)(2,1)S(1)}, bf16[272,256]{1,0:T(8,128)(2,1)S(1)}, u32[]{:S(2)}, u32[]{:S(2)}) %collective-permute-start.12) | collective-permute-done | bytes 139296 | tf_op jit(solution)/shard_map/ppermute | solution.py:36
  82.0 2.9 %collective-permute-start.17 = (bf16[272,256]{1,0:T(8,128)(2,1)S(1)}, bf16[272,256]{1,0:T(8,128)(2,1)S(1)}, u32[]{:S(2)}, u32[]{:S(2)}) collective-permute-start(bf16[272,256]{1,0:T(8,128)(2,1)S(1)} %add_convert_fusion.3), channel_id=1, source_target_pairs={{0,1},{1,0},{2,3},{3,2},{4,5},{5,4},{6,7},{7,6},{8,9},{9,8},{10,11... | collective-permute-start | bytes 417800 | tf_op jit(solution)/shard_map/ppermute | solution.py:36
  84.9 1.5 %columns_z1_z3.1 = (bf16[512,256]{1,0:T(8,128)(2,1)S(1)}, bf16[512,256]{1,0:T(8,128)(2,1)S(1)}) custom-call(s32[4,512]{1,0:T(4,128)S(1)} %get-tuple-element.24.plan, bf16[17,128,256]{2,1,0:T(8,128)(2,1)S(1)} %get-tuple-element.36.panel, bf16[384,128,128]{2,1,0:T(8,128)(2,1)S(1)} %get-tuple-element.26.values, ...), custom_call_target="tpu_custom_call" | custom-call | flops 3221225472 | bytes 1000 | tf_op jit(solution)/shard_map/columns_z1_z3/pallas_call | solution.py:214
  86.4 1.8 %collective-permute-start.23 = (bf16[512,256]{1,0:T(8,128)(2,1)S(1)}, bf16[512,256]{1,0:T(8,128)(2,1)S(1)}, u32[]{:S(2)}, u32[]{:S(2)}) collective-permute-start(bf16[512,256]{1,0:T(8,128)(2,1)S(1)} %get-tuple-element.37), channel_id=1, source_target_pairs={{0,16},{16,32},{32,48},{48,0},{1,17},{17,33},{33,49},{49,1},{2,18}... | collective-permute-start | bytes 786440 | tf_op jit(solution)/shard_map/ppermute | solution.py:31
  88.9 2.2 %collective-permute-start.19 = (bf16[272,256]{1,0:T(8,128)(2,1)S(1)}, bf16[272,256]{1,0:T(8,128)(2,1)S(1)}, u32[]{:S(2)}, u32[]{:S(2)}) collective-permute-start(bf16[272,256]{1,0:T(8,128)(2,1)S(1)} %add_convert_fusion.2), channel_id=1, source_target_pairs={{0,2},{2,0},{4,6},{6,4},{1,3},{3,1},{5,7},{7,5},{8,10},{10,8},{12,... | collective-permute-start | bytes 417800 | tf_op jit(solution)/shard_map/ppermute | solution.py:36
  91.1 0.9 collective-permute-start.24
  92.0 1.4 %columns_z2.1 = bf16[512,256]{1,0:T(8,128)(2,1)S(1)} custom-call(s32[4,512]{1,0:T(4,128)S(1)} %get-tuple-element.24.plan, bf16[17,128,256]{2,1,0:T(8,128)(2,1)S(1)} %get-tuple-element.36.panel, bf16[384,128,128]{2,1,0:T(8,128)(2,1)S(1)} %get-tuple-element.26.values, bf16[1536,256]{1,0:T(8,128)(2,1)S(1)} %collective-permute-done.18.refs_0_), custom_call_target="tpu_custom_call" | custom-call | flops 1610612736 | bytes 1000 | tf_op jit(solution)/shard_map/columns_z2/pallas_call | solution.py:214
  93.4 2.1 %collective-permute-start.22 = (bf16[512,256]{1,0:T(8,128)(2,1)S(1)}, bf16[512,256]{1,0:T(8,128)(2,1)S(1)}, u32[]{:S(2)}, u32[]{:S(2)}) collective-permute-start(bf16[512,256]{1,0:T(8,128)(2,1)S(1)} %columns_z2.1), channel_id=1, source_target_pairs={{0,32},{16,48},{32,0},{48,16},{1,33},{17,49},{33,1},{49,17},{2,34}... | collective-permute-start | bytes 786440 | tf_op jit(solution)/shard_map/ppermute | solution.py:31
  95.5 2.7 %collective-permute-start.20 = (bf16[272,256]{1,0:T(8,128)(2,1)S(1)}, bf16[272,256]{1,0:T(8,128)(2,1)S(1)}, u32[]{:S(2)}, u32[]{:S(2)}) collective-permute-start(bf16[272,256]{1,0:T(8,128)(2,1)S(1)} %add_convert_fusion.1), channel_id=1, source_target_pairs={{0,4},{2,6},{4,0},{6,2},{1,5},{3,7},{5,1},{7,3},{8,12},{10,14},{12... | collective-permute-start | bytes 417800 | tf_op jit(solution)/shard_map/ppermute | solution.py:36
  98.2 1.5 %collective-permute-done.24 = bf16[512,256]{1,0:T(8,128)(2,1)S(1)} collective-permute-done((bf16[512,256]{1,0:T(8,128)(2,1)S(1)}, bf16[512,256]{1,0:T(8,128)(2,1)S(1)}, u32[]{:S(2)}, u32[]{:S(2)}) %collective-permute-start.24) | collective-permute-done | bytes 262176 | tf_op jit(solution)/shard_map/ppermute | solution.py:31
  99.7 4.5 %collective-permute-done.22 = bf16[512,256]{1,0:T(8,128)(2,1)S(1)} collective-permute-done((bf16[512,256]{1,0:T(8,128)(2,1)S(1)}, bf16[512,256]{1,0:T(8,128)(2,1)S(1)}, u32[]{:S(2)}, u32[]{:S(2)}) %collective-permute-start.22) | collective-permute-done | bytes 262176 | tf_op jit(solution)/shard_map/ppermute | solution.py:31
  104.4 0.8 collective-permute-start.25
  105.8 0.7 slice.28
  106.6 2.9 %collective-permute-done.25 = bf16[256,256]{1,0:T(8,128)(2,1)S(1)} collective-permute-done((bf16[256,256]{1,0:T(8,128)(2,1)S(1)}, bf16[256,256]{1,0:T(8,128)(2,1)S(1)}, u32[]{:S(2)}, u32[]{:S(2)}) %collective-permute-start.25) | collective-permute-done | bytes 131104 | tf_op jit(solution)/shard_map/ppermute | solution.py:36
  109.5 0.7 fusion
  (46 shorter events, 2.1 us)
Async XLA Ops:
  0.6 5.5 %collective-permute-start = (bf16[256,256]{1,0:T(8,128)(2,1)}, bf16[256,256]{1,0:T(8,128)(2,1)S(1)}, u32[]{:S(2)}, u32[]{:S(2)}) collective-permute-start(bf16[256,256]{1,0:T(8,128)(2,1)} %param.8), channel_id=1, source_target_pairs={{0,64},{64,0},{1,65},{65,1},{2,66},{66,2},{3,67},{67,3},{4,68},{68... | collective-permute-start | bytes 393224 | tf_op jit(solution)/shard_map/ppermute | solution.py:36
  6.2 11.1 %collective-permute-start.1 = (bf16[512,256]{1,0:T(8,128)(2,1)S(1)}, bf16[512,256]{1,0:T(8,128)(2,1)S(1)}, u32[]{:S(2)}, u32[]{:S(2)}) collective-permute-start(bf16[512,256]{1,0:T(8,128)(2,1)S(1)} %get-tuple-element.46), channel_id=1, source_target_pairs={{0,32},{16,48},{32,0},{48,16},{1,33},{17,49},{33,1},{49,17},{2,34}... | collective-permute-start | bytes 786440 | tf_op jit(solution)/shard_map/ppermute | solution.py:31
  9.2 11.8 %collective-permute-start.2 = (bf16[512,256]{1,0:T(8,128)(2,1)S(1)}, bf16[512,256]{1,0:T(8,128)(2,1)S(1)}, u32[]{:S(2)}, u32[]{:S(2)}) collective-permute-start(bf16[512,256]{1,0:T(8,128)(2,1)S(1)} %get-tuple-element.46), channel_id=1, source_target_pairs={{0,16},{16,32},{32,48},{48,0},{1,17},{17,33},{33,49},{49,1},{2,18}... | collective-permute-start | bytes 786440 | tf_op jit(solution)/shard_map/ppermute | solution.py:31
  9.2 11.8 %collective-permute-start.3 = (bf16[512,256]{1,0:T(8,128)(2,1)S(1)}, bf16[512,256]{1,0:T(8,128)(2,1)S(1)}, u32[]{:S(2)}, u32[]{:S(2)}) collective-permute-start(bf16[512,256]{1,0:T(8,128)(2,1)S(1)} %get-tuple-element.46), channel_id=1, source_target_pairs={{0,48},{16,0},{32,16},{48,32},{1,49},{17,1},{33,17},{49,33},{2,50}... | collective-permute-start | bytes 786440 | tf_op jit(solution)/shard_map/ppermute | solution.py:31
  21.1 2.7 %collective-permute-start.4 = (bf16[2048,256]{1,0:T(8,128)(2,1)S(1)}, bf16[2048,256]{1,0:T(8,128)(2,1)S(1)}, u32[]{:S(2)}, u32[]{:S(2)}) collective-permute-start(bf16[2048,256]{1,0:T(8,128)(2,1)S(1)} %constant_dynamic-update-slice_fusion.2.own_ref), channel_id=1, source_target_pairs={{0,8},{8,0},{1,9},{9,1},{2,10},{10,2},{3,11},{11,3},{4,12},{12,4},... | collective-permute-start | bytes 3145736 | tf_op jit(solution)/shard_map/ppermute | solution.py:36
  25.2 10.7 %collective-permute-start.5 = (bf16[512,256]{1,0:T(8,128)(2,1)S(1)}, bf16[512,256]{1,0:T(8,128)(2,1)S(1)}, u32[]{:S(2)}, u32[]{:S(2)}) collective-permute-start(bf16[512,256]{1,0:T(8,128)(2,1)S(1)} %get-tuple-element.28), channel_id=1, source_target_pairs={{0,4},{2,6},{4,0},{6,2},{1,5},{3,7},{5,1},{7,3},{8,12},{10,14},{12... | collective-permute-start | bytes 786440 | tf_op jit(solution)/shard_map/ppermute | solution.py:31
  30.3 18.5 %copy-start = (bf16[256,256]{1,0:T(8,128)(2,1)S(1)}, bf16[256,256]{1,0:T(8,128)(2,1)}, u32[]{:S(2)}) copy-start(bf16[256,256]{1,0:T(8,128)(2,1)} %weight.1) | copy-start | bytes 393220
  30.3 18.5 %copy-start.1 = (bf16[256,256]{1,0:T(8,128)(2,1)S(1)}, bf16[256,256]{1,0:T(8,128)(2,1)}, u32[]{:S(2)}) copy-start(bf16[256,256]{1,0:T(8,128)(2,1)} %cot.1) | copy-start | bytes 393220
  30.3 18.5 %copy-start.2 = (f32[256]{0:T(256)S(1)}, f32[256]{0:T(256)}, u32[]{:S(2)}) copy-start(f32[256]{0:T(256)} %param.10) | copy-start | bytes 3076
  30.3 11.3 %collective-permute-start.6 = (bf16[512,256]{1,0:T(8,128)(2,1)S(1)}, bf16[512,256]{1,0:T(8,128)(2,1)S(1)}, u32[]{:S(2)}, u32[]{:S(2)}) collective-permute-start(bf16[512,256]{1,0:T(8,128)(2,1)S(1)} %get-tuple-element.29), channel_id=1, source_target_pairs={{0,2},{2,4},{4,6},{6,0},{1,3},{3,5},{5,7},{7,1},{8,10},{10,12},{12... | collective-permute-start | bytes 786440 | tf_op jit(solution)/shard_map/ppermute | solution.py:31
  32.1 9.5 %collective-permute-start.7 = (bf16[512,256]{1,0:T(8,128)(2,1)S(1)}, bf16[512,256]{1,0:T(8,128)(2,1)S(1)}, u32[]{:S(2)}, u32[]{:S(2)}) collective-permute-start(bf16[512,256]{1,0:T(8,128)(2,1)S(1)} %get-tuple-element.30), channel_id=1, source_target_pairs={{0,6},{2,0},{4,2},{6,4},{1,7},{3,1},{5,3},{7,5},{8,14},{10,8},{12,... | collective-permute-start | bytes 786440 | tf_op jit(solution)/shard_map/ppermute | solution.py:31
  41.7 7.1 %collective-permute-start.8 = (bf16[256,256]{1,0:T(8,128)(2,1)S(1)}, bf16[256,256]{1,0:T(8,128)(2,1)S(1)}, u32[]{:S(2)}, u32[]{:S(2)}) collective-permute-start(bf16[256,256]{1,0:T(8,128)(2,1)S(1)} %slice.38), channel_id=1, source_target_pairs={{0,1},{1,0},{2,3},{3,2},{4,5},{5,4},{6,7},{7,6},{8,9},{9,8},{10,11... | collective-permute-start | bytes 393224 | tf_op jit(solution)/shard_map/ppermute | solution.py:36
  49.7 3.3 %collective-permute-start.9 = (bf16[272,256]{1,0:T(8,128)(2,1)S(1)}, bf16[272,256]{1,0:T(8,128)(2,1)S(1)}, u32[]{:S(2)}, u32[]{:S(2)}) collective-permute-start(bf16[272,256]{1,0:T(8,128)(2,1)S(1)} %get-tuple-element.32), channel_id=1, source_target_pairs={{0,8},{8,0},{1,9},{9,1},{2,10},{10,2},{3,11},{11,3},{4,12},{12,4},... | collective-permute-start | bytes 417800 | tf_op jit(solution)/shard_map/ppermute | solution.py:36
  49.7 7.4 %collective-permute-start.13 = (bf16[256,256]{1,0:T(8,128)(2,1)S(1)}, bf16[256,256]{1,0:T(8,128)(2,1)S(1)}, u32[]{:S(2)}, u32[]{:S(2)}) collective-permute-start(bf16[256,256]{1,0:T(8,128)(2,1)S(1)} %get-tuple-element.33), channel_id=1, source_target_pairs={{0,1},{1,0},{2,3},{3,2},{4,5},{5,4},{6,7},{7,6},{8,9},{9,8},{10,11... | collective-permute-start | bytes 393224 | tf_op jit(solution)/shard_map/ppermute | solution.py:36
  53.1 8.8 %collective-permute-start.10 = (bf16[272,256]{1,0:T(8,128)(2,1)S(1)}, bf16[272,256]{1,0:T(8,128)(2,1)S(1)}, u32[]{:S(2)}, u32[]{:S(2)}) collective-permute-start(bf16[272,256]{1,0:T(8,128)(2,1)S(1)} %add_convert_fusion.6), channel_id=1, source_target_pairs={{0,32},{16,48},{32,0},{48,16},{1,33},{17,49},{33,1},{49,17},{2,34}... | collective-permute-start | bytes 417800 | tf_op jit(solution)/shard_map/ppermute | solution.py:36
  57.2 10.8 %collective-permute-start.14 = (bf16[512,256]{1,0:T(8,128)(2,1)S(1)}, bf16[512,256]{1,0:T(8,128)(2,1)S(1)}, u32[]{:S(2)}, u32[]{:S(2)}) collective-permute-start(bf16[512,256]{1,0:T(8,128)(2,1)S(1)} %get-tuple-element.42), channel_id=1, source_target_pairs={{0,4},{2,6},{4,0},{6,2},{1,5},{3,7},{5,1},{7,3},{8,12},{10,14},{12... | collective-permute-start | bytes 786440 | tf_op jit(solution)/shard_map/ppermute | solution.py:31
  59.9 12.5 %collective-permute-start.16 = (bf16[512,256]{1,0:T(8,128)(2,1)S(1)}, bf16[512,256]{1,0:T(8,128)(2,1)S(1)}, u32[]{:S(2)}, u32[]{:S(2)}) collective-permute-start(bf16[512,256]{1,0:T(8,128)(2,1)S(1)} %get-tuple-element.42), channel_id=1, source_target_pairs={{0,6},{2,0},{4,2},{6,4},{1,7},{3,1},{5,3},{7,5},{8,14},{10,8},{12,... | collective-permute-start | bytes 786440 | tf_op jit(solution)/shard_map/ppermute | solution.py:31
  61.1 11.2 %collective-permute-start.15 = (bf16[512,256]{1,0:T(8,128)(2,1)S(1)}, bf16[512,256]{1,0:T(8,128)(2,1)S(1)}, u32[]{:S(2)}, u32[]{:S(2)}) collective-permute-start(bf16[512,256]{1,0:T(8,128)(2,1)S(1)} %get-tuple-element.42), channel_id=1, source_target_pairs={{0,2},{2,4},{4,6},{6,0},{1,3},{3,5},{5,7},{7,1},{8,10},{10,12},{12... | collective-permute-start | bytes 786440 | tf_op jit(solution)/shard_map/ppermute | solution.py:31
  61.9 14.3 %collective-permute-start.11 = (bf16[272,256]{1,0:T(8,128)(2,1)S(1)}, bf16[272,256]{1,0:T(8,128)(2,1)S(1)}, u32[]{:S(2)}, u32[]{:S(2)}) collective-permute-start(bf16[272,256]{1,0:T(8,128)(2,1)S(1)} %add_convert_fusion.5), channel_id=1, source_target_pairs={{0,16},{16,0},{32,48},{48,32},{1,17},{17,1},{33,49},{49,33},{2,18}... | collective-permute-start | bytes 417800 | tf_op jit(solution)/shard_map/ppermute | solution.py:36
  73.9 11.0 %collective-permute-start.18 = (bf16[1536,256]{1,0:T(8,128)(2,1)S(1)}, bf16[1536,256]{1,0:T(8,128)(2,1)S(1)}, u32[]{:S(2)}, u32[]{:S(2)}) collective-permute-start(bf16[1536,256]{1,0:T(8,128)(2,1)S(1)} %get-tuple-element.34), channel_id=1, source_target_pairs={{0,8},{8,0},{1,9},{9,1},{2,10},{10,2},{3,11},{11,3},{4,12},{12,4},... | collective-permute-start | bytes 2359304 | tf_op jit(solution)/shard_map/ppermute | solution.py:36
  76.3 5.7 %collective-permute-start.12 = (bf16[272,256]{1,0:T(8,128)(2,1)S(1)}, bf16[272,256]{1,0:T(8,128)(2,1)S(1)}, u32[]{:S(2)}, u32[]{:S(2)}) collective-permute-start(bf16[272,256]{1,0:T(8,128)(2,1)S(1)} %add_convert_fusion.4), channel_id=1, source_target_pairs={{0,64},{64,0},{1,65},{65,1},{2,66},{66,2},{3,67},{67,3},{4,68},{68... | collective-permute-start | bytes 417800 | tf_op jit(solution)/shard_map/ppermute | solution.py:36
  78.3 19.9 %collective-permute-start.21 = (bf16[512,256]{1,0:T(8,128)(2,1)S(1)}, bf16[512,256]{1,0:T(8,128)(2,1)S(1)}, u32[]{:S(2)}, u32[]{:S(2)}) collective-permute-start(bf16[512,256]{1,0:T(8,128)(2,1)S(1)} %get-tuple-element.40), channel_id=1, source_target_pairs={{0,8},{8,0},{1,9},{9,1},{2,10},{10,2},{3,11},{11,3},{4,12},{12,4},... | collective-permute-start | bytes 786440 | tf_op jit(solution)/shard_map/ppermute | solution.py:36
  82.0 6.8 %collective-permute-start.17 = (bf16[272,256]{1,0:T(8,128)(2,1)S(1)}, bf16[272,256]{1,0:T(8,128)(2,1)S(1)}, u32[]{:S(2)}, u32[]{:S(2)}) collective-permute-start(bf16[272,256]{1,0:T(8,128)(2,1)S(1)} %add_convert_fusion.3), channel_id=1, source_target_pairs={{0,1},{1,0},{2,3},{3,2},{4,5},{5,4},{6,7},{7,6},{8,9},{9,8},{10,11... | collective-permute-start | bytes 417800 | tf_op jit(solution)/shard_map/ppermute | solution.py:36
  86.4 13.3 %collective-permute-start.23 = (bf16[512,256]{1,0:T(8,128)(2,1)S(1)}, bf16[512,256]{1,0:T(8,128)(2,1)S(1)}, u32[]{:S(2)}, u32[]{:S(2)}) collective-permute-start(bf16[512,256]{1,0:T(8,128)(2,1)S(1)} %get-tuple-element.37), channel_id=1, source_target_pairs={{0,16},{16,32},{32,48},{48,0},{1,17},{17,33},{33,49},{49,1},{2,18}... | collective-permute-start | bytes 786440 | tf_op jit(solution)/shard_map/ppermute | solution.py:31
  88.9 6.6 %collective-permute-start.19 = (bf16[272,256]{1,0:T(8,128)(2,1)S(1)}, bf16[272,256]{1,0:T(8,128)(2,1)S(1)}, u32[]{:S(2)}, u32[]{:S(2)}) collective-permute-start(bf16[272,256]{1,0:T(8,128)(2,1)S(1)} %add_convert_fusion.2), channel_id=1, source_target_pairs={{0,2},{2,0},{4,6},{6,4},{1,3},{3,1},{5,7},{7,5},{8,10},{10,8},{12,... | collective-permute-start | bytes 417800 | tf_op jit(solution)/shard_map/ppermute | solution.py:36
  91.1 8.7 %collective-permute-start.24 = (bf16[512,256]{1,0:T(8,128)(2,1)S(1)}, bf16[512,256]{1,0:T(8,128)(2,1)S(1)}, u32[]{:S(2)}, u32[]{:S(2)}) collective-permute-start(bf16[512,256]{1,0:T(8,128)(2,1)S(1)} %get-tuple-element.41), channel_id=1, source_target_pairs={{0,48},{16,0},{32,16},{48,32},{1,49},{17,1},{33,17},{49,33},{2,50}... | collective-permute-start | bytes 786440 | tf_op jit(solution)/shard_map/ppermute | solution.py:31
  93.4 10.9 %collective-permute-start.22 = (bf16[512,256]{1,0:T(8,128)(2,1)S(1)}, bf16[512,256]{1,0:T(8,128)(2,1)S(1)}, u32[]{:S(2)}, u32[]{:S(2)}) collective-permute-start(bf16[512,256]{1,0:T(8,128)(2,1)S(1)} %columns_z2.1), channel_id=1, source_target_pairs={{0,32},{16,48},{32,0},{48,16},{1,33},{17,49},{33,1},{49,17},{2,34}... | collective-permute-start | bytes 786440 | tf_op jit(solution)/shard_map/ppermute | solution.py:31
  95.5 9.8 %collective-permute-start.20 = (bf16[272,256]{1,0:T(8,128)(2,1)S(1)}, bf16[272,256]{1,0:T(8,128)(2,1)S(1)}, u32[]{:S(2)}, u32[]{:S(2)}) collective-permute-start(bf16[272,256]{1,0:T(8,128)(2,1)S(1)} %add_convert_fusion.1), channel_id=1, source_target_pairs={{0,4},{2,6},{4,0},{6,2},{1,5},{3,7},{5,1},{7,3},{8,12},{10,14},{12... | collective-permute-start | bytes 417800 | tf_op jit(solution)/shard_map/ppermute | solution.py:36
  104.4 5.0 %collective-permute-start.25 = (bf16[256,256]{1,0:T(8,128)(2,1)S(1)}, bf16[256,256]{1,0:T(8,128)(2,1)S(1)}, u32[]{:S(2)}, u32[]{:S(2)}) collective-permute-start(bf16[256,256]{1,0:T(8,128)(2,1)S(1)} %slice.37), channel_id=1, source_target_pairs={{0,64},{64,0},{1,65},{65,1},{2,66},{66,2},{3,67},{67,3},{4,68},{68... | collective-permute-start | bytes 393224 | tf_op jit(solution)/shard_map/ppermute | solution.py:36

commit v4 on v3

--- a/solution.py
+++ b/solution.py
@@ -223,39 +223,42 @@
     )(plan, panel, values, *adds, *after)
 
 
-def dense_kernel(near, far, weight, bias, cot, mixed_ref, back_ref, grads_ref):
-    f32 = jnp.float32
-    agg = (near[...] + far[...].astype(f32)).astype(jnp.bfloat16)
+def dense_kernel(mine, theirs, weight, bias, cot, far_cot, mixed_ref, back_ref, grads_ref):
+    f32, bf16 = jnp.float32, jnp.bfloat16
+    turned = jnp.concatenate([theirs[F : 2 * F, :], theirs[0:F, :]], axis=0)
+    agg = (mine[...].astype(f32) + turned.astype(f32)).astype(bf16)
     w = weight[...]
     pre = jnp.dot(agg, w, preferred_element_type=f32) + bias[...]
     sig = jax.nn.sigmoid(pre)
-    mixed_ref[...] = (pre * sig).astype(jnp.bfloat16)
-    slope = (cot[...].astype(f32) * sig * (1.0 + pre * (1.0 - sig))).astype(jnp.bfloat16)
+    mixed_ref[...] = (pre[:F] * sig[:F]).astype(bf16)
+    both_cot = jnp.concatenate([cot[...], far_cot[...]], axis=0).astype(f32)
+    slope = (both_cot * sig * (1.0 + pre * (1.0 - sig))).astype(bf16)
     back = lax.dot_general(slope, w, (((1,), (1,)), ((), ())), preferred_element_type=f32)
-    back_ref[...] = back.astype(jnp.bfloat16)
-    wsum = lax.dot_general(agg, slope, (((0,), (0,)), ((), ())), preferred_element_type=f32)
-    bsum = jnp.sum(slope.astype(f32), axis=0, keepdims=True)
-    grads_ref[0:F, :] = wsum.astype(jnp.bfloat16)
-    grads_ref[F : F + 16, :] = jnp.broadcast_to(bsum, (16, F)).astype(jnp.bfloat16)
-
-
-def dense(near, far, weight, bias, cot):
+    back_ref[...] = back.astype(bf16)
+    wsum = lax.dot_general(
+        agg[:F], slope[:F], (((0,), (0,)), ((), ())), preferred_element_type=f32
+    )
+    bsum = jnp.sum(slope[:F].astype(f32), axis=0, keepdims=True)
+    grads_ref[0:F, :] = wsum.astype(bf16)
+    grads_ref[F : F + 16, :] = jnp.broadcast_to(bsum, (16, F)).astype(bf16)
+
+
+def dense(mine, theirs, weight, bias, cot, far_cot):
     return pl.pallas_call(
         dense_kernel,
         out_shape=(
             jax.ShapeDtypeStruct((F, F), jnp.bfloat16),
-            jax.ShapeDtypeStruct((F, F), jnp.bfloat16),
+            jax.ShapeDtypeStruct((2 * F, F), jnp.bfloat16),
             jax.ShapeDtypeStruct((F + 16, F), jnp.bfloat16),
         ),
-        in_specs=[VM] * 5,
+        in_specs=[VM] * 6,
         out_specs=(VM, VM, VM),
         compiler_params=pltpu.CompilerParams(vmem_limit_bytes=8 << 20),
         name="dense_part",
-    )(near, far, weight, bias.reshape(1, F), cot)
-
-
-def gather(piece, pair_axis, ring_axis):
-    both = jnp.concatenate([piece, swap(piece, pair_axis)], axis=0)
+    )(mine, theirs, weight, bias.reshape(1, F), cot, far_cot)
+
+
+def gather(both, ring_axis):
     parts = [both] + [shift(both, ring_axis, by) for by in SHIFTS[1:]]
     return jnp.concatenate(parts, axis=0)
 
@@ -276,8 +279,9 @@
         tile_count, here, tile_row[0, 0], tile_col[0, 0], tile_values[0, 0]
     )
 
-    own = gather(features, "xl", "z")
-    own = tie(own, plan, turned)
+    own = gather(jnp.concatenate([features, swap(features, "xl")], axis=0), "z")
+    far_cot = swap(cotangent, "xh")
+    own = tie(own, plan, turned, far_cot)
     other = swap(own, "k")
     part, panel = call_first(forward_first, "rows_y2", 0, 4, CB, plan, here, (own, other), values)
     got = shift(part, "y", 2)
@@ -287,16 +291,16 @@
         False, "rows_y0", 12, rows_of(4, dtype=f32), plan, panel, values, add=got, base=0
     )
     total = total + one.astype(f32) + three.astype(f32)
-    far = swap(total[F:].astype(bf16), "xh")
-    mixed, back, grads = dense(total[:F], far, weight, bias, cotangent)
-
-    pieces = gather(back, "xh", "y")
-    for axis, bit in (("k", 1), ("z", 2), ("z", 1)):
+    total = total.astype(bf16)
+    mixed, back, grads = dense(total, swap(total, "xh"), weight, bias, cotangent, far_cot)
+
+    pieces = gather(back, "y")
+    for axis, bit in (("k", 1), ("z", 2),):
         grads = add_up(grads, axis, bit)
     sent, panel = call_first(
         backward_first, "columns_far", 0, 12, RB, turned, here, (pieces,), values
     )
-    grads = add_up(grads, "xl", 1, (sent,))
+    grads = add_up(grads, "z", 1, (sent,))
     got = swap(sent, "k")
     sent, zero = call_later(True, "columns_z0", 12, rows_of(4, 4), turned, panel, values)
     total = zero.astype(f32) + swap(sent, "k").astype(f32)
@@ -305,16 +309,18 @@
     one, three = call_later(
         True, "columns_z1_z3", 24, rows_of(4, 4), turned, panel, values, got, 4 * TILE
     )
-    grads = add_up(grads, "xh", 1, (one,))
+    grads = add_up(grads, "xl", 1, (one,))
     one, three = shift(one, "z", 1), shift(three, "z", 3)
     total = total + two.astype(f32) + one.astype(f32) + three.astype(f32)
     far = swap(total[F:].astype(bf16), "xl")
     feature_grad = (total[:F] + far.astype(f32)).astype(bf16)
 
-    grads = add_up(add_up(grads, "y", 1), "y", 2)
+    grads = add_up(add_up(grads, "xh"), "y", 2)
+    got = swap(grads, "y", 1)
     scale = 1.0 / jnp.sqrt(f32(NODES))
-    grads = grads.astype(f32) * scale
-    return (mixed, grads[:F], grads[F], feature_grad)
+    weight_grad = (grads[:F].astype(f32) + got[:F].astype(f32)) * scale
+    bias_grad = (grads[F].astype(f32) + got[F].astype(f32)) * scale
+    return (mixed, weight_grad, bias_grad, feature_grad)
 
 
 def solution(mesh):

time: 110 us -> 109 us (level)
  starting transfers between devices: 45.6 us -> 41.3 us
  waiting for transfers between devices: 42.8 us -> 46.8 us
  local copies, waits for them, and re-layouts: 2.56 us -> 1.16 us
  other arithmetic: 1.18 us -> 2.54 us
    ppermute x14, starting transfers between devices: 24.5 us -> 17.1 us  [swap(): return lax.ppermute(value, axis, [(i, i ^ bit) for i in range(n)])]
    ppermute x12, starting transfers between devices: 21.1 us -> 24.2 us  [shift(): return lax.ppermute(value, axis, [(i, (i + by) % n) for i in range(n)])]
    ppermute x14, waiting for transfers between devices: 17.3 us -> 20.2 us  [swap(): return lax.ppermute(value, axis, [(i, i ^ bit) for i in range(n)])]
    slice x4 -> x0, local copies, waits for them, and re-layouts: 1.32 us -> none  [the longest x2 1.28 us: on_device(): return (mixed, grads[:F], grads[F], feature_grad)]
    mul x1 -> x2, other arithmetic: 0.04 us -> 1.31 us  [the longest x1 0.74 us: on_device(): weight_grad = (grads[:F].astype(f32) + got[:F].astype(f32)) * scale]
  transfers between devices with their start and end apart: 26 -> 26, of which waited for: 14 -> 14; matrix products, arithmetic and copies ran while one was open for 3% -> 2% of each run, Pallas kernels for 13% -> 13%
where the time goes in v4:
time: 109 us; the launch traced here: 110 us
  waiting for transfers between devices  46.8 us (43%)
  starting transfers between devices  41.3 us (38%)
  Pallas kernels  16.7 us (15%)
  other arithmetic  2.54 us (2%)
  between operations  1.55 us (1%)
  local copies, waits for them, and re-layouts  1.16 us (1%)
    ppermute x12, waiting for transfers between devices, shift(): return lax.ppermute(value, axis, [(i, (i + by) % n) for i in range(n)])  26.6 us
    ppermute x12, starting transfers between devices, shift(): return lax.ppermute(value, axis, [(i, (i + by) % n) for i in range(n)])  24.2 us
    ppermute x14, waiting for transfers between devices, swap(): return lax.ppermute(value, axis, [(i, i ^ bit) for i in range(n)])  20.2 us
    ppermute x14, starting transfers between devices, swap(): return lax.ppermute(value, axis, [(i, i ^ bit) for i in range(n)])  17.1 us
    pallas_call x5, Pallas kernels, call_later(): pl.pallas_call(functools.partial(later, flip, first, len(outs), base), ou...  7.5 us
    pallas_call x1, Pallas kernels, order(): pl.pallas_call(order_kernel, out_shape=(table, table, pltpu.VMEM((KT, TIL...  5.29 us
    pallas_call x2, Pallas kernels, call_first(): pl.pallas_call(functools.partial(kernel, first), out_shape=rows_of(keys)...  2.9 us
  transfers between devices with their start and end apart: 26, of which 14 were waited for; matrix products, arithmetic and copies ran while one was open for 2% of the time, Pallas kernels for 13%

profile of v4, /device:TPU:32, one launch (start us, length us, event | category | flops | bytes accessed | tf_op | source)
XLA Modules:
  0.0 110.1 jit_solution(11109023558596803366)
XLA Ops:
  0.6 1.6 %collective-permute-start = (bf16[256,256]{1,0:T(8,128)(2,1)}, bf16[256,256]{1,0:T(8,128)(2,1)S(1)}, u32[]{:S(2)}, u32[]{:S(2)}) collective-permute-start(bf16[256,256]{1,0:T(8,128)(2,1)} %param.8), channel_id=1, source_target_pairs={{0,64},{64,0},{1,65},{65,1},{2,66},{66,2},{3,67},{67,3},{4,68},{68... | collective-permute-start | bytes 393224 | tf_op jit(solution)/shard_map/ppermute | solution.py:36
  2.2 1.0 constant_dynamic-update-slice_fusion.1
  3.2 3.0 %collective-permute-done = bf16[256,256]{1,0:T(8,128)(2,1)S(1)} collective-permute-done((bf16[256,256]{1,0:T(8,128)(2,1)}, bf16[256,256]{1,0:T(8,128)(2,1)S(1)}, u32[]{:S(2)}, u32[]{:S(2)}) %collective-permute-start) | collective-permute-done | bytes 131104 | tf_op jit(solution)/shard_map/ppermute | solution.py:36
  6.2 3.1 %collective-permute-start.1 = (bf16[512,256]{1,0:T(8,128)(2,1)S(1)}, bf16[512,256]{1,0:T(8,128)(2,1)S(1)}, u32[]{:S(2)}, u32[]{:S(2)}) collective-permute-start(bf16[512,256]{1,0:T(8,128)(2,1)S(1)} %get-tuple-element.42), channel_id=1, source_target_pairs={{0,32},{16,48},{32,0},{48,16},{1,33},{17,49},{33,1},{49,17},{2,34}... | collective-permute-start | bytes 786440 | tf_op jit(solution)/shard_map/ppermute | solution.py:31
  9.2 2.0 %collective-permute-start.3 = (bf16[512,256]{1,0:T(8,128)(2,1)S(1)}, bf16[512,256]{1,0:T(8,128)(2,1)S(1)}, u32[]{:S(2)}, u32[]{:S(2)}) collective-permute-start(bf16[512,256]{1,0:T(8,128)(2,1)S(1)} %get-tuple-element.42), channel_id=1, source_target_pairs={{0,48},{16,0},{32,16},{48,32},{1,49},{17,1},{33,17},{49,33},{2,50}... | collective-permute-start | bytes 786440 | tf_op jit(solution)/shard_map/ppermute | solution.py:31
  11.3 3.0 %collective-permute-start.4 = (bf16[256,256]{1,0:T(8,128)(2,1)}, bf16[256,256]{1,0:T(8,128)(2,1)S(1)}, u32[]{:S(2)}, u32[]{:S(2)}) collective-permute-start(bf16[256,256]{1,0:T(8,128)(2,1)} %cot.1), channel_id=1, source_target_pairs={{0,1},{1,0},{2,3},{3,2},{4,5},{5,4},{6,7},{7,6},{8,9},{9,8},{10,11... | collective-permute-start | bytes 393224 | tf_op jit(solution)/shard_map/ppermute | solution.py:36
  14.9 0.1 stack.23.here
  15.0 5.3 %order_tiles.1 = (s32[4,512]{1,0:T(4,128)S(1)}, s32[4,512]{1,0:T(4,128)S(1)}, bf16[384,128,128]{2,1,0:T(8,128)(2,1)S(1)}) custom-call(s32[1,1]{1,0:T(1,128)S(6)} %copy.17.count_ref, s32[8]{0:T(128)S(1)} %stack.23.here, s32[1,384]{1,0:T(1,128)} %bitcast.12, s32[1,384]{1,0:T(1,128)} %bitcast.13, bf16[384,128,128]{2,1,0:T(8,128)(2,1)} %bitcast.11), custom_call_target="tpu_custom_call" | custom-call | tf_op jit(solution)/shard_map/order_tiles/pallas_call | solution.py:99
  20.4 0.7 collective-permute-done.2
  21.2 2.6 %collective-permute-done.5.other_ref = bf16[2048,256]{1,0:T(8,128)(2,1)S(1)} collective-permute-done((bf16[2048,256]{1,0:T(8,128)(2,1)S(1)}, bf16[2048,256]{1,0:T(8,128)(2,1)S(1)}, u32[]{:S(2)}, u32[]{:S(2)}) %collective-permute-start.5) | collective-permute-done | bytes 1048608 | tf_op jit(solution)/shard_map/ppermute | solution.py:36
  23.9 1.4 %rows_y2.1 = (bf16[512,256]{1,0:T(8,128)(2,1)S(1)}, bf16[33,128,256]{2,1,0:T(8,128)(2,1)S(1)}) custom-call(s32[4,512]{1,0:T(4,128)S(1)} %get-tuple-element.23.plan, s32[8]{0:T(128)S(1)} %stack.23.here, bf16[2048,256]{1,0:T(8,128)(2,1)S(1)} %constant_dynamic-update-slice_fusion.2.own_ref, bf16[2048,256]{1,0:T(8,128)(2,1)S(1)} %collective-permute-done.5.other_ref, ...), custom_call_target="tpu_custom_call" | custom-call | flops 3221225472 | bytes 1000 | tf_op jit(solution)/shard_map/rows_y2/pallas_call | solution.py:199
  25.2 4.2 %collective-permute-start.6 = (bf16[512,256]{1,0:T(8,128)(2,1)S(1)}, bf16[512,256]{1,0:T(8,128)(2,1)S(1)}, u32[]{:S(2)}, u32[]{:S(2)}) collective-permute-start(bf16[512,256]{1,0:T(8,128)(2,1)S(1)} %get-tuple-element.28), channel_id=1, source_target_pairs={{0,4},{2,6},{4,0},{6,2},{1,5},{3,7},{5,1},{7,3},{8,12},{10,14},{12... | collective-permute-start | bytes 786440 | tf_op jit(solution)/shard_map/ppermute | solution.py:31
  29.5 1.8 %rows_y1_y3.1 = (bf16[512,256]{1,0:T(8,128)(2,1)S(1)}, bf16[512,256]{1,0:T(8,128)(2,1)S(1)}) custom-call(s32[4,512]{1,0:T(4,128)S(1)} %get-tuple-element.23.plan, bf16[33,128,256]{2,1,0:T(8,128)(2,1)S(1)} %get-tuple-element.27.panel, bf16[384,128,128]{2,1,0:T(8,128)(2,1)S(1)} %get-tuple-element.26.values), custom_call_target="tpu_custom_call" | custom-call | flops 6442450944 | bytes 1000 | tf_op jit(solution)/shard_map/rows_y1_y3/pallas_call | solution.py:214
  31.4 3.2 %collective-permute-start.8 = (bf16[512,256]{1,0:T(8,128)(2,1)S(1)}, bf16[512,256]{1,0:T(8,128)(2,1)S(1)}, u32[]{:S(2)}, u32[]{:S(2)}) collective-permute-start(bf16[512,256]{1,0:T(8,128)(2,1)S(1)} %get-tuple-element.30), channel_id=1, source_target_pairs={{0,6},{2,0},{4,2},{6,4},{1,7},{3,1},{5,3},{7,5},{8,14},{10,8},{12,... | collective-permute-start | bytes 786440 | tf_op jit(solution)/shard_map/ppermute | solution.py:31
  34.6 2.1 %collective-permute-done.6.refs_0_ = bf16[512,256]{1,0:T(8,128)(2,1)S(1)} collective-permute-done((bf16[512,256]{1,0:T(8,128)(2,1)S(1)}, bf16[512,256]{1,0:T(8,128)(2,1)S(1)}, u32[]{:S(2)}, u32[]{:S(2)}) %collective-permute-start.6) | collective-permute-done | bytes 262176 | tf_op jit(solution)/shard_map/ppermute | solution.py:31
  36.7 1.3 %rows_y0.1 = f32[512,256]{1,0:T(8,128)S(1)} custom-call(s32[4,512]{1,0:T(4,128)S(1)} %get-tuple-element.23.plan, bf16[33,128,256]{2,1,0:T(8,128)(2,1)S(1)} %get-tuple-element.27.panel, bf16[384,128,128]{2,1,0:T(8,128)(2,1)S(1)} %get-tuple-element.26.values, bf16[512,256]{1,0:T(8,128)(2,1)S(1)} %collective-permute-done.6.refs_0_), custom_call_target="tpu_custom_call" | custom-call | flops 3221225472 | bytes 1000 | tf_op jit(solution)/shard_map/rows_y0/pallas_call | solution.py:214
  38.0 4.2 %collective-permute-done.7 = bf16[512,256]{1,0:T(8,128)(2,1)S(1)} collective-permute-done((bf16[512,256]{1,0:T(8,128)(2,1)S(1)}, bf16[512,256]{1,0:T(8,128)(2,1)S(1)}, u32[]{:S(2)}, u32[]{:S(2)}) %collective-permute-start.7) | collective-permute-done | bytes 262176 | tf_op jit(solution)/shard_map/ppermute | solution.py:31
  42.2 0.1 add_convert_fusion.mine
  42.3 2.1 %collective-permute-start.9 = (bf16[512,256]{1,0:T(8,128)(2,1)S(1)}, bf16[512,256]{1,0:T(8,128)(2,1)S(1)}, u32[]{:S(2)}, u32[]{:S(2)}) collective-permute-start(bf16[512,256]{1,0:T(8,128)(2,1)S(1)} %add_convert_fusion.mine), channel_id=1, source_target_pairs={{0,1},{1,0},{2,3},{3,2},{4,5},{5,4},{6,7},{7,6},{8,9},{9,8},{10,11... | collective-permute-start | bytes 786440 | tf_op jit(solution)/shard_map/ppermute | solution.py:36
  44.5 7.8 %collective-permute-done.9.theirs = bf16[512,256]{1,0:T(8,128)(2,1)S(1)} collective-permute-done((bf16[512,256]{1,0:T(8,128)(2,1)S(1)}, bf16[512,256]{1,0:T(8,128)(2,1)S(1)}, u32[]{:S(2)}, u32[]{:S(2)}) %collective-permute-start.9) | collective-permute-done | bytes 262176 | tf_op jit(solution)/shard_map/ppermute | solution.py:36
  52.3 1.0 dense_part.1
  53.3 2.7 %collective-permute-start.15 = (bf16[512,256]{1,0:T(8,128)(2,1)S(1)}, bf16[512,256]{1,0:T(8,128)(2,1)S(1)}, u32[]{:S(2)}, u32[]{:S(2)}) collective-permute-start(bf16[512,256]{1,0:T(8,128)(2,1)S(1)} %get-tuple-element.33), channel_id=1, source_target_pairs={{0,6},{2,0},{4,2},{6,4},{1,7},{3,1},{5,3},{7,5},{8,14},{10,8},{12,... | collective-permute-start | bytes 786440 | tf_op jit(solution)/shard_map/ppermute | solution.py:31
  55.9 1.5 %collective-permute-start.13 = (bf16[512,256]{1,0:T(8,128)(2,1)S(1)}, bf16[512,256]{1,0:T(8,128)(2,1)S(1)}, u32[]{:S(2)}, u32[]{:S(2)}) collective-permute-start(bf16[512,256]{1,0:T(8,128)(2,1)S(1)} %get-tuple-element.33), channel_id=1, source_target_pairs={{0,4},{2,6},{4,0},{6,2},{1,5},{3,7},{5,1},{7,3},{8,12},{10,14},{12... | collective-permute-start | bytes 786440 | tf_op jit(solution)/shard_map/ppermute | solution.py:31
  57.5 2.5 %collective-permute-start.11 = (bf16[272,256]{1,0:T(8,128)(2,1)S(1)}, bf16[272,256]{1,0:T(8,128)(2,1)S(1)}, u32[]{:S(2)}, u32[]{:S(2)}) collective-permute-start(bf16[272,256]{1,0:T(8,128)(2,1)S(1)} %add_convert_fusion.6), channel_id=1, source_target_pairs={{0,32},{16,48},{32,0},{48,16},{1,33},{17,49},{33,1},{49,17},{2,34}... | collective-permute-start | bytes 417800 | tf_op jit(solution)/shard_map/ppermute | solution.py:36
  60.0 7.9 %collective-permute-done.15 = bf16[512,256]{1,0:T(8,128)(2,1)S(1)} collective-permute-done((bf16[512,256]{1,0:T(8,128)(2,1)S(1)}, bf16[512,256]{1,0:T(8,128)(2,1)S(1)}, u32[]{:S(2)}, u32[]{:S(2)}) %collective-permute-start.15) | collective-permute-done | bytes 262176 | tf_op jit(solution)/shard_map/ppermute | solution.py:31
  67.8 3.4 %collective-permute-done.14 = bf16[512,256]{1,0:T(8,128)(2,1)S(1)} collective-permute-done((bf16[512,256]{1,0:T(8,128)(2,1)S(1)}, bf16[512,256]{1,0:T(8,128)(2,1)S(1)}, u32[]{:S(2)}, u32[]{:S(2)}) %collective-permute-start.14) | collective-permute-done | bytes 262176 | tf_op jit(solution)/shard_map/ppermute | solution.py:31
  71.3 1.5 %columns_far.1 = (bf16[1536,256]{1,0:T(8,128)(2,1)S(1)}, bf16[17,128,256]{2,1,0:T(8,128)(2,1)S(1)}) custom-call(s32[4,512]{1,0:T(4,128)S(1)} %get-tuple-element.24.plan, s32[8]{0:T(128)S(1)} %stack.23.here, bf16[2048,256]{1,0:T(8,128)(2,1)S(1)} %pad_maximum_fusion.ref, bf16[384,128,128]{2,1,0:T(8,128)(2,1)S(1)} %get-tuple-element.26.values), custom_call_target="tpu_custom_call" | custom-call | flops 4831838208 | bytes 1000 | tf_op jit(solution)/shard_map/columns_far/pallas_call | solution.py:199
  72.8 1.9 %collective-permute-start.17 = (bf16[1536,256]{1,0:T(8,128)(2,1)S(1)}, bf16[1536,256]{1,0:T(8,128)(2,1)S(1)}, u32[]{:S(2)}, u32[]{:S(2)}) collective-permute-start(bf16[1536,256]{1,0:T(8,128)(2,1)S(1)} %get-tuple-element.34), channel_id=1, source_target_pairs={{0,8},{8,0},{1,9},{9,1},{2,10},{10,2},{3,11},{11,3},{4,12},{12,4},... | collective-permute-start | bytes 2359304 | tf_op jit(solution)/shard_map/ppermute | solution.py:36
  74.8 1.4 %columns_z0.1 = (bf16[512,256]{1,0:T(8,128)(2,1)S(1)}, bf16[512,256]{1,0:T(8,128)(2,1)S(1)}) custom-call(s32[4,512]{1,0:T(4,128)S(1)} %get-tuple-element.24.plan, bf16[17,128,256]{2,1,0:T(8,128)(2,1)S(1)} %get-tuple-element.36.panel, bf16[384,128,128]{2,1,0:T(8,128)(2,1)S(1)} %get-tuple-element.26.values), custom_call_target="tpu_custom_call" | custom-call | flops 3221225472 | bytes 1000 | tf_op jit(solution)/shard_map/columns_z0/pallas_call | solution.py:214
  76.2 1.9 %collective-permute-start.21 = (bf16[512,256]{1,0:T(8,128)(2,1)S(1)}, bf16[512,256]{1,0:T(8,128)(2,1)S(1)}, u32[]{:S(2)}, u32[]{:S(2)}) collective-permute-start(bf16[512,256]{1,0:T(8,128)(2,1)S(1)} %get-tuple-element.40), channel_id=1, source_target_pairs={{0,8},{8,0},{1,9},{9,1},{2,10},{10,2},{3,11},{11,3},{4,12},{12,4},... | collective-permute-start | bytes 786440 | tf_op jit(solution)/shard_map/ppermute | solution.py:36
  78.1 2.3 %collective-permute-done.12 = bf16[272,256]{1,0:T(8,128)(2,1)S(1)} collective-permute-done((bf16[272,256]{1,0:T(8,128)(2,1)S(1)}, bf16[272,256]{1,0:T(8,128)(2,1)S(1)}, u32[]{:S(2)}, u32[]{:S(2)}) %collective-permute-start.12) | collective-permute-done | bytes 139296 | tf_op jit(solution)/shard_map/ppermute | solution.py:36
  80.5 0.4 collective-permute-start.16
  80.8 1.7 %columns_z1_z3.1 = (bf16[512,256]{1,0:T(8,128)(2,1)S(1)}, bf16[512,256]{1,0:T(8,128)(2,1)S(1)}) custom-call(s32[4,512]{1,0:T(4,128)S(1)} %get-tuple-element.24.plan, bf16[17,128,256]{2,1,0:T(8,128)(2,1)S(1)} %get-tuple-element.36.panel, bf16[384,128,128]{2,1,0:T(8,128)(2,1)S(1)} %get-tuple-element.26.values, ...), custom_call_target="tpu_custom_call" | custom-call | flops 3221225472 | bytes 1000 | tf_op jit(solution)/shard_map/columns_z1_z3/pallas_call | solution.py:214
  82.5 3.0 %collective-permute-start.23 = (bf16[512,256]{1,0:T(8,128)(2,1)S(1)}, bf16[512,256]{1,0:T(8,128)(2,1)S(1)}, u32[]{:S(2)}, u32[]{:S(2)}) collective-permute-start(bf16[512,256]{1,0:T(8,128)(2,1)S(1)} %get-tuple-element.37), channel_id=1, source_target_pairs={{0,16},{16,32},{32,48},{48,0},{1,17},{17,33},{33,49},{49,1},{2,18}... | collective-permute-start | bytes 786440 | tf_op jit(solution)/shard_map/ppermute | solution.py:31
  85.5 0.1 collective-permute-done.16
  85.6 2.6 %collective-permute-start.18 = (bf16[272,256]{1,0:T(8,128)(2,1)S(1)}, bf16[272,256]{1,0:T(8,128)(2,1)S(1)}, u32[]{:S(2)}, u32[]{:S(2)}) collective-permute-start(bf16[272,256]{1,0:T(8,128)(2,1)S(1)} %add_convert_fusion.3), channel_id=1, source_target_pairs={{0,1},{1,0},{2,3},{3,2},{4,5},{5,4},{6,7},{7,6},{8,9},{9,8},{10,11... | collective-permute-start | bytes 417800 | tf_op jit(solution)/shard_map/ppermute | solution.py:36
  88.2 0.4 collective-permute-start.24
  88.7 1.4 %columns_z2.1 = bf16[512,256]{1,0:T(8,128)(2,1)S(1)} custom-call(s32[4,512]{1,0:T(4,128)S(1)} %get-tuple-element.24.plan, bf16[17,128,256]{2,1,0:T(8,128)(2,1)S(1)} %get-tuple-element.36.panel, bf16[384,128,128]{2,1,0:T(8,128)(2,1)S(1)} %get-tuple-element.26.values, bf16[1536,256]{1,0:T(8,128)(2,1)S(1)} %collective-permute-done.17.refs_0_), custom_call_target="tpu_custom_call" | custom-call | flops 1610612736 | bytes 1000 | tf_op jit(solution)/shard_map/columns_z2/pallas_call | solution.py:214
  90.1 4.0 %collective-permute-start.22 = (bf16[512,256]{1,0:T(8,128)(2,1)S(1)}, bf16[512,256]{1,0:T(8,128)(2,1)S(1)}, u32[]{:S(2)}, u32[]{:S(2)}) collective-permute-start(bf16[512,256]{1,0:T(8,128)(2,1)S(1)} %columns_z2.1), channel_id=1, source_target_pairs={{0,32},{16,48},{32,0},{48,16},{1,33},{17,49},{33,1},{49,17},{2,34}... | collective-permute-start | bytes 786440 | tf_op jit(solution)/shard_map/ppermute | solution.py:31
  94.2 4.6 %collective-permute-done.24 = bf16[512,256]{1,0:T(8,128)(2,1)S(1)} collective-permute-done((bf16[512,256]{1,0:T(8,128)(2,1)S(1)}, bf16[512,256]{1,0:T(8,128)(2,1)S(1)}, u32[]{:S(2)}, u32[]{:S(2)}) %collective-permute-start.24) | collective-permute-done | bytes 262176 | tf_op jit(solution)/shard_map/ppermute | solution.py:31
  98.8 3.8 %collective-permute-done.22 = bf16[512,256]{1,0:T(8,128)(2,1)S(1)} collective-permute-done((bf16[512,256]{1,0:T(8,128)(2,1)S(1)}, bf16[512,256]{1,0:T(8,128)(2,1)S(1)}, u32[]{:S(2)}, u32[]{:S(2)}) %collective-permute-start.22) | collective-permute-done | bytes 262176 | tf_op jit(solution)/shard_map/ppermute | solution.py:31
  102.6 0.2 convert_add_fusion
  102.8 0.9 collective-permute-start.25
  103.8 4.0 %collective-permute-done.25 = bf16[256,256]{1,0:T(8,128)(2,1)S(1)} collective-permute-done((bf16[256,256]{1,0:T(8,128)(2,1)S(1)}, bf16[256,256]{1,0:T(8,128)(2,1)S(1)}, u32[]{:S(2)}, u32[]{:S(2)}) %collective-permute-start.25) | collective-permute-done | bytes 131104 | tf_op jit(solution)/shard_map/ppermute | solution.py:36
  107.8 0.7 fusion
  108.5 0.3 collective-permute-done.20
  108.8 0.6 fusion.2
  109.4 0.7 add_multiply_fusion
  (39 shorter events, 0.9 us)
Async XLA Ops:
  0.6 5.5 %collective-permute-start = (bf16[256,256]{1,0:T(8,128)(2,1)}, bf16[256,256]{1,0:T(8,128)(2,1)S(1)}, u32[]{:S(2)}, u32[]{:S(2)}) collective-permute-start(bf16[256,256]{1,0:T(8,128)(2,1)} %param.8), channel_id=1, source_target_pairs={{0,64},{64,0},{1,65},{65,1},{2,66},{66,2},{3,67},{67,3},{4,68},{68... | collective-permute-start | bytes 393224 | tf_op jit(solution)/shard_map/ppermute | solution.py:36
  6.2 14.2 %collective-permute-start.1 = (bf16[512,256]{1,0:T(8,128)(2,1)S(1)}, bf16[512,256]{1,0:T(8,128)(2,1)S(1)}, u32[]{:S(2)}, u32[]{:S(2)}) collective-permute-start(bf16[512,256]{1,0:T(8,128)(2,1)S(1)} %get-tuple-element.42), channel_id=1, source_target_pairs={{0,32},{16,48},{32,0},{48,16},{1,33},{17,49},{33,1},{49,17},{2,34}... | collective-permute-start | bytes 786440 | tf_op jit(solution)/shard_map/ppermute | solution.py:31
  9.2 11.8 %collective-permute-start.2 = (bf16[512,256]{1,0:T(8,128)(2,1)S(1)}, bf16[512,256]{1,0:T(8,128)(2,1)S(1)}, u32[]{:S(2)}, u32[]{:S(2)}) collective-permute-start(bf16[512,256]{1,0:T(8,128)(2,1)S(1)} %get-tuple-element.42), channel_id=1, source_target_pairs={{0,16},{16,32},{32,48},{48,0},{1,17},{17,33},{33,49},{49,1},{2,18}... | collective-permute-start | bytes 786440 | tf_op jit(solution)/shard_map/ppermute | solution.py:31
  9.2 11.8 %collective-permute-start.3 = (bf16[512,256]{1,0:T(8,128)(2,1)S(1)}, bf16[512,256]{1,0:T(8,128)(2,1)S(1)}, u32[]{:S(2)}, u32[]{:S(2)}) collective-permute-start(bf16[512,256]{1,0:T(8,128)(2,1)S(1)} %get-tuple-element.42), channel_id=1, source_target_pairs={{0,48},{16,0},{32,16},{48,32},{1,49},{17,1},{33,17},{49,33},{2,50}... | collective-permute-start | bytes 786440 | tf_op jit(solution)/shard_map/ppermute | solution.py:31
  11.3 9.9 %collective-permute-start.4 = (bf16[256,256]{1,0:T(8,128)(2,1)}, bf16[256,256]{1,0:T(8,128)(2,1)S(1)}, u32[]{:S(2)}, u32[]{:S(2)}) collective-permute-start(bf16[256,256]{1,0:T(8,128)(2,1)} %cot.1), channel_id=1, source_target_pairs={{0,1},{1,0},{2,3},{3,2},{4,5},{5,4},{6,7},{7,6},{8,9},{9,8},{10,11... | collective-permute-start | bytes 393224 | tf_op jit(solution)/shard_map/ppermute | solution.py:36
  21.1 2.7 %collective-permute-start.5 = (bf16[2048,256]{1,0:T(8,128)(2,1)S(1)}, bf16[2048,256]{1,0:T(8,128)(2,1)S(1)}, u32[]{:S(2)}, u32[]{:S(2)}) collective-permute-start(bf16[2048,256]{1,0:T(8,128)(2,1)S(1)} %constant_dynamic-update-slice_fusion.2.own_ref), channel_id=1, source_target_pairs={{0,8},{8,0},{1,9},{9,1},{2,10},{10,2},{3,11},{11,3},{4,12},{12,4},... | collective-permute-start | bytes 3145736 | tf_op jit(solution)/shard_map/ppermute | solution.py:36
  25.2 11.4 %collective-permute-start.6 = (bf16[512,256]{1,0:T(8,128)(2,1)S(1)}, bf16[512,256]{1,0:T(8,128)(2,1)S(1)}, u32[]{:S(2)}, u32[]{:S(2)}) collective-permute-start(bf16[512,256]{1,0:T(8,128)(2,1)S(1)} %get-tuple-element.28), channel_id=1, source_target_pairs={{0,4},{2,6},{4,0},{6,2},{1,5},{3,7},{5,1},{7,3},{8,12},{10,14},{12... | collective-permute-start | bytes 786440 | tf_op jit(solution)/shard_map/ppermute | solution.py:31
  31.3 10.9 %collective-permute-start.7 = (bf16[512,256]{1,0:T(8,128)(2,1)S(1)}, bf16[512,256]{1,0:T(8,128)(2,1)S(1)}, u32[]{:S(2)}, u32[]{:S(2)}) collective-permute-start(bf16[512,256]{1,0:T(8,128)(2,1)S(1)} %get-tuple-element.29), channel_id=1, source_target_pairs={{0,2},{2,4},{4,6},{6,0},{1,3},{3,5},{5,7},{7,1},{8,10},{10,12},{12... | collective-permute-start | bytes 786440 | tf_op jit(solution)/shard_map/ppermute | solution.py:31
  31.4 20.9 %copy-start = (bf16[256,256]{1,0:T(8,128)(2,1)S(1)}, bf16[256,256]{1,0:T(8,128)(2,1)}, u32[]{:S(2)}) copy-start(bf16[256,256]{1,0:T(8,128)(2,1)} %weight.1) | copy-start | bytes 393220
  31.4 20.9 %copy-start.1 = (bf16[256,256]{1,0:T(8,128)(2,1)S(1)}, bf16[256,256]{1,0:T(8,128)(2,1)}, u32[]{:S(2)}) copy-start(bf16[256,256]{1,0:T(8,128)(2,1)} %cot.1) | copy-start | bytes 393220
  31.4 20.9 %copy-start.2 = (f32[256]{0:T(256)S(1)}, f32[256]{0:T(256)}, u32[]{:S(2)}) copy-start(f32[256]{0:T(256)} %param.10) | copy-start | bytes 3076
  31.4 10.8 %collective-permute-start.8 = (bf16[512,256]{1,0:T(8,128)(2,1)S(1)}, bf16[512,256]{1,0:T(8,128)(2,1)S(1)}, u32[]{:S(2)}, u32[]{:S(2)}) collective-permute-start(bf16[512,256]{1,0:T(8,128)(2,1)S(1)} %get-tuple-element.30), channel_id=1, source_target_pairs={{0,6},{2,0},{4,2},{6,4},{1,7},{3,1},{5,3},{7,5},{8,14},{10,8},{12,... | collective-permute-start | bytes 786440 | tf_op jit(solution)/shard_map/ppermute | solution.py:31
  42.3 9.9 %collective-permute-start.9 = (bf16[512,256]{1,0:T(8,128)(2,1)S(1)}, bf16[512,256]{1,0:T(8,128)(2,1)S(1)}, u32[]{:S(2)}, u32[]{:S(2)}) collective-permute-start(bf16[512,256]{1,0:T(8,128)(2,1)S(1)} %add_convert_fusion.mine), channel_id=1, source_target_pairs={{0,1},{1,0},{2,3},{3,2},{4,5},{5,4},{6,7},{7,6},{8,9},{9,8},{10,11... | collective-permute-start | bytes 786440 | tf_op jit(solution)/shard_map/ppermute | solution.py:36
  53.3 4.2 %collective-permute-start.10 = (bf16[272,256]{1,0:T(8,128)(2,1)S(1)}, bf16[272,256]{1,0:T(8,128)(2,1)S(1)}, u32[]{:S(2)}, u32[]{:S(2)}) collective-permute-start(bf16[272,256]{1,0:T(8,128)(2,1)S(1)} %get-tuple-element.32), channel_id=1, source_target_pairs={{0,8},{8,0},{1,9},{9,1},{2,10},{10,2},{3,11},{11,3},{4,12},{12,4},... | collective-permute-start | bytes 417800 | tf_op jit(solution)/shard_map/ppermute | solution.py:36
  53.3 14.6 %collective-permute-start.15 = (bf16[512,256]{1,0:T(8,128)(2,1)S(1)}, bf16[512,256]{1,0:T(8,128)(2,1)S(1)}, u32[]{:S(2)}, u32[]{:S(2)}) collective-permute-start(bf16[512,256]{1,0:T(8,128)(2,1)S(1)} %get-tuple-element.33), channel_id=1, source_target_pairs={{0,6},{2,0},{4,2},{6,4},{1,7},{3,1},{5,3},{7,5},{8,14},{10,8},{12,... | collective-permute-start | bytes 786440 | tf_op jit(solution)/shard_map/ppermute | solution.py:31
  55.9 15.3 %collective-permute-start.14 = (bf16[512,256]{1,0:T(8,128)(2,1)S(1)}, bf16[512,256]{1,0:T(8,128)(2,1)S(1)}, u32[]{:S(2)}, u32[]{:S(2)}) collective-permute-start(bf16[512,256]{1,0:T(8,128)(2,1)S(1)} %get-tuple-element.33), channel_id=1, source_target_pairs={{0,2},{2,4},{4,6},{6,0},{1,3},{3,5},{5,7},{7,1},{8,10},{10,12},{12... | collective-permute-start | bytes 786440 | tf_op jit(solution)/shard_map/ppermute | solution.py:31
  55.9 15.3 %collective-permute-start.13 = (bf16[512,256]{1,0:T(8,128)(2,1)S(1)}, bf16[512,256]{1,0:T(8,128)(2,1)S(1)}, u32[]{:S(2)}, u32[]{:S(2)}) collective-permute-start(bf16[512,256]{1,0:T(8,128)(2,1)S(1)} %get-tuple-element.33), channel_id=1, source_target_pairs={{0,4},{2,6},{4,0},{6,2},{1,5},{3,7},{5,1},{7,3},{8,12},{10,14},{12... | collective-permute-start | bytes 786440 | tf_op jit(solution)/shard_map/ppermute | solution.py:31
  57.5 17.2 %collective-permute-start.11 = (bf16[272,256]{1,0:T(8,128)(2,1)S(1)}, bf16[272,256]{1,0:T(8,128)(2,1)S(1)}, u32[]{:S(2)}, u32[]{:S(2)}) collective-permute-start(bf16[272,256]{1,0:T(8,128)(2,1)S(1)} %add_convert_fusion.6), channel_id=1, source_target_pairs={{0,32},{16,48},{32,0},{48,16},{1,33},{17,49},{33,1},{49,17},{2,34}... | collective-permute-start | bytes 417800 | tf_op jit(solution)/shard_map/ppermute | solution.py:36
  72.8 8.0 %collective-permute-start.17 = (bf16[1536,256]{1,0:T(8,128)(2,1)S(1)}, bf16[1536,256]{1,0:T(8,128)(2,1)S(1)}, u32[]{:S(2)}, u32[]{:S(2)}) collective-permute-start(bf16[1536,256]{1,0:T(8,128)(2,1)S(1)} %get-tuple-element.34), channel_id=1, source_target_pairs={{0,8},{8,0},{1,9},{9,1},{2,10},{10,2},{3,11},{11,3},{4,12},{12,4},... | collective-permute-start | bytes 2359304 | tf_op jit(solution)/shard_map/ppermute | solution.py:36
  74.7 5.7 %collective-permute-start.12 = (bf16[272,256]{1,0:T(8,128)(2,1)S(1)}, bf16[272,256]{1,0:T(8,128)(2,1)S(1)}, u32[]{:S(2)}, u32[]{:S(2)}) collective-permute-start(bf16[272,256]{1,0:T(8,128)(2,1)S(1)} %add_convert_fusion.5), channel_id=1, source_target_pairs={{0,16},{16,0},{32,48},{48,32},{1,17},{17,1},{33,49},{49,33},{2,18}... | collective-permute-start | bytes 417800 | tf_op jit(solution)/shard_map/ppermute | solution.py:36
  76.2 18.0 %collective-permute-start.21 = (bf16[512,256]{1,0:T(8,128)(2,1)S(1)}, bf16[512,256]{1,0:T(8,128)(2,1)S(1)}, u32[]{:S(2)}, u32[]{:S(2)}) collective-permute-start(bf16[512,256]{1,0:T(8,128)(2,1)S(1)} %get-tuple-element.40), channel_id=1, source_target_pairs={{0,8},{8,0},{1,9},{9,1},{2,10},{10,2},{3,11},{11,3},{4,12},{12,4},... | collective-permute-start | bytes 786440 | tf_op jit(solution)/shard_map/ppermute | solution.py:36
  80.5 5.1 %collective-permute-start.16 = (bf16[272,256]{1,0:T(8,128)(2,1)S(1)}, bf16[272,256]{1,0:T(8,128)(2,1)S(1)}, u32[]{:S(2)}, u32[]{:S(2)}) collective-permute-start(bf16[272,256]{1,0:T(8,128)(2,1)S(1)} %add_convert_fusion.4), channel_id=1, source_target_pairs={{0,64},{64,0},{1,65},{65,1},{2,66},{66,2},{3,67},{67,3},{4,68},{68... | collective-permute-start | bytes 417800 | tf_op jit(solution)/shard_map/ppermute | solution.py:36
  82.5 16.3 %collective-permute-start.23 = (bf16[512,256]{1,0:T(8,128)(2,1)S(1)}, bf16[512,256]{1,0:T(8,128)(2,1)S(1)}, u32[]{:S(2)}, u32[]{:S(2)}) collective-permute-start(bf16[512,256]{1,0:T(8,128)(2,1)S(1)} %get-tuple-element.37), channel_id=1, source_target_pairs={{0,16},{16,32},{32,48},{48,0},{1,17},{17,33},{33,49},{49,1},{2,18}... | collective-permute-start | bytes 786440 | tf_op jit(solution)/shard_map/ppermute | solution.py:31
  85.6 8.5 %collective-permute-start.18 = (bf16[272,256]{1,0:T(8,128)(2,1)S(1)}, bf16[272,256]{1,0:T(8,128)(2,1)S(1)}, u32[]{:S(2)}, u32[]{:S(2)}) collective-permute-start(bf16[272,256]{1,0:T(8,128)(2,1)S(1)} %add_convert_fusion.3), channel_id=1, source_target_pairs={{0,1},{1,0},{2,3},{3,2},{4,5},{5,4},{6,7},{7,6},{8,9},{9,8},{10,11... | collective-permute-start | bytes 417800 | tf_op jit(solution)/shard_map/ppermute | solution.py:36
  88.2 10.6 %collective-permute-start.24 = (bf16[512,256]{1,0:T(8,128)(2,1)S(1)}, bf16[512,256]{1,0:T(8,128)(2,1)S(1)}, u32[]{:S(2)}, u32[]{:S(2)}) collective-permute-start(bf16[512,256]{1,0:T(8,128)(2,1)S(1)} %get-tuple-element.41), channel_id=1, source_target_pairs={{0,48},{16,0},{32,16},{48,32},{1,49},{17,1},{33,17},{49,33},{2,50}... | collective-permute-start | bytes 786440 | tf_op jit(solution)/shard_map/ppermute | solution.py:31
  90.1 12.5 %collective-permute-start.22 = (bf16[512,256]{1,0:T(8,128)(2,1)S(1)}, bf16[512,256]{1,0:T(8,128)(2,1)S(1)}, u32[]{:S(2)}, u32[]{:S(2)}) collective-permute-start(bf16[512,256]{1,0:T(8,128)(2,1)S(1)} %columns_z2.1), channel_id=1, source_target_pairs={{0,32},{16,48},{32,0},{48,16},{1,33},{17,49},{33,1},{49,17},{2,34}... | collective-permute-start | bytes 786440 | tf_op jit(solution)/shard_map/ppermute | solution.py:31
  94.1 9.5 %collective-permute-start.19 = (bf16[272,256]{1,0:T(8,128)(2,1)S(1)}, bf16[272,256]{1,0:T(8,128)(2,1)S(1)}, u32[]{:S(2)}, u32[]{:S(2)}) collective-permute-start(bf16[272,256]{1,0:T(8,128)(2,1)S(1)} %add_convert_fusion.2), channel_id=1, source_target_pairs={{0,4},{2,6},{4,0},{6,2},{1,5},{3,7},{5,1},{7,3},{8,12},{10,14},{12... | collective-permute-start | bytes 417800 | tf_op jit(solution)/shard_map/ppermute | solution.py:36
  102.8 5.0 %collective-permute-start.25 = (bf16[256,256]{1,0:T(8,128)(2,1)S(1)}, bf16[256,256]{1,0:T(8,128)(2,1)S(1)}, u32[]{:S(2)}, u32[]{:S(2)}) collective-permute-start(bf16[256,256]{1,0:T(8,128)(2,1)S(1)} %slice.45), channel_id=1, source_target_pairs={{0,64},{64,0},{1,65},{65,1},{2,66},{66,2},{3,67},{67,3},{4,68},{68... | collective-permute-start | bytes 393224 | tf_op jit(solution)/shard_map/ppermute | solution.py:36
  103.7 5.1 %collective-permute-start.20 = (bf16[272,256]{1,0:T(8,128)(2,1)S(1)}, bf16[272,256]{1,0:T(8,128)(2,1)S(1)}, u32[]{:S(2)}, u32[]{:S(2)}) collective-permute-start(bf16[272,256]{1,0:T(8,128)(2,1)S(1)} %add_convert_fusion.1), channel_id=1, source_target_pairs={{0,2},{2,0},{4,6},{6,4},{1,3},{3,1},{5,7},{7,5},{8,10},{10,8},{12,... | collective-permute-start | bytes 417800 | tf_op jit(solution)/shard_map/ppermute | solution.py:36
